TPU v7x, 32 devices: a whole 2x2x4 slice. The times are simulated.
32 devices in a mesh: rep: 4 (over z), ep: 8 (over y, x, core).
Axes of the slice: x: 2, y: 2, z: 4, core: 2. Of those that a mesh axis runs over, the one named last changes fastest.
Arguments:
- hidden_in: bfloat16 [4096, 2048], P(('rep', 'ep')), may hold values from -3 to 3
- tree_queries: bfloat16 [4096, 2048], P(('rep', 'ep')), may hold values from -6 to 6
- tree_keys: bfloat16 [4096, 2048], P(('rep', 'ep')), may hold values from -6 to 6
- tree_values: bfloat16 [4096, 2048], P(('rep', 'ep')), may hold values from -12 to 12
- tree_parents: int32 [64, 64], P(('rep', 'ep')), may hold values from -1 to 62, as said below
- accepted_nodes: int32 [64, 16], P(('rep', 'ep')), may hold values from 0 to 63
- request_prompt: int32 [64], P(('rep', 'ep')), may hold values from 0 to 3
- prompt_lengths: int32 [16], P('rep'), may hold values from 24 to 192, as said below
- prompt_keys: bfloat16 [16, 192, 2048], P('rep', 'ep'), may hold values from -6 to 6
- prompt_values: bfloat16 [16, 192, 2048], P('rep', 'ep'), may hold values from -12 to 12
- out_proj: bfloat16 [2048, 2048], P('rep'), may hold values from -0.125 to 0.125
- norm_gain: float32 [2048], replicated, may hold values from 0.1 to 1.9
- expert_ids: int32 [4096, 8], P(('rep', 'ep')), may hold values from 0 to 31, all different within a row; in each aligned block of 128 rows (0 to 127, 128 to 255, ...) at most 40 rows name the same one
- gate_weights: float32 [4096, 8], P(('rep', 'ep')), may hold values from 0.05 to 0.5
- expert_gate_up: bfloat16 [32, 2048, 1024], P('ep'), may hold values from -0.125 to 0.125
- expert_down: bfloat16 [32, 512, 2048], P('ep'), may hold values from -0.25 to 0.25
Outputs:
- layer_out: bfloat16 [4096, 2048], P(('rep', 'ep'))
- accepted_cache: bfloat16 [64, 16, 4096], P(('rep', 'ep'))
Inputs may be any that keep to these rules, and one draw needn't show every extreme that they name: `tree_parents`: node 0 of every request has parent -1; every other node's parent is one of the 8 nodes before it. `request_prompt`: index of the request's prompt among the 4 prompts of its index of rep. `prompt_lengths`: among the 4 prompts of each index of rep, one has all 192 positions. `expert_ids`: each row names 8 different experts; on the rows of one device no expert is named by more than 40 rows.
All inputs are finite; a program needn't handle non-finite values.
Results may differ from a plain program's by a relative error of at most 0.012.
Values may be sent and summed in bfloat16 or wider, within the bound.
No kernel may reach another device: no remote copies, remote signals or barrier semaphores. Data moves between devices by JAX's collectives and lax.ppermute only.
A program may use at most 128 MiB of HBM per device.

v0:
```python
import math

import jax
import jax.numpy as jnp
from jax import lax
from jax.sharding import PartitionSpec as P

HEADS = 16
HEAD_DIM = 128
CAP = 40


NEG_FILL = -1e30
EPSILON = 1e-05


def ancestry(parents):
    tree_width = parents.shape[-1]
    node_ids = jnp.arange(tree_width, dtype=jnp.int32)
    linked = jnp.logical_or(
        parents[..., :, None] == node_ids[None, :], node_ids[:, None] == node_ids[None, :]
    )
    closure = linked.astype(jnp.float32)
    for repeat in range(tree_width.bit_length()):
        closure = jnp.minimum(
            1.0, jnp.einsum("rij,rjk->rik", closure, closure, precision=lax.Precision.HIGHEST)
        )
    return closure > 0.5


def fold_block(running, scores, visible, product):
    highest, summed, gathered = running
    masked = jnp.where(visible[None], scores, NEG_FILL)
    updated = jnp.maximum(highest, jnp.max(masked, axis=-1))
    factor = jnp.exp(highest - updated)
    exp_weights = jnp.where(visible[None], jnp.exp(masked - updated[..., None]), 0.0)
    summed = summed * factor + jnp.sum(exp_weights, axis=-1)
    gathered = gathered * jnp.transpose(factor)[:, :, None] + product(
        exp_weights.astype(jnp.bfloat16)
    )
    return (updated, summed, gathered)


def per_device(
    hidden_in,
    tree_queries,
    tree_keys,
    tree_values,
    tree_parents,
    accepted_nodes,
    request_prompt,
    prompt_lengths,
    prompt_keys,
    prompt_values,
    out_proj,
    norm_gain,
    expert_ids,
    gate_weights,
    expert_gate_up,
    expert_down,
):
    tok_rows, feature_count = hidden_in.shape
    req_count, tree_len = tree_parents.shape
    prompt_count = prompt_keys.shape[0]
    score_scale = 1.0 / math.sqrt(HEAD_DIM)
    queries = tree_queries.reshape(tok_rows, HEADS, HEAD_DIM)
    own_keys = tree_keys.reshape(tok_rows, HEADS, HEAD_DIM)
    own_values = tree_values.reshape(tok_rows, HEADS, HEAD_DIM)
    token_request = jnp.arange(tok_rows, dtype=jnp.int32) // tree_len
    token_prompt = request_prompt[token_request]
    request_length = prompt_lengths[request_prompt]
    token_length = request_length[token_request]
    prompt_range = jnp.arange(prompt_count, dtype=jnp.int32)
    running = (
        jnp.full((HEADS, tok_rows), NEG_FILL, jnp.float32),
        jnp.zeros((HEADS, tok_rows), jnp.float32),
        jnp.zeros((tok_rows, HEADS, HEAD_DIM), jnp.float32),
    )
    page_keys = lax.all_gather(prompt_keys, "ep", axis=1, tiled=True)
    page_values = lax.all_gather(prompt_values, "ep", axis=1, tiled=True)
    rows_here = page_keys.shape[1]
    shaped_keys = page_keys.reshape(prompt_count, rows_here, HEADS, HEAD_DIM)
    flat_values = page_values.reshape(prompt_count * rows_here, HEADS, HEAD_DIM)
    scores = (
        jnp.einsum("thd,pkhd->htpk", queries, shaped_keys, preferred_element_type=jnp.float32)
        * score_scale
    )
    scores = scores.reshape(HEADS, tok_rows, prompt_count * rows_here)
    positions = jnp.arange(rows_here, dtype=jnp.int32)
    same_prompt = (token_prompt[:, None] == prompt_range[None, :])[:, :, None]
    in_length = (positions[None, :] < token_length[:, None])[:, None, :]
    visible = jnp.logical_and(same_prompt, in_length).reshape(tok_rows, prompt_count * rows_here)

    def product(weights):
        return jnp.einsum("htk,khd->thd", weights, flat_values, preferred_element_type=jnp.float32)

    running = fold_block(running, scores, visible, product)
    tree_seen = ancestry(tree_parents)
    node_index = jnp.arange(tok_rows, dtype=jnp.int32) % tree_len
    row_seen = tree_seen[token_request, node_index]
    same_request = token_request[:, None] == jnp.arange(req_count, dtype=jnp.int32)[None, :]
    tree_visible = jnp.logical_and(same_request[:, :, None], row_seen[:, None, :]).reshape(
        tok_rows, tok_rows
    )
    tree_scores = (
        jnp.einsum("thd,khd->htk", queries, own_keys, preferred_element_type=jnp.float32)
        * score_scale
    )

    def tree_product(weights):
        return jnp.einsum("htk,khd->thd", weights, own_values, preferred_element_type=jnp.float32)

    highest, summed, gathered = fold_block(running, tree_scores, tree_visible, tree_product)
    attended = (
        (gathered / jnp.transpose(summed)[:, :, None])
        .reshape(tok_rows, feature_count)
        .astype(jnp.bfloat16)
    )
    projected = jnp.dot(
        attended,
        lax.all_gather(out_proj, "rep", axis=0, tiled=True),
        preferred_element_type=jnp.float32,
    )
    residual = hidden_in.astype(jnp.float32) + projected
    normed = (
        residual
        * lax.rsqrt(jnp.mean(residual * residual, axis=-1, keepdims=True) + EPSILON)
        * norm_gain
    ).astype(jnp.bfloat16)
    top_count = expert_ids.shape[1]
    local_experts = expert_gate_up.shape[0]
    hidden_units = expert_down.shape[1]
    ep_size = lax.axis_size("ep")
    expert_total = local_experts * ep_size
    flat_ids = expert_ids.reshape(-1)
    onehot = (flat_ids[:, None] == jnp.arange(expert_total, dtype=jnp.int32)[None, :]).astype(
        jnp.int32
    )
    earlier = jnp.cumsum(onehot, axis=0) - onehot
    slot_index = jnp.sum(earlier * onehot, axis=1)
    target = flat_ids * CAP + slot_index
    source_rows = jnp.arange(flat_ids.shape[0], dtype=jnp.int32) // top_count
    outgoing = (
        jnp.zeros((expert_total * CAP, feature_count), jnp.bfloat16)
        .at[target]
        .set(normed[source_rows])
    )
    outgoing = outgoing.reshape(ep_size, local_experts, CAP, feature_count)
    incoming = lax.all_to_all(outgoing, "ep", split_axis=0, concat_axis=0, tiled=True)
    slots_here = incoming.shape[2]
    results = []
    for expert in range(local_experts):
        rows_in = incoming[:, expert].reshape(ep_size * slots_here, feature_count)
        joint_proj = jnp.dot(rows_in, expert_gate_up[expert], preferred_element_type=jnp.float32)
        activated = (
            jax.nn.silu(joint_proj[:, :hidden_units]) * joint_proj[:, hidden_units:]
        ).astype(jnp.bfloat16)
        produced = jnp.dot(
            activated, expert_down[expert], preferred_element_type=jnp.float32
        ).astype(jnp.bfloat16)
        results.append(produced.reshape(ep_size, slots_here, feature_count))
    replies = jnp.stack(results, axis=1)
    returned = lax.all_to_all(replies, "ep", split_axis=0, concat_axis=0, tiled=True)
    picked = returned.reshape(expert_total * CAP, feature_count)[target].reshape(
        tok_rows, top_count, feature_count
    )
    mixture = jnp.sum(gate_weights[:, :, None] * picked, axis=1)
    layer_out = (residual + mixture).astype(jnp.bfloat16)
    accepted_rows = jnp.arange(req_count, dtype=jnp.int32)[:, None] * tree_len + accepted_nodes
    accepted_cache = jnp.concatenate(
        [tree_keys[accepted_rows], tree_values[accepted_rows]], axis=-1
    )
    return (layer_out, accepted_cache)


def solution(mesh):
    in_specs = (
        P(("rep", "ep"), None),
        P(("rep", "ep"), None),
        P(("rep", "ep"), None),
        P(("rep", "ep"), None),
        P(("rep", "ep"), None),
        P(("rep", "ep"), None),
        P(("rep", "ep")),
        P("rep"),
        P("rep", "ep", None),
        P("rep", "ep", None),
        P("rep", None),
        P(),
        P(("rep", "ep"), None),
        P(("rep", "ep"), None),
        P("ep", None, None),
        P("ep", None, None),
    )
    out_specs = (P(("rep", "ep"), None), P(("rep", "ep"), None, None))
    return jax.shard_map(
        per_device, mesh=mesh, in_specs=in_specs, out_specs=out_specs, check_vma=False
    )
```

profile of v0, /device:TPU:0, one launch (start us, length us, event | category | flops | bytes accessed | tf_op | source)
XLA Modules:
  0.0 434.6 jit_solution(8469758025861679995)
XLA Ops:
  7.3 0.7 all-gather.4.cloned.1.call-update
  8.0 0.7 all-gather.6.cloned.1.call-update
  8.8 0.7 all-gather.8.cloned.1.call-update
  9.5 0.8 copy.58
  10.5 1.0 convolution_minimum_fusion.6
  12.6 1.1 gather_fusion.1
  13.9 0.6 gather_fusion
  14.5 0.6 fusion.98
  15.1 1.3 fusion.85
  16.4 0.6 fusion.97
  17.0 1.3 fusion.86
  18.6 1.0 copy.67
  19.6 9.5 %reduce-window.6 = s32[32,8,128]{2,1,0:T(8,128)S(1)} reduce-window(s32[32,8,128]{2,1,0:T(8,128)S(1)} %fusion.72, s32[]{:T(128)} %constant.79.clone.1), window={size=1x1x128 pad=0_0x0_0x127_0}, to_apply=%region_4.5 | reduce-window | flops 4161536 | bytes 262148 | tf_op jit(solution)/shard_map/reduce-window
  30.0 1.5 fusion.99
  31.5 13.5 %all-gather.4.cloned.1.call-done = bf16[4,192,2048]{2,1,0:T(8,128)(2,1)} async-done(((bf16[4,24,2048]{2,1,0:T(8,128)(2,1)}), bf16[4,192,2048]{2,1,0:T(8,128)(2,1)}) %all-gather.4.cloned.1.call-update) | async-done | bytes 3145744 | tf_op jit(solution)/shard_map/all_gather | solution.py:79
  45.0 2.8 copy_bitcast_fusion
  47.8 1.0 fusion.54
  48.8 0.8 select_reduce_fusion.1
  49.7 4.1 select_reduce_fusion
  53.8 6.7 %copy.49 = f32[16,128,768]{2,1,0:T(8,128)} copy(f32[16,128,768]{1,2,0:T(8,128)} %bitcast.175) | data formatting | bytes 12582912 | tf_op jit(solution)/shard_map/reshape | solution.py:88
  60.5 18.8 %all-gather.6.cloned.1.call-done = bf16[4,192,2048]{2,1,0:T(8,128)(2,1)} async-done(((bf16[4,24,2048]{2,1,0:T(8,128)(2,1)}), bf16[4,192,2048]{2,1,0:T(8,128)(2,1)}) %all-gather.6.cloned.1.call-update) | async-done | bytes 3145744 | tf_op jit(solution)/shard_map/all_gather | solution.py:80
  79.3 3.0 copy.71
  82.5 0.5 copy-done.3
  83.0 3.0 fusion.39
  86.0 0.3 fusion.42
  86.4 144.1 %all-gather.8.cloned.1.call-done = bf16[2048,2048]{1,0:T(8,128)(2,1)} async-done(((bf16[512,2048]{1,0:T(8,128)(2,1)}), bf16[2048,2048]{1,0:T(8,128)(2,1)}) %all-gather.8.cloned.1.call-update) | async-done | bytes 8388624 | tf_op jit(solution)/shard_map/all_gather | solution.py:121
  230.5 4.8 %multiply_reduce_fusion = (f32[128]{0:T(128)S(1)}, f32[128,2048]{1,0:T(8,128)S(1)}) fusion(bf16[128,2048]{0,1:T(8,128)(2,1)S(1)} %bitcast.180, bf16[2048,2048]{1,0:T(8,128)(2,1)} %all-gather.8.cloned.1.call-done, bf16[128,2048]{1,0:T(8,128)(2,1)S(1)} %copy-done.7), kind=kOutput, calls=%fused_computation.68 | convolution fusion | flops 1074790272 | bytes 10486272 | tf_op jit(solution)/shard_map/dot_general | solution.py:119
  235.5 23.3 %scatter_custom_fusion = bf16[1280,2048]{1,0:T(8,128)(2,1)} fusion(s32[1024]{0:T(1024)S(1)} %bitcast.199, bf16[128,2048]{1,0:T(8,128)(2,1)S(1)} %multiply_convert_fusion, s32[1024]{0:T(1024)S(1)} %broadcast_clamp_fusion.1, bf16[]{:T(256)} %constant.90.clone.1), kind=kCustom, calls=%fused_computation.21 | custom fusion | bytes 5242882 | tf_op jit(solution)/shard_map/scatter | solution.py:146
  258.7 64.5 %all_to_all.10 = bf16[8,4,40,2048]{3,2,1,0:T(8,128)(2,1)S(1)} all-to-all(bf16[8,4,40,2048]{3,2,1,0:T(8,128)(2,1)} %bitcast.176), channel_id=1, replica_groups=mesh['rep'=4,'ep'=8] {'ep'}, dimensions={0} | all-to-all | bytes 10485760 | tf_op jit(solution)/shard_map/all_to_all | solution.py:149
  323.3 0.8 fusion.96
  324.1 4.1 fusion.7
  328.3 1.5 fusion.5
  329.9 2.6 convolution_convert_fusion.3
  332.5 0.3 slice-done.5
  332.9 0.9 convolution_convert_fusion.2
  333.7 1.5 fusion.3
  335.3 0.9 convolution_convert_fusion.1
  336.2 1.5 fusion.1
  337.7 2.5 convolution_convert_fusion
  340.2 2.7 pad_maximum_fusion
  342.9 5.0 %all-to-all-start.1 = ((bf16[8,4,40,2048]{3,2,1,0:T(8,128)(2,1)}), bf16[8,4,40,2048]{3,2,1,0:T(8,128)(2,1)}, u32[]{:S(2)}, u32[]{:S(2)}) async-start(bf16[8,4,40,2048]{3,2,1,0:T(8,128)(2,1)} %pad_maximum_fusion), calls=%async_computation.1 | async-start | bytes 10485760 | tf_op jit(solution)/shard_map/all_to_all | solution.py:163
  348.1 0.6 gather_fusion.3
  348.8 0.7 gather_fusion.4
  349.6 0.7 pad_maximum_fusion.1
  350.3 58.0 %all-to-all-done.1 = bf16[8,4,40,2048]{3,2,1,0:T(8,128)(2,1)} async-done(((bf16[8,4,40,2048]{3,2,1,0:T(8,128)(2,1)}), bf16[8,4,40,2048]{3,2,1,0:T(8,128)(2,1)}, u32[]{:S(2)}, u32[]{:S(2)}) %all-to-all-start.1) | async-done | bytes 5242912 | tf_op jit(solution)/shard_map/all_to_all | solution.py:163
  408.3 12.1 %gather_fusion.2 = bf16[1024,2048]{1,0:T(8,128)(2,1)} fusion(bf16[1280,2048]{1,0:T(8,128)(2,1)} %bitcast.47, s32[1024]{0:T(1024)S(1)} %broadcast_clamp_fusion), kind=kCustom, calls=%fused_computation.3 | custom fusion | bytes 8392704 | tf_op jit(solution)/shard_map/gather | solution.py:164
  420.4 6.5 %fusion = f32[128,2048]{1,0:T(8,128)S(1)} fusion(bf16[1024,2048]{1,0:T(8,128)(2,1)} %gather_fusion.2, f32[128,8]{1,0:T(8,128)S(1)} %copy.56), kind=kLoop, calls=%fused_computation.8 | loop fusion | flops 6029312 | bytes 5246976 | tf_op jit(solution)/shard_map/reduce_sum | solution.py:167
  426.9 0.9 add_convert_fusion
  (88 shorter events, 3.4 us)
Async XLA Ops:
  7.2 22.8 %copy-start = (bf16[128,2048]{1,0:T(8,128)(2,1)S(1)}, bf16[128,2048]{1,0:T(8,128)(2,1)}, u32[]{:S(2)}) copy-start(bf16[128,2048]{1,0:T(8,128)(2,1)} %param.17) | copy-start | bytes 1572868
  7.2 22.3 %copy-start.9 = (s32[128,8]{0,1:T(8,128)S(1)}, s32[128,8]{0,1:T(8,128)}, u32[]{:S(2)}) copy-start(s32[128,8]{0,1:T(8,128)} %param.28) | copy-start | bytes 12292
  7.2 6.6 %copy-start.12 = (s32[2]{0:T(128)S(1)}, s32[2]{0:T(128)}, u32[]{:S(2)}) copy-start(s32[2]{0:T(128)} %param.22) | copy-start | bytes 28
  7.2 6.7 %copy-start.2 = (s32[4]{0:T(128)S(1)}, s32[4]{0:T(128)}, u32[]{:S(2)}) copy-start(s32[4]{0:T(128)} %param.23) | copy-start | bytes 52
  7.2 11.4 %copy-start.4 = (bf16[128,2048]{1,0:T(8,128)(2,1)S(1)}, bf16[128,2048]{1,0:T(8,128)(2,1)}, u32[]{:S(2)}) copy-start(bf16[128,2048]{1,0:T(8,128)(2,1)} %param.19) | copy-start | bytes 1572868
  7.2 22.8 %copy-start.5 = (bf16[128,2048]{1,0:T(8,128)(2,1)S(1)}, bf16[128,2048]{1,0:T(8,128)(2,1)}, u32[]{:S(2)}) copy-start(bf16[128,2048]{1,0:T(8,128)(2,1)} %param.18) | copy-start | bytes 1572868
  7.2 37.8 %all-gather.4.cloned.1.call-start = ((), (), s32[]{:S(2)}) async-start(), calls=%async_computation.2 | async-start | bytes 3538944 | tf_op jit(solution)/shard_map/all_gather | solution.py:79
  8.0 71.3 %all-gather.6.cloned.1.call-start = ((), (), s32[]{:S(2)}) async-start(), calls=%async_computation.3 | async-start | bytes 3538944 | tf_op jit(solution)/shard_map/all_gather | solution.py:80
  8.7 221.8 %all-gather.8.cloned.1.call-start = ((), (), s32[]{:S(2)}) async-start(), calls=%async_computation.4 | async-start | bytes 10485760 | tf_op jit(solution)/shard_map/all_gather | solution.py:121
  60.5 21.8 %copy-start.6 = (f32[16,128,128]{1,2,0:T(8,128)S(1)}, f32[16,128,128]{1,2,0:T(8,128)}, u32[]{:S(2)}) copy-start(f32[16,128,128]{1,2,0:T(8,128)} %get-tuple-element.18) | copy-start | bytes 3145732
  79.3 3.7 copy-start.3
  83.0 3.0 copy-start.8
  86.0 144.5 %copy-start.7 = (bf16[128,2048]{1,0:T(8,128)(2,1)S(1)}, bf16[128,2048]{1,0:T(8,128)(2,1)}, u32[]{:S(2)}) copy-start(bf16[128,2048]{1,0:T(8,128)(2,1)} %param.16) | copy-start | bytes 1572868
  230.5 4.8 %copy-start.10 = (f32[2048]{0:T(1024)S(1)}, f32[2048]{0:T(1024)}, u32[]{:S(2)}) copy-start(f32[2048]{0:T(1024)} %param.27) | copy-start | bytes 24580
  258.7 69.5 %slice-start = ((s8[16777216]{0:T(1024)(128)(4,1)}), s8[4194304]{0:T(1024)(128)(4,1)S(1)}, s32[]{:S(2)}) async-start(s8[16777216]{0:T(1024)(128)(4,1)} %bitcast.202), calls=%async_computation.5 | async-start | bytes 8388608
  258.7 69.5 %slice-start.1 = ((s8[16777216]{0:T(1024)(128)(4,1)}), s8[4194304]{0:T(1024)(128)(4,1)S(1)}, s32[]{:S(2)}) async-start(s8[16777216]{0:T(1024)(128)(4,1)} %bitcast.202), calls=%async_computation.6 | async-start | bytes 8388608
  323.3 5.0 %slice-start.2 = ((s8[16777216]{0:T(1024)(128)(4,1)}), s8[4194304]{0:T(1024)(128)(4,1)S(1)}, s32[]{:S(2)}) async-start(s8[16777216]{0:T(1024)(128)(4,1)} %bitcast.202), calls=%async_computation.7 | async-start | bytes 8388608
  324.1 4.2 slice-start.3
  328.3 4.2 slice-start.4
  329.9 3.0 slice-start.5
  342.9 5.1 %copy-start.13 = (s32[2,16]{1,0:T(2,128)S(1)}, s32[2,16]{1,0:T(2,128)}, u32[]{:S(2)}) copy-start(s32[2,16]{1,0:T(2,128)} %param.21) | copy-start | bytes 388
  342.9 6.5 %copy-start.11 = (f32[128,8]{0,1:T(8,128)S(1)}, f32[128,8]{0,1:T(8,128)}, u32[]{:S(2)}) copy-start(f32[128,8]{0,1:T(8,128)} %param.29) | copy-start | bytes 12292
  342.9 65.4 %all-to-all-start.1 = ((bf16[8,4,40,2048]{3,2,1,0:T(8,128)(2,1)}), bf16[8,4,40,2048]{3,2,1,0:T(8,128)(2,1)}, u32[]{:S(2)}, u32[]{:S(2)}) async-start(bf16[8,4,40,2048]{3,2,1,0:T(8,128)(2,1)} %pad_maximum_fusion), calls=%async_computation.1 | async-start | bytes 10485760 | tf_op jit(solution)/shard_map/all_to_all | solution.py:163
  408.3 19.5 %copy-start.1 = (bf16[128,2048]{1,0:T(8,128)(2,1)S(1)}, bf16[128,2048]{1,0:T(8,128)(2,1)}, u32[]{:S(2)}) copy-start(bf16[128,2048]{1,0:T(8,128)(2,1)} %param.17) | copy-start | bytes 1572868
Sparse Core Ops, SparseCore 0:
  10.0 35.0 all-gather.3
  46.9 32.3 all-gather.5
  80.8 149.6 all-gather.7
where the time goes:
time: 438 us; the launch traced here: 435 us
  waiting for transfers between devices  237 us (54%)
  blocking collectives  64.5 us (15%)
  local copies, waits for them, and re-layouts  56.7 us (13%)
  other arithmetic  28.8 us (7%)
  matrix products  28.3 us (6%)
  between operations  14.6 us (3%)
  starting transfers between devices  5.15 us (1%)
    all_gather x1, waiting for transfers between devices, per_device(): lax.all_gather(out_proj, 'rep', axis=0, tiled=True)  144 us
    all_to_all x1, blocking collectives, per_device(): lax.all_to_all(outgoing, 'ep', split_axis=0, concat_axis=0, tiled=True)  64.5 us
    all_to_all x1, waiting for transfers between devices, per_device(): lax.all_to_all(replies, 'ep', split_axis=0, concat_axis=0, tiled=True)  58 us
    scatter x1, local copies, waits for them, and re-layouts, per_device(): outgoing = jnp.zeros((expert_total * CAP, feature_count), jnp.bfloat16).a...  23.3 us
    all_gather x1, waiting for transfers between devices, per_device(): page_values = lax.all_gather(prompt_values, 'ep', axis=1, tiled=True)  18.8 us
    all_gather x1, waiting for transfers between devices, per_device(): page_keys = lax.all_gather(prompt_keys, 'ep', axis=1, tiled=True)  13.5 us
    gather x1, local copies, waits for them, and re-layouts, per_device(): returned.reshape(expert_total * CAP, feature_count)[target]  12.1 us
    another operation x3, other arithmetic  9.67 us
  transfers between devices with their start and end apart: 4, of which 4 were waited for; matrix products, arithmetic and copies ran while one was open for 11% of the time, Pallas kernels for 0%

commit v1 on v0

v1 whole, which is shorter than its diff:
```python
import math

import jax
import jax.numpy as jnp
from jax import lax
from jax.experimental import pallas as pl
from jax.experimental.pallas import tpu as pltpu
from jax.sharding import PartitionSpec as P

HEADS = 16
HEAD_DIM = 128
CAP = 40

NEG_FILL = -1e30
EPSILON = 1e-05
VMEM_LIMIT = 56 * 1024 * 1024

F32 = jnp.float32
BF16 = jnp.bfloat16


def ancestry(parents):
    tree_width = parents.shape[-1]
    node_ids = jnp.arange(tree_width, dtype=jnp.int32)
    linked = jnp.logical_or(
        parents[..., :, None] == node_ids[None, :], node_ids[:, None] == node_ids[None, :]
    )
    closure = linked.astype(F32)
    for repeat in range(tree_width.bit_length()):
        closure = jnp.minimum(1.0, jnp.einsum("rij,rjk->rik", closure, closure))
    return closure > 0.5


def flip(value, bits, size):
    return lax.ppermute(value, "ep", [(i, i ^ bits) for i in range(size)])


def gather_halves(first, second):
    x_first, y_second = flip(first, 2, 8), flip(second, 4, 8)
    x_second, y_first = flip(second, 2, 8), flip(first, 4, 8)
    s_first, s_second = flip(first, 1, 8), flip(second, 1, 8)
    d_first, d_second = flip(x_first, 4, 8), flip(y_second, 2, 8)
    mine = [(first, second), (x_first, x_second), (y_first, y_second), (d_first, d_second)]
    blocks = []
    for index, pair in enumerate(mine):
        other = (s_first, s_second) if index == 0 else tuple(flip(half, 1, 8) for half in pair)
        blocks += [pair, other]
    return blocks


def attention_body(key_count, *refs):
    queries, tree_keys, tree_values, prompt_bias, tree_bias, accepted = refs[:6]
    keys, values = refs[6 : 6 + key_count], refs[6 + key_count : 6 + 2 * key_count]
    attended, cache, bias = refs[6 + 2 * key_count :]
    rows, features = queries.shape
    prompt_rows = prompt_bias.shape[1]
    request_rows = rows // prompt_bias.shape[0]
    for request in range(prompt_bias.shape[0]):
        bias[request * request_rows : (request + 1) * request_rows, :prompt_rows] = jnp.broadcast_to(
            prompt_bias[request : request + 1, :], (request_rows, prompt_rows)
        )
    bias[:, prompt_rows:] = tree_bias[...]
    scale = 1.0 / math.sqrt(HEAD_DIM)
    for head in range(features // HEAD_DIM):
        lanes = slice(head * HEAD_DIM, (head + 1) * HEAD_DIM)
        all_keys = jnp.concatenate([ref[:, lanes] for ref in keys] + [tree_keys[:, lanes]], axis=0)
        all_values = jnp.concatenate([ref[:, lanes] for ref in values] + [tree_values[:, lanes]], axis=0)
        scores = lax.dot_general(
            queries[:, lanes], all_keys, (((1,), (1,)), ((), ())), preferred_element_type=F32
        )
        scores = scores * scale + bias[...]
        weights = jnp.exp(scores - jnp.max(scores, axis=-1, keepdims=True))
        total = jnp.sum(weights, axis=-1, keepdims=True)
        mixed = jnp.dot(weights.astype(BF16), all_values, preferred_element_type=F32)
        attended[head] = (mixed / total).astype(BF16)
    chosen = accepted[...] == lax.broadcasted_iota(jnp.int32, (accepted.shape[0], rows), 1)
    chosen = jnp.where(chosen, 1.0, 0.0).astype(BF16)
    cache[:, :features] = jnp.dot(chosen, tree_keys[...], preferred_element_type=F32).astype(BF16)
    cache[:, features:] = jnp.dot(chosen, tree_values[...], preferred_element_type=F32).astype(BF16)


def attention(queries, tree_keys, tree_values, prompt_bias, tree_bias, accepted, keys, values):
    rows, features = queries.shape
    heads = features // HEAD_DIM
    width = prompt_bias.shape[1] + rows
    return pl.pallas_call(
        lambda *refs: attention_body(len(keys), *refs),
        out_shape=(
            jax.ShapeDtypeStruct((heads, rows, HEAD_DIM), BF16),
            jax.ShapeDtypeStruct((accepted.shape[0], 2 * features), BF16),
        ),
        scratch_shapes=[pltpu.VMEM((rows, width), F32)],
        compiler_params=pltpu.CompilerParams(vmem_limit_bytes=VMEM_LIMIT),
        cost_estimate=pl.CostEstimate(
            flops=4 * rows * width * features, bytes_accessed=8 * 2**20, transcendentals=heads * rows * width
        ),
        name="attention",
    )(queries, tree_keys, tree_values, prompt_bias, tree_bias, accepted, *keys, *values)


def project_body(layout, head_order, attended, hidden, gain, *refs):
    weights = refs[: len(refs) - 4]
    residual, normed_first, normed_second, ordered = refs[len(refs) - 4 :]
    rows, features = hidden.shape
    for index in range(features // HEAD_DIM):
        ordered[:, index * HEAD_DIM : (index + 1) * HEAD_DIM] = attended[head_order[index]]
    step = 256
    squares = jnp.zeros((rows, 1), F32)
    for column in range(0, features, step):
        pieces = []
        for parts in layout:
            for ref_index, low, high in parts:
                if low <= column < high:
                    pieces.append(weights[ref_index][:, column - low : column - low + step])
        joined = jnp.concatenate(pieces, axis=0)
        total = jnp.dot(ordered[...], joined, preferred_element_type=F32)
        total = total + hidden[:, column : column + step].astype(F32)
        residual[:, column : column + step] = total
        squares = squares + jnp.sum(total * total, axis=-1, keepdims=True)
    factor = lax.rsqrt(squares / features + EPSILON)
    half = rows // 2
    normed_first[...] = (residual[:half, :] * factor[:half] * gain[...]).astype(BF16)
    normed_second[...] = (residual[half:, :] * factor[half:] * gain[...]).astype(BF16)


def project(head_order, attended, hidden, gain, weights, layout):
    rows, features = hidden.shape
    whole = pl.BlockSpec(memory_space=pltpu.VMEM)
    return pl.pallas_call(
        lambda *refs: project_body(layout, *refs),
        out_shape=(
            jax.ShapeDtypeStruct((rows, features), F32),
            jax.ShapeDtypeStruct((rows // 2, features), BF16),
            jax.ShapeDtypeStruct((rows // 2, features), BF16),
        ),
        in_specs=[pl.BlockSpec(memory_space=pltpu.SMEM)] + [whole] * (3 + len(weights)),
        out_specs=(whole,) * 3,
        scratch_shapes=[pltpu.VMEM((rows, features), BF16)],
        compiler_params=pltpu.CompilerParams(vmem_limit_bytes=VMEM_LIMIT),
        cost_estimate=pl.CostEstimate(
            flops=2 * rows * features * features, bytes_accessed=10 * 2**20, transcendentals=0
        ),
        name="project",
    )(head_order, attended, hidden, gain, *weights)


def fetch_projection(out_proj):
    shard_rows, features = out_proj.shape
    heads_here = shard_rows // HEAD_DIM
    me, core = lax.axis_index("rep"), lax.axis_index("ep")
    parity = (core // 2 + core // 4) % 2
    quarter = 2 * parity + core % 2
    far = 2 * (1 - parity) + core % 2
    block = lax.dynamic_slice_in_dim(out_proj, quarter * HEAD_DIM, HEAD_DIM, 0)
    up1 = lax.ppermute(block, "rep", [(0, 1), (1, 2), (2, 3)])
    down1 = lax.ppermute(block, "rep", [(1, 0), (2, 1), (3, 2)])
    up2 = lax.ppermute(up1, "rep", [(1, 2), (2, 3)])
    down2 = lax.ppermute(down1, "rep", [(1, 0), (2, 1)])
    up3 = lax.ppermute(up2, "rep", [(2, 3)])
    down3 = lax.ppermute(down2, "rep", [(1, 0)])
    came = [
        jnp.where(me == 0, down1, up1),
        jnp.where(me == 0, down2, jnp.where(me == 3, up2, down1)),
        jnp.where(me == 0, down3, jnp.where(me == 1, down2, jnp.where(me == 2, up2, up3))),
    ]
    shards = [
        jnp.where(me == 0, 1, me - 1),
        jnp.where(me == 0, 2, jnp.where(me == 3, 1, me + 1)),
        jnp.where(me == 0, 3, jnp.where(me == 1, 3, 0)),
    ]
    half = features // 2
    weights, layout = [out_proj], [[(0, 0, features)]]
    order = [me * heads_here + i for i in range(heads_here)]
    for arrived, shard in zip(came, shards):
        left, right = flip(arrived[:, :half], 2, 8), flip(arrived[:, half:], 4, 8)
        first = len(weights)
        weights += [arrived, flip(arrived, 1, 8), left, right, flip(left, 1, 8), flip(right, 1, 8)]
        layout += [
            [(first, 0, features)],
            [(first + 1, 0, features)],
            [(first + 2, 0, half), (first + 3, half, features)],
            [(first + 4, 0, half), (first + 5, half, features)],
        ]
        base = shard * heads_here
        order += [base + quarter, base + (quarter ^ 1), base + far, base + (far ^ 1)]
    return weights, layout, jnp.stack(order).astype(jnp.int32)


def experts_body(source_count, per_pair, first_expert, ids, gates, gate_up_hbm, down_hbm, *refs):
    sources = refs[:source_count]
    same_core, other_core = refs[source_count : source_count + 2]
    gate_up, down, picked, produced, hidden, chosen, slot_gates, sems = refs[source_count + 2 :]
    local_experts, features, _ = gate_up.shape
    units = down.shape[1]
    pairs, top, tokens = ids.shape
    slots = 2 * CAP
    copies = []
    for expert in range(local_experts):
        copies.append(
            (
                pltpu.make_async_copy(gate_up_hbm.at[expert], gate_up.at[expert], sems.at[0, expert]),
                pltpu.make_async_copy(down_hbm.at[expert], down.at[expert], sems.at[1, expert]),
            )
        )
        copies[-1][0].start()
        copies[-1][1].start()
    earlier = lax.broadcasted_iota(jnp.int32, (tokens, tokens), 0)
    later = lax.broadcasted_iota(jnp.int32, (tokens, tokens), 1)
    before = jnp.where(earlier < later, 1.0, 0.0).astype(BF16)
    slot_ids = lax.broadcasted_iota(jnp.int32, (slots, tokens), 0).astype(F32)
    for pair in range(pairs):
        hits, shares = [], []
        for expert in range(local_experts):
            match = ids[pair] == first_expert[0] + expert
            hits.append(jnp.max(jnp.where(match, 1.0, 0.0), axis=0, keepdims=True))
            shares.append(jnp.sum(jnp.where(match, gates[pair], 0.0), axis=0, keepdims=True))
        stacked = jnp.concatenate(hits + [jnp.zeros((16 - local_experts, tokens), F32)], axis=0)
        places = jnp.dot(stacked.astype(BF16), before, preferred_element_type=F32)
        for expert in range(local_experts):
            place = jnp.where(hits[expert] > 0.5, places[expert : expert + 1], -1.0)
            taken = jnp.where(slot_ids == place, 1.0, 0.0)
            chosen[pair, expert * slots : (expert + 1) * slots, :] = taken.astype(BF16)
            slot_gates[expert, pair * slots : (pair + 1) * slots, :] = jnp.sum(
                taken * shares[expert], axis=1, keepdims=True
            )
        group = sources[pair * per_pair : (pair + 1) * per_pair]
        step = 512
        for column in range(0, features, step):
            rows = jnp.concatenate([ref[:, column : column + step] for ref in group], axis=0)
            for expert in range(local_experts):
                picked[expert, pair * slots : (pair + 1) * slots, column : column + step] = jnp.dot(
                    chosen[pair, expert * slots : (expert + 1) * slots, :], rows, preferred_element_type=F32
                ).astype(BF16)
    chunk = slots * min(pairs, 4)
    for expert in range(local_experts):
        copies[expert][0].wait()
        for low in range(0, pairs * slots, chunk):
            rows = picked[expert, low : low + chunk, :]
            gate_rows = slot_gates[expert, low : low + chunk, :]
            for column in range(0, units, 256):
                gate = jnp.dot(rows, gate_up[expert, :, column : column + 256], preferred_element_type=F32)
                up = jnp.dot(
                    rows, gate_up[expert, :, units + column : units + column + 256], preferred_element_type=F32
                )
                active = gate / (1.0 + jnp.exp(-gate)) * up * gate_rows
                hidden[low : low + chunk, column : column + 256] = active.astype(BF16)
        copies[expert][1].wait()
        for low in range(0, pairs * slots, chunk):
            for column in range(0, features, 512):
                result = jnp.dot(
                    hidden[low : low + chunk, :], down[expert, :, column : column + 512], preferred_element_type=F32
                ).astype(BF16)
                for inner in range(chunk // slots):
                    produced[
                        low // slots + inner, expert * slots : (expert + 1) * slots, column : column + 512
                    ] = result[inner * slots : (inner + 1) * slots]
    for pair in range(pairs):
        for column in range(0, features, 512):
            mixture = lax.dot_general(
                chosen[pair], produced[pair, :, column : column + 512], (((0,), (0,)), ((), ())),
                preferred_element_type=F32,
            ).astype(BF16)
            same_core[pair, :, column : column + 512] = mixture[: tokens // 2]
            other_core[pair, :, column : column + 512] = mixture[tokens // 2 :]


def experts(first_expert, ids, gates, gate_up, down, sources, per_pair):
    pairs, top, tokens = ids.shape
    local_experts, features, _ = gate_up.shape
    units = down.shape[1]
    slots = 2 * CAP
    whole = pl.BlockSpec(memory_space=pltpu.VMEM)
    hbm = pl.BlockSpec(memory_space=pl.ANY)
    return pl.pallas_call(
        lambda *refs: experts_body(len(sources), per_pair, *refs),
        out_shape=(jax.ShapeDtypeStruct((pairs, tokens // 2, features), BF16),) * 2,
        in_specs=[pl.BlockSpec(memory_space=pltpu.SMEM), whole, whole, hbm, hbm] + [whole] * len(sources),
        out_specs=(whole, whole),
        scratch_shapes=[
            pltpu.VMEM(gate_up.shape, BF16),
            pltpu.VMEM(down.shape, BF16),
            pltpu.VMEM((local_experts, pairs * slots, features), BF16),
            pltpu.VMEM((pairs, local_experts * slots, features), BF16),
            pltpu.VMEM((pairs * slots, units), BF16),
            pltpu.VMEM((pairs, local_experts * slots, tokens), BF16),
            pltpu.VMEM((local_experts, pairs * slots, 1), F32),
            pltpu.SemaphoreType.DMA((2, local_experts)),
        ],
        compiler_params=pltpu.CompilerParams(vmem_limit_bytes=VMEM_LIMIT),
        cost_estimate=pl.CostEstimate(
            flops=6 * local_experts * pairs * slots * features * units, bytes_accessed=32 * 2**20, transcendentals=0
        ),
        name="experts",
    )(first_expert, ids, gates, gate_up, down, *sources)


def add_rows(left, right):
    return (left.astype(F32) + right.astype(F32)).astype(BF16)


def return_sums(same_core, other_core):
    swapped = flip(other_core, 1, 8)
    near_x, near_y, across = [add_rows(same_core[g], swapped[g]) for g in (1, 2, 3)]
    half = near_x.shape[0] // 2
    across_first, across_second = flip(across[:half], 2, 8), flip(across[half:], 4, 8)
    x_first, y_second = flip(near_x[:half], 2, 8), flip(near_y[half:], 4, 8)
    x_second = flip(add_rows(near_x[half:], across_second), 2, 8)
    y_first = flip(add_rows(near_y[:half], across_first), 4, 8)
    return [
        same_core[0].astype(F32),
        swapped[0].astype(F32),
        jnp.concatenate([x_first, x_second], axis=0).astype(F32),
        jnp.concatenate([y_first, y_second], axis=0).astype(F32),
    ]


def per_device(
    hidden_in,
    tree_queries,
    tree_keys,
    tree_values,
    tree_parents,
    accepted_nodes,
    request_prompt,
    prompt_lengths,
    prompt_keys,
    prompt_values,
    out_proj,
    norm_gain,
    expert_ids,
    gate_weights,
    expert_gate_up,
    expert_down,
):
    tok_rows, features = hidden_in.shape
    req_count, tree_len = tree_parents.shape
    prompt_count, rows_here, _ = prompt_keys.shape
    top_count = expert_ids.shape[1]
    local_experts = expert_gate_up.shape[0]
    ep_size, rep_size = lax.axis_size("ep"), lax.axis_size("rep")
    me = lax.axis_index("ep")
    planes = ep_size == 8

    if planes:
        flat = (prompt_count * rows_here, features)
        blocks = gather_halves(prompt_keys.reshape(flat), prompt_values.reshape(flat))
        keys, values = [block[0] for block in blocks], [block[1] for block in blocks]
        source = me ^ jnp.arange(ep_size, dtype=jnp.int32)
        position = source[:, None, None] * rows_here + jnp.arange(rows_here, dtype=jnp.int32)[None, None, :]
        shape = (ep_size, prompt_count, rows_here)
        position = jnp.broadcast_to(position, shape).reshape(-1)
        prompt = jnp.broadcast_to(jnp.arange(prompt_count, dtype=jnp.int32)[None, :, None], shape).reshape(-1)
    else:
        all_rows = rows_here * ep_size
        keys = [lax.all_gather(prompt_keys, "ep", axis=1, tiled=True).reshape(-1, features)]
        values = [lax.all_gather(prompt_values, "ep", axis=1, tiled=True).reshape(-1, features)]
        position = jnp.tile(jnp.arange(all_rows, dtype=jnp.int32), prompt_count)
        prompt = jnp.repeat(jnp.arange(prompt_count, dtype=jnp.int32), all_rows)
    request_length = prompt_lengths[request_prompt]
    in_prompt = (prompt[None, :] == request_prompt[:, None]) & (position[None, :] < request_length[:, None])
    prompt_bias = jnp.where(in_prompt, 0.0, NEG_FILL).astype(F32)

    if planes and rep_size == 4 and out_proj.shape[0] == 4 * HEAD_DIM:
        proj_weights, proj_layout, head_order = fetch_projection(out_proj)
    else:
        proj_weights = [lax.all_gather(out_proj, "rep", axis=0, tiled=True)]
        proj_layout = [[(0, 0, features)]]
        head_order = jnp.arange(features // HEAD_DIM, dtype=jnp.int32)

    routing = jnp.concatenate([expert_ids.astype(F32).T, gate_weights.T], axis=0)
    routing = lax.all_gather(routing, "ep", axis=0)
    if planes:
        routing = routing[source]
    routing = routing.reshape(ep_size // 2, 2, 2 * top_count, tok_rows)
    routing = jnp.concatenate([routing[:, 0], routing[:, 1]], axis=-1)
    all_ids, all_gates = routing[:, :top_count].astype(jnp.int32), routing[:, top_count:]

    tree_seen = ancestry(tree_parents)
    same_request = jnp.eye(req_count, dtype=jnp.bool_)
    tree_visible = (tree_seen[:, :, None, :] & same_request[:, None, :, None]).reshape(tok_rows, tok_rows)
    tree_bias = jnp.where(tree_visible, 0.0, NEG_FILL).astype(F32)
    accepted = (jnp.arange(req_count, dtype=jnp.int32)[:, None] * tree_len + accepted_nodes).reshape(-1, 1)
    attended, cache = attention(
        tree_queries, tree_keys, tree_values, prompt_bias, tree_bias, accepted, keys, values
    )
    accepted_cache = cache.reshape(req_count, accepted_nodes.shape[1], 2 * features)

    residual, normed_first, normed_second = project(
        head_order, attended, hidden_in, norm_gain.reshape(1, features), proj_weights, proj_layout
    )

    first_expert = (me * local_experts).astype(jnp.int32).reshape(1)
    if planes:
        sources = [half for block in gather_halves(normed_first, normed_second) for half in block]
        per_pair = 4
    else:
        everyone = lax.all_gather(jnp.concatenate([normed_first, normed_second], axis=0), "ep", axis=0, tiled=True)
        sources = [everyone[i * 2 * tok_rows : (i + 1) * 2 * tok_rows] for i in range(ep_size // 2)]
        per_pair = 1
    same_core, other_core = experts(
        first_expert, all_ids, all_gates, expert_gate_up, expert_down, sources, per_pair
    )
    if planes:
        terms = return_sums(same_core, other_core)
    else:
        shares = jnp.stack([same_core, other_core], axis=1).reshape(ep_size, tok_rows, features)
        shares = lax.all_to_all(shares, "ep", split_axis=0, concat_axis=0, tiled=True)
        terms = [jnp.sum(shares.astype(F32), axis=0)]
    layer_out = residual
    for term in terms:
        layer_out = layer_out + term
    return (layer_out.astype(BF16), accepted_cache)


def solution(mesh):
    in_specs = (
        P(("rep", "ep"), None),
        P(("rep", "ep"), None),
        P(("rep", "ep"), None),
        P(("rep", "ep"), None),
        P(("rep", "ep"), None),
        P(("rep", "ep"), None),
        P(("rep", "ep")),
        P("rep"),
        P("rep", "ep", None),
        P("rep", "ep", None),
        P("rep", None),
        P(),
        P(("rep", "ep"), None),
        P(("rep", "ep"), None),
        P("ep", None, None),
        P("ep", None, None),
    )
    out_specs = (P(("rep", "ep"), None), P(("rep", "ep"), None, None))
    return jax.shard_map(
        per_device, mesh=mesh, in_specs=in_specs, out_specs=out_specs, check_vma=False
    )
```

time: 438 us -> 196 us (0.45)
  waiting for transfers between devices: 237 us -> 82.4 us
  blocking collectives: 64.5 us -> 10.4 us
  local copies, waits for them, and re-layouts: 56.7 us -> 10.5 us
  starting transfers between devices: 5.15 us -> 42 us
  Pallas kernels: 0 us -> 36.1 us
  matrix products: 28.3 us -> 3.92 us
  other arithmetic: 28.8 us -> 9.18 us
  between operations: 14.6 us -> 1.32 us
    all_gather x3 -> x0, waiting for transfers between devices: 176 us -> none  [the longest x1 144 us: per_device(): lax.all_gather(out_proj, 'rep', axis=0, tiled=True)]
    ppermute x0 -> x56, waiting for transfers between devices: none -> 82.4 us  [the longest x50 54.7 us: flip(): return lax.ppermute(value, 'ep', [(i, i ^ bits) for i in range(size)])]
    all_to_all x1 -> x0, blocking collectives: 64.5 us -> none  [per_device(): lax.all_to_all(outgoing, 'ep', split_axis=0, concat_axis=0, tiled=True)]
    all_to_all x1 -> x0, waiting for transfers between devices: 58 us -> none  [per_device(): lax.all_to_all(replies, 'ep', split_axis=0, concat_axis=0, tiled=True)]
    ppermute x0 -> x56, starting transfers between devices: none -> 42 us  [the longest x50 31.8 us: flip(): return lax.ppermute(value, 'ep', [(i, i ^ bits) for i in range(size)])]
    pallas_call x0 -> x3, Pallas kernels: none -> 36.1 us  [the longest x1 19.8 us: experts(): pl.pallas_call(lambda *refs: experts_body(len(sources), per_pair, *refs),...]
    dot_general x19 -> x4, matrix products: 27.3 us -> 3.92 us  [ancestry(): closure = jnp.minimum(1.0, jnp.einsum('rij,rjk->rik', closure, closure))]
    scatter x1 -> x0, local copies, waits for them, and re-layouts: 23.3 us -> none  [per_device(): outgoing = jnp.zeros((expert_total * CAP, feature_count), jnp.bfloat16).a...]
  transfers between devices with their start and end apart: 4 -> 56, of which waited for: 4 -> 22; matrix products, arithmetic and copies ran while one was open for 11% -> 8% of each run, Pallas kernels for 0% -> 5%
where the time goes in v1:
time: 196 us
  waiting for transfers between devices  82.4 us (42%)
  starting transfers between devices  42 us (21%)
  Pallas kernels  36.1 us (18%)
  local copies, waits for them, and re-layouts  10.5 us (5%)
  blocking collectives  10.4 us (5%)
  other arithmetic  9.18 us (5%)
  matrix products  3.92 us (2%)
    ppermute x50, waiting for transfers between devices, flip(): return lax.ppermute(value, 'ep', [(i, i ^ bits) for i in range(size)])  54.7 us
    ppermute x50, starting transfers between devices, flip(): return lax.ppermute(value, 'ep', [(i, i ^ bits) for i in range(size)])  31.8 us
    pallas_call x1, Pallas kernels, experts(): pl.pallas_call(lambda *refs: experts_body(len(sources), per_pair, *refs),...  19.8 us
    ppermute x1, waiting for transfers between devices, fetch_projection(): down2 = lax.ppermute(down1, 'rep', [(1, 0), (2, 1)])  11.5 us
    all_gather x1, blocking collectives, per_device(): routing = lax.all_gather(routing, 'ep', axis=0)  10.4 us
    pallas_call x1, Pallas kernels, attention(): pl.pallas_call(lambda *refs: attention_body(len(keys), *refs), out_shape=...  10.1 us
    ppermute x1, waiting for transfers between devices, fetch_projection(): down3 = lax.ppermute(down2, 'rep', [(1, 0)])  7.02 us
    pallas_call x1, Pallas kernels, project(): pl.pallas_call(lambda *refs: project_body(layout, *refs), out_shape=(jax....  6.21 us
  transfers between devices with their start and end apart: 56, of which 22 were waited for; matrix products, arithmetic and copies ran while one was open for 8% of the time, Pallas kernels for 5%

profile of v1, /device:TPU:0, one launch (start us, length us, event | category | flops | bytes accessed | tf_op | source)
XLA Modules:
  0.0 195.8 jit_solution(8464457312852208079)
XLA Ops:
  0.7 1.1 constant_dynamic-slice_fusion
  1.8 5.0 %collective-permute-start.15 = (bf16[128,2048]{1,0:T(8,128)(2,1)S(1)}, bf16[128,2048]{1,0:T(8,128)(2,1)S(1)}, u32[]{:S(2)}, u32[]{:S(2)}) collective-permute-start(bf16[128,2048]{1,0:T(8,128)(2,1)S(1)} %constant_dynamic-slice_fusion), channel_id=1, source_target_pairs={{0,8},{8,16},{16,24},{1,9},{9,17},{17,25},{2,10},{10,18},{18,26},{... | collective-permute-start | bytes 1572872 | tf_op jit(solution)/shard_map/ppermute | solution.py:155
  6.7 1.3 collective-permute-start.14
  8.0 1.6 collective-permute-start.3
  9.6 1.5 collective-permute-start.1
  11.1 1.0 convolution_minimum_fusion.6
  12.1 5.8 %collective-permute-done.15 = bf16[128,2048]{1,0:T(8,128)(2,1)S(1)} collective-permute-done((bf16[128,2048]{1,0:T(8,128)(2,1)S(1)}, bf16[128,2048]{1,0:T(8,128)(2,1)S(1)}, u32[]{:S(2)}, u32[]{:S(2)}) %collective-permute-start.15) | collective-permute-done | bytes 524320 | tf_op jit(solution)/shard_map/ppermute | solution.py:155
  18.6 3.5 %collective-permute-done.14 = bf16[128,2048]{1,0:T(8,128)(2,1)S(1)} collective-permute-done((bf16[128,2048]{1,0:T(8,128)(2,1)S(1)}, bf16[128,2048]{1,0:T(8,128)(2,1)S(1)}, u32[]{:S(2)}, u32[]{:S(2)}) %collective-permute-start.14) | collective-permute-done | bytes 524320 | tf_op jit(solution)/shard_map/ppermute | solution.py:156
  22.0 1.3 collective-permute-start.21
  23.6 0.9 convolution_minimum_fusion.2
  25.2 11.5 %collective-permute-done.21 = bf16[128,2048]{1,0:T(8,128)(2,1)S(1)} collective-permute-done((bf16[128,2048]{1,0:T(8,128)(2,1)S(1)}, bf16[128,2048]{1,0:T(8,128)(2,1)S(1)}, u32[]{:S(2)}, u32[]{:S(2)}) %collective-permute-start.21) | collective-permute-done | bytes 524320 | tf_op jit(solution)/shard_map/ppermute | solution.py:158
  36.7 1.3 collective-permute-start.28
  38.5 1.8 fusion
  40.3 1.5 collective-permute-start.10
  41.9 1.5 collective-permute-start.8
  43.4 7.0 %collective-permute-done.28 = bf16[128,2048]{1,0:T(8,128)(2,1)S(1)} collective-permute-done((bf16[128,2048]{1,0:T(8,128)(2,1)S(1)}, bf16[128,2048]{1,0:T(8,128)(2,1)S(1)}, u32[]{:S(2)}, u32[]{:S(2)}) %collective-permute-start.28) | collective-permute-done | bytes 524320 | tf_op jit(solution)/shard_map/ppermute | solution.py:160
  51.2 1.7 select_select_fusion
  52.9 1.6 collective-permute-start.5
  54.7 1.5 collective-permute-start.12
  56.8 7.9 %collective-permute-done.5.refs_12_ = bf16[96,2048]{1,0:T(8,128)(2,1)S(1)} collective-permute-done((bf16[96,2048]{1,0:T(8,128)(2,1)}, bf16[96,2048]{1,0:T(8,128)(2,1)S(1)}, u32[]{:S(2)}, u32[]{:S(2)}) %collective-permute-start.5) | collective-permute-done | bytes 393248 | tf_op jit(solution)/shard_map/ppermute | solution.py:35
  64.7 1.3 collective-permute-done.12.refs_20_
  66.8 1.5 collective-permute-start.31
  68.3 1.4 collective-permute-start.25
  71.0 4.2 %collective-permute-done.32.refs_20_ = bf16[128,1024]{1,0:T(8,128)(2,1)S(1)} collective-permute-done((bf16[128,1024]{1,0:T(8,128)(2,1)S(1)}, bf16[128,1024]{1,0:T(8,128)(2,1)S(1)}, u32[]{:S(2)}, u32[]{:S(2)}) %collective-permute-start.32) | collective-permute-done | bytes 262176 | tf_op jit(solution)/shard_map/ppermute | solution.py:35
  75.2 1.5 collective-permute-start.17
  76.7 4.2 %collective-permute-done.25.refs_14_ = bf16[128,1024]{1,0:T(8,128)(2,1)} collective-permute-done((bf16[128,1024]{1,0:T(8,128)(2,1)S(1)}, bf16[128,1024]{1,0:T(8,128)(2,1)}, u32[]{:S(2)}, u32[]{:S(2)}) %collective-permute-start.25) | collective-permute-done | bytes 262176 | tf_op jit(solution)/shard_map/ppermute | solution.py:35
  81.7 4.3 %collective-permute-done.18.refs_8_ = bf16[128,1024]{1,0:T(8,128)(2,1)S(1)} collective-permute-done((bf16[128,1024]{1,0:T(8,128)(2,1)S(1)}, bf16[128,1024]{1,0:T(8,128)(2,1)S(1)}, u32[]{:S(2)}, u32[]{:S(2)}) %collective-permute-start.18) | collective-permute-done | bytes 262176 | tf_op jit(solution)/shard_map/ppermute | solution.py:35
  95.7 10.1 %attention.1 = (bf16[16,128,128]{2,1,0:T(8,128)(2,1)}, bf16[32,4096]{1,0:T(8,128)(2,1)}) custom-call(bf16[128,2048]{1,0:T(8,128)(2,1)} %refs_0_.1, bf16[128,2048]{1,0:T(8,128)(2,1)} %refs_1_.1, bf16[128,2048]{1,0:T(8,128)(2,1)} %refs_2_.2, f32[2,768]{1,0:T(2,128)} %and_select_fusion.1.refs_3_, f32[128,128]{1,0:T(8,128)} %select_n.110.refs_4_, ...), custom_call_target="tpu_custom_call" | custom-call | flops 939524096 | bytes 8388608 | tf_op jit(solution)/shard_map/attention/pallas_call | solution.py:86
  107.2 6.2 %project.1 = (f32[128,2048]{1,0:T(8,128)}, bf16[64,2048]{1,0:T(8,128)(2,1)}, bf16[64,2048]{1,0:T(8,128)(2,1)}) custom-call(s32[16]{0:T(128)} %stack.67.refs_0_, bf16[16,128,128]{2,1,0:T(8,128)(2,1)} %get-tuple-element.9.refs_1_, bf16[128,2048]{1,0:T(8,128)(2,1)} %refs_2_.3, f32[1,2048]{1,0:T(1,128)} %bitcast.78, bf16[512,2048]{1,0:T(8,128)(2,1)} %refs_4_.2, ...), custom_call_target="tpu_custom_call" | custom-call | flops 1073741824 | bytes 10485760 | tf_op jit(solution)/shard_map/project/pallas_call | solution.py:129
  113.4 1.5 collective-permute-start.41
  114.9 1.5 collective-permute-start.37
  117.5 5.3 %collective-permute-done.41.refs_13_ = bf16[64,2048]{1,0:T(8,128)(2,1)S(1)} collective-permute-done((bf16[64,2048]{1,0:T(8,128)(2,1)}, bf16[64,2048]{1,0:T(8,128)(2,1)S(1)}, u32[]{:S(2)}, u32[]{:S(2)}) %collective-permute-start.41) | collective-permute-done | bytes 262176 | tf_op jit(solution)/shard_map/ppermute | solution.py:35
  122.7 1.6 collective-permute-done.37.refs_9_
  124.9 3.2 %collective-permute-done.42.refs_14_ = bf16[64,2048]{1,0:T(8,128)(2,1)S(1)} collective-permute-done((bf16[64,2048]{1,0:T(8,128)(2,1)}, bf16[64,2048]{1,0:T(8,128)(2,1)S(1)}, u32[]{:S(2)}, u32[]{:S(2)}) %collective-permute-start.42) | collective-permute-done | bytes 262176 | tf_op jit(solution)/shard_map/ppermute | solution.py:35
  128.1 1.6 collective-permute-start.46
  129.7 10.4 %all-gather = f32[128,128]{1,0:T(8,128)S(1)} all-gather(f32[16,128]{1,0:T(8,128)S(1)} %pad_maximum_fusion.1), channel_id=2, replica_groups=mesh['rep'=4,'ep'=8] {'ep'}, dimensions={0}, use_global_device_ids=true | all-gather | bytes 73728 | tf_op jit(solution)/shard_map/all_gather | solution.py:371
  144.5 19.8 %experts.1 = (bf16[4,128,2048]{2,1,0:T(8,128)(2,1)}, bf16[4,128,2048]{2,1,0:T(8,128)(2,1)}) custom-call(s32[1]{0:T(128)} %bitcast.19.refs_0_, s32[4,8,256]{2,1,0:T(8,128)} %get-tuple-element.31.refs_1_, f32[4,8,256]{2,1,0:T(8,128)} %get-tuple-element.30.refs_2_, bf16[4,2048,1024]{2,1,0:T(8,128)(2,1)} %refs_3_.1, bf16[4,512,2048]{2,1,0:T(8,128)(2,1)} %refs_4_.3, ...), custom_call_target="tpu_custom_call" | custom-call | flops 8053063680 | bytes 33554432 | tf_op jit(solution)/shard_map/experts/pallas_call | solution.py:274
  164.7 4.0 %collective-permute-done.49 = bf16[4,128,2048]{2,1,0:T(8,128)(2,1)S(1)} collective-permute-done((bf16[4,128,2048]{2,1,0:T(8,128)(2,1)}, bf16[4,128,2048]{2,1,0:T(8,128)(2,1)S(1)}, u32[]{:S(2)}, u32[]{:S(2)}) %collective-permute-start.49) | collective-permute-done | bytes 2097184 | tf_op jit(solution)/shard_map/ppermute | solution.py:35
  168.7 1.8 add_convert_fusion
  170.6 0.9 collective-permute-start.50
  171.5 1.2 collective-permute-start.53
  172.7 0.9 collective-permute-start.55
  173.6 1.2 collective-permute-start.51
  174.8 10.0 %collective-permute-done.53 = bf16[64,2048]{1,0:T(8,128)(2,1)S(1)} collective-permute-done((bf16[64,2048]{1,0:T(8,128)(2,1)S(1)}, bf16[64,2048]{1,0:T(8,128)(2,1)S(1)}, u32[]{:S(2)}, u32[]{:S(2)}) %collective-permute-start.53) | collective-permute-done | bytes 262176 | tf_op jit(solution)/shard_map/ppermute | solution.py:35
  184.9 0.9 collective-permute-start.54
  187.3 5.4 %collective-permute-done.54 = bf16[64,2048]{1,0:T(8,128)(2,1)S(1)} collective-permute-done((bf16[64,2048]{1,0:T(8,128)(2,1)S(1)}, bf16[64,2048]{1,0:T(8,128)(2,1)S(1)}, u32[]{:S(2)}, u32[]{:S(2)}) %collective-permute-start.54) | collective-permute-done | bytes 262176 | tf_op jit(solution)/shard_map/ppermute | solution.py:35
  192.7 0.9 collective-permute-done.52
  193.6 2.2 %fusion.3 = bf16[128,2048]{1,0:T(8,128)(2,1)} fusion(f32[128,2048]{1,0:T(8,128)S(1)} %copy-done.4, bf16[4,128,2048]{2,1,0:T(8,128)(2,1)S(1)} %collective-permute-done.49, bf16[64,2048]{1,0:T(8,128)(2,1)S(1)} %collective-permute-done.52, bf16[64,2048]{1,0:T(8,128)(2,1)S(1)} %collective-permute-done.50, bf16[64,2048]{1,0:T(8,128)(2,1)S(1)} %collective-permute-done.55, ...), kind=kLoop, calls=%fused_computation.13 | loop fusion | flops 3932160 | bytes 3670016 | tf_op jit(solution)/shard_map/convert_element_type | solution.py:412
  (211 shorter events, 25.5 us)
Async XLA Ops:
  1.8 16.1 %collective-permute-start.15 = (bf16[128,2048]{1,0:T(8,128)(2,1)S(1)}, bf16[128,2048]{1,0:T(8,128)(2,1)S(1)}, u32[]{:S(2)}, u32[]{:S(2)}) collective-permute-start(bf16[128,2048]{1,0:T(8,128)(2,1)S(1)} %constant_dynamic-slice_fusion), channel_id=1, source_target_pairs={{0,8},{8,16},{16,24},{1,9},{9,17},{17,25},{2,10},{10,18},{18,26},{... | collective-permute-start | bytes 1572872 | tf_op jit(solution)/shard_map/ppermute | solution.py:155
  6.7 15.3 %collective-permute-start.14 = (bf16[128,2048]{1,0:T(8,128)(2,1)S(1)}, bf16[128,2048]{1,0:T(8,128)(2,1)S(1)}, u32[]{:S(2)}, u32[]{:S(2)}) collective-permute-start(bf16[128,2048]{1,0:T(8,128)(2,1)S(1)} %constant_dynamic-slice_fusion), channel_id=1, source_target_pairs={{8,0},{16,8},{24,16},{9,1},{17,9},{25,17},{10,2},{18,10},{26,18},{... | collective-permute-start | bytes 1572872 | tf_op jit(solution)/shard_map/ppermute | solution.py:156
  8.0 32.3 %collective-permute-start.3 = (bf16[96,2048]{1,0:T(8,128)(2,1)}, bf16[96,2048]{1,0:T(8,128)(2,1)S(1)}, u32[]{:S(2)}, u32[]{:S(2)}) collective-permute-start(bf16[96,2048]{1,0:T(8,128)(2,1)} %bitcast.68), channel_id=1, source_target_pairs={{0,4},{1,5},{2,6},{3,7},{4,0},{5,1},{6,2},{7,3},{8,12},{9,13},{10,... | collective-permute-start | bytes 1179656 | tf_op jit(solution)/shard_map/ppermute | solution.py:35
  9.6 32.2 %collective-permute-start.1 = (bf16[96,2048]{1,0:T(8,128)(2,1)}, bf16[96,2048]{1,0:T(8,128)(2,1)}, u32[]{:S(2)}, u32[]{:S(2)}) collective-permute-start(bf16[96,2048]{1,0:T(8,128)(2,1)} %bitcast.69), channel_id=1, source_target_pairs={{0,2},{1,3},{2,0},{3,1},{4,6},{5,7},{6,4},{7,5},{8,10},{9,11},{10,... | collective-permute-start | bytes 1179656 | tf_op jit(solution)/shard_map/ppermute | solution.py:35
  11.1 41.8 %collective-permute-start = (bf16[96,2048]{1,0:T(8,128)(2,1)}, bf16[96,2048]{1,0:T(8,128)(2,1)}, u32[]{:S(2)}, u32[]{:S(2)}) collective-permute-start(bf16[96,2048]{1,0:T(8,128)(2,1)} %bitcast.70), channel_id=1, source_target_pairs={{0,1},{1,0},{2,3},{3,2},{4,5},{5,4},{6,7},{7,6},{8,9},{9,8},{10,11... | collective-permute-start | bytes 1179656 | tf_op jit(solution)/shard_map/ppermute | solution.py:35
  17.9 6.6 %collective-permute-start.22 = (bf16[128,2048]{1,0:T(8,128)(2,1)S(1)}, bf16[128,2048]{1,0:T(8,128)(2,1)S(1)}, u32[]{:S(2)}, u32[]{:S(2)}) collective-permute-start(bf16[128,2048]{1,0:T(8,128)(2,1)S(1)} %collective-permute-done.15), channel_id=1, source_target_pairs={{8,16},{16,24},{9,17},{17,25},{10,18},{18,26},{11,19},{19,27},{12,... | collective-permute-start | bytes 1572872 | tf_op jit(solution)/shard_map/ppermute | solution.py:157
  22.0 14.6 %collective-permute-start.21 = (bf16[128,2048]{1,0:T(8,128)(2,1)S(1)}, bf16[128,2048]{1,0:T(8,128)(2,1)S(1)}, u32[]{:S(2)}, u32[]{:S(2)}) collective-permute-start(bf16[128,2048]{1,0:T(8,128)(2,1)S(1)} %collective-permute-done.14), channel_id=1, source_target_pairs={{8,0},{16,8},{9,1},{17,9},{10,2},{18,10},{11,3},{19,11},{12,4},{20... | collective-permute-start | bytes 1572872 | tf_op jit(solution)/shard_map/ppermute | solution.py:158
  24.5 18.8 %collective-permute-start.29 = (bf16[128,2048]{1,0:T(8,128)(2,1)S(1)}, bf16[128,2048]{1,0:T(8,128)(2,1)S(1)}, u32[]{:S(2)}, u32[]{:S(2)}) collective-permute-start(bf16[128,2048]{1,0:T(8,128)(2,1)S(1)} %collective-permute-done.22), channel_id=1, source_target_pairs={{16,24},{17,25},{18,26},{19,27},{20,28},{21,29},{22,30},{23,31}} | collective-permute-start | bytes 1572872 | tf_op jit(solution)/shard_map/ppermute | solution.py:159
  36.7 13.7 %collective-permute-start.28 = (bf16[128,2048]{1,0:T(8,128)(2,1)S(1)}, bf16[128,2048]{1,0:T(8,128)(2,1)S(1)}, u32[]{:S(2)}, u32[]{:S(2)}) collective-permute-start(bf16[128,2048]{1,0:T(8,128)(2,1)S(1)} %collective-permute-done.21), channel_id=1, source_target_pairs={{8,0},{9,1},{10,2},{11,3},{12,4},{13,5},{14,6},{15,7}} | collective-permute-start | bytes 1572872 | tf_op jit(solution)/shard_map/ppermute | solution.py:160
  40.3 14.2 %collective-permute-start.10 = (bf16[96,2048]{1,0:T(8,128)(2,1)}, bf16[96,2048]{1,0:T(8,128)(2,1)S(1)}, u32[]{:S(2)}, u32[]{:S(2)}) collective-permute-start(bf16[96,2048]{1,0:T(8,128)(2,1)} %bitcast.72), channel_id=1, source_target_pairs={{0,4},{1,5},{2,6},{3,7},{4,0},{5,1},{6,2},{7,3},{8,12},{9,13},{10,... | collective-permute-start | bytes 1179656 | tf_op jit(solution)/shard_map/ppermute | solution.py:35
  41.9 12.9 %collective-permute-start.8 = (bf16[96,2048]{1,0:T(8,128)(2,1)}, bf16[96,2048]{1,0:T(8,128)(2,1)S(1)}, u32[]{:S(2)}, u32[]{:S(2)}) collective-permute-start(bf16[96,2048]{1,0:T(8,128)(2,1)} %bitcast.73), channel_id=1, source_target_pairs={{0,2},{1,3},{2,0},{3,1},{4,6},{5,7},{6,4},{7,5},{8,10},{9,11},{10,... | collective-permute-start | bytes 1179656 | tf_op jit(solution)/shard_map/ppermute | solution.py:35
  43.3 12.9 %collective-permute-start.7 = (bf16[96,2048]{1,0:T(8,128)(2,1)}, bf16[96,2048]{1,0:T(8,128)(2,1)S(1)}, u32[]{:S(2)}, u32[]{:S(2)}) collective-permute-start(bf16[96,2048]{1,0:T(8,128)(2,1)} %bitcast.74), channel_id=1, source_target_pairs={{0,1},{1,0},{2,3},{3,2},{4,5},{5,4},{6,7},{7,6},{8,9},{9,8},{10,11... | collective-permute-start | bytes 1179656 | tf_op jit(solution)/shard_map/ppermute | solution.py:35
  51.2 5.1 %collective-permute-start.4 = (bf16[96,2048]{1,0:T(8,128)(2,1)S(1)}, bf16[96,2048]{1,0:T(8,128)(2,1)S(1)}, u32[]{:S(2)}, u32[]{:S(2)}) collective-permute-start(bf16[96,2048]{1,0:T(8,128)(2,1)S(1)} %collective-permute-done.3.refs_10_), channel_id=1, source_target_pairs={{0,1},{1,0},{2,3},{3,2},{4,5},{5,4},{6,7},{7,6},{8,9},{9,8},{10,11... | collective-permute-start | bytes 1179656 | tf_op jit(solution)/shard_map/ppermute | solution.py:35
  52.9 11.8 %collective-permute-start.5 = (bf16[96,2048]{1,0:T(8,128)(2,1)}, bf16[96,2048]{1,0:T(8,128)(2,1)S(1)}, u32[]{:S(2)}, u32[]{:S(2)}) collective-permute-start(bf16[96,2048]{1,0:T(8,128)(2,1)} %collective-permute-done.1.refs_8_), channel_id=1, source_target_pairs={{0,4},{1,5},{2,6},{3,7},{4,0},{5,1},{6,2},{7,3},{8,12},{9,13},{10,... | collective-permute-start | bytes 1179656 | tf_op jit(solution)/shard_map/ppermute | solution.py:35
  54.5 11.5 %collective-permute-start.2 = (bf16[96,2048]{1,0:T(8,128)(2,1)}, bf16[96,2048]{1,0:T(8,128)(2,1)S(1)}, u32[]{:S(2)}, u32[]{:S(2)}) collective-permute-start(bf16[96,2048]{1,0:T(8,128)(2,1)} %collective-permute-done.1.refs_8_), channel_id=1, source_target_pairs={{0,1},{1,0},{2,3},{3,2},{4,5},{5,4},{6,7},{7,6},{8,9},{9,8},{10,11... | collective-permute-start | bytes 1179656 | tf_op jit(solution)/shard_map/ppermute | solution.py:35
  54.7 11.3 %collective-permute-start.12 = (bf16[96,2048]{1,0:T(8,128)(2,1)S(1)}, bf16[96,2048]{1,0:T(8,128)(2,1)S(1)}, u32[]{:S(2)}, u32[]{:S(2)}) collective-permute-start(bf16[96,2048]{1,0:T(8,128)(2,1)S(1)} %collective-permute-done.10.refs_18_), channel_id=1, source_target_pairs={{0,2},{1,3},{2,0},{3,1},{4,6},{5,7},{6,4},{7,5},{8,10},{9,11},{10,... | collective-permute-start | bytes 1179656 | tf_op jit(solution)/shard_map/ppermute | solution.py:35
  56.2 10.5 %collective-permute-start.11 = (bf16[96,2048]{1,0:T(8,128)(2,1)S(1)}, bf16[96,2048]{1,0:T(8,128)(2,1)S(1)}, u32[]{:S(2)}, u32[]{:S(2)}) collective-permute-start(bf16[96,2048]{1,0:T(8,128)(2,1)S(1)} %collective-permute-done.10.refs_18_), channel_id=1, source_target_pairs={{0,1},{1,0},{2,3},{3,2},{4,5},{5,4},{6,7},{7,6},{8,9},{9,8},{10,11... | collective-permute-start | bytes 1179656 | tf_op jit(solution)/shard_map/ppermute | solution.py:35
  56.3 12.0 %collective-permute-start.9 = (bf16[96,2048]{1,0:T(8,128)(2,1)S(1)}, bf16[96,2048]{1,0:T(8,128)(2,1)S(1)}, u32[]{:S(2)}, u32[]{:S(2)}) collective-permute-start(bf16[96,2048]{1,0:T(8,128)(2,1)S(1)} %collective-permute-done.8.refs_16_), channel_id=1, source_target_pairs={{0,1},{1,0},{2,3},{3,2},{4,5},{5,4},{6,7},{7,6},{8,9},{9,8},{10,11... | collective-permute-start | bytes 1179656 | tf_op jit(solution)/shard_map/ppermute | solution.py:35
  66.1 9.2 %collective-permute-start.32 = (bf16[128,1024]{1,0:T(8,128)(2,1)S(1)}, bf16[128,1024]{1,0:T(8,128)(2,1)S(1)}, u32[]{:S(2)}, u32[]{:S(2)}) collective-permute-start(bf16[128,1024]{1,0:T(8,128)(2,1)S(1)} %get-tuple-element.24), channel_id=1, source_target_pairs={{0,4},{1,5},{2,6},{3,7},{4,0},{5,1},{6,2},{7,3},{8,12},{9,13},{10,... | collective-permute-start | bytes 786440 | tf_op jit(solution)/shard_map/ppermute | solution.py:35
  66.8 10.0 %collective-permute-start.31 = (bf16[128,1024]{1,0:T(8,128)(2,1)S(1)}, bf16[128,1024]{1,0:T(8,128)(2,1)S(1)}, u32[]{:S(2)}, u32[]{:S(2)}) collective-permute-start(bf16[128,1024]{1,0:T(8,128)(2,1)S(1)} %get-tuple-element.25), channel_id=1, source_target_pairs={{0,2},{1,3},{2,0},{3,1},{4,6},{5,7},{6,4},{7,5},{8,10},{9,11},{10,... | collective-permute-start | bytes 786440 | tf_op jit(solution)/shard_map/ppermute | solution.py:35
  68.3 12.7 %collective-permute-start.25 = (bf16[128,1024]{1,0:T(8,128)(2,1)S(1)}, bf16[128,1024]{1,0:T(8,128)(2,1)}, u32[]{:S(2)}, u32[]{:S(2)}) collective-permute-start(bf16[128,1024]{1,0:T(8,128)(2,1)S(1)} %get-tuple-element.26), channel_id=1, source_target_pairs={{0,4},{1,5},{2,6},{3,7},{4,0},{5,1},{6,2},{7,3},{8,12},{9,13},{10,... | collective-permute-start | bytes 786440 | tf_op jit(solution)/shard_map/ppermute | solution.py:35
  69.8 11.9 %collective-permute-start.24 = (bf16[128,1024]{1,0:T(8,128)(2,1)S(1)}, bf16[128,1024]{1,0:T(8,128)(2,1)}, u32[]{:S(2)}, u32[]{:S(2)}) collective-permute-start(bf16[128,1024]{1,0:T(8,128)(2,1)S(1)} %get-tuple-element.27), channel_id=1, source_target_pairs={{0,2},{1,3},{2,0},{3,1},{4,6},{5,7},{6,4},{7,5},{8,10},{9,11},{10,... | collective-permute-start | bytes 786440 | tf_op jit(solution)/shard_map/ppermute | solution.py:35
  70.4 15.6 %collective-permute-start.18 = (bf16[128,1024]{1,0:T(8,128)(2,1)S(1)}, bf16[128,1024]{1,0:T(8,128)(2,1)S(1)}, u32[]{:S(2)}, u32[]{:S(2)}) collective-permute-start(bf16[128,1024]{1,0:T(8,128)(2,1)S(1)} %get-tuple-element.28), channel_id=1, source_target_pairs={{0,4},{1,5},{2,6},{3,7},{4,0},{5,1},{6,2},{7,3},{8,12},{9,13},{10,... | collective-permute-start | bytes 786440 | tf_op jit(solution)/shard_map/ppermute | solution.py:35
  75.2 11.0 %collective-permute-start.17 = (bf16[128,1024]{1,0:T(8,128)(2,1)S(1)}, bf16[128,1024]{1,0:T(8,128)(2,1)S(1)}, u32[]{:S(2)}, u32[]{:S(2)}) collective-permute-start(bf16[128,1024]{1,0:T(8,128)(2,1)S(1)} %get-tuple-element.29), channel_id=1, source_target_pairs={{0,2},{1,3},{2,0},{3,1},{4,6},{5,7},{6,4},{7,5},{8,10},{9,11},{10,... | collective-permute-start | bytes 786440 | tf_op jit(solution)/shard_map/ppermute | solution.py:35
  76.7 9.9 %collective-permute-start.34 = (bf16[128,1024]{1,0:T(8,128)(2,1)S(1)}, bf16[128,1024]{1,0:T(8,128)(2,1)S(1)}, u32[]{:S(2)}, u32[]{:S(2)}) collective-permute-start(bf16[128,1024]{1,0:T(8,128)(2,1)S(1)} %collective-permute-done.32.refs_20_), channel_id=1, source_target_pairs={{0,1},{1,0},{2,3},{3,2},{4,5},{5,4},{6,7},{7,6},{8,9},{9,8},{10,11... | collective-permute-start | bytes 786440 | tf_op jit(solution)/shard_map/ppermute | solution.py:35
  81.0 5.9 %collective-permute-start.33 = (bf16[128,1024]{1,0:T(8,128)(2,1)S(1)}, bf16[128,1024]{1,0:T(8,128)(2,1)S(1)}, u32[]{:S(2)}, u32[]{:S(2)}) collective-permute-start(bf16[128,1024]{1,0:T(8,128)(2,1)S(1)} %collective-permute-done.31.refs_19_), channel_id=1, source_target_pairs={{0,1},{1,0},{2,3},{3,2},{4,5},{5,4},{6,7},{7,6},{8,9},{9,8},{10,11... | collective-permute-start | bytes 786440 | tf_op jit(solution)/shard_map/ppermute | solution.py:35
  81.7 24.2 %collective-permute-start.30 = (bf16[128,2048]{1,0:T(8,128)(2,1)S(1)}, bf16[128,2048]{1,0:T(8,128)(2,1)S(1)}, u32[]{:S(2)}, u32[]{:S(2)}) collective-permute-start(bf16[128,2048]{1,0:T(8,128)(2,1)S(1)} %get-tuple-element.19.refs_17_), channel_id=1, source_target_pairs={{0,1},{1,0},{2,3},{3,2},{4,5},{5,4},{6,7},{7,6},{8,9},{9,8},{10,11... | collective-permute-start | bytes 1572872 | tf_op jit(solution)/shard_map/ppermute | solution.py:35
  86.0 19.8 %collective-permute-start.23 = (bf16[128,2048]{1,0:T(8,128)(2,1)S(1)}, bf16[128,2048]{1,0:T(8,128)(2,1)S(1)}, u32[]{:S(2)}, u32[]{:S(2)}) collective-permute-start(bf16[128,2048]{1,0:T(8,128)(2,1)S(1)} %get-tuple-element.20.refs_11_), channel_id=1, source_target_pairs={{0,1},{1,0},{2,3},{3,2},{4,5},{5,4},{6,7},{7,6},{8,9},{9,8},{10,11... | collective-permute-start | bytes 1572872 | tf_op jit(solution)/shard_map/ppermute | solution.py:35
  86.2 19.6 %collective-permute-start.16 = (bf16[128,2048]{1,0:T(8,128)(2,1)S(1)}, bf16[128,2048]{1,0:T(8,128)(2,1)S(1)}, u32[]{:S(2)}, u32[]{:S(2)}) collective-permute-start(bf16[128,2048]{1,0:T(8,128)(2,1)S(1)} %get-tuple-element.21.refs_5_), channel_id=1, source_target_pairs={{0,1},{1,0},{2,3},{3,2},{4,5},{5,4},{6,7},{7,6},{8,9},{9,8},{10,11... | collective-permute-start | bytes 1572872 | tf_op jit(solution)/shard_map/ppermute | solution.py:35
  86.6 7.8 %collective-permute-start.27 = (bf16[128,1024]{1,0:T(8,128)(2,1)}, bf16[128,1024]{1,0:T(8,128)(2,1)}, u32[]{:S(2)}, u32[]{:S(2)}) collective-permute-start(bf16[128,1024]{1,0:T(8,128)(2,1)} %collective-permute-done.25.refs_14_), channel_id=1, source_target_pairs={{0,1},{1,0},{2,3},{3,2},{4,5},{5,4},{6,7},{7,6},{8,9},{9,8},{10,11... | collective-permute-start | bytes 786440 | tf_op jit(solution)/shard_map/ppermute | solution.py:35
  86.9 8.0 %collective-permute-start.26 = (bf16[128,1024]{1,0:T(8,128)(2,1)}, bf16[128,1024]{1,0:T(8,128)(2,1)}, u32[]{:S(2)}, u32[]{:S(2)}) collective-permute-start(bf16[128,1024]{1,0:T(8,128)(2,1)} %collective-permute-done.24.refs_13_), channel_id=1, source_target_pairs={{0,1},{1,0},{2,3},{3,2},{4,5},{5,4},{6,7},{7,6},{8,9},{9,8},{10,11... | collective-permute-start | bytes 786440 | tf_op jit(solution)/shard_map/ppermute | solution.py:35
  94.5 11.3 %collective-permute-start.20 = (bf16[128,1024]{1,0:T(8,128)(2,1)S(1)}, bf16[128,1024]{1,0:T(8,128)(2,1)S(1)}, u32[]{:S(2)}, u32[]{:S(2)}) collective-permute-start(bf16[128,1024]{1,0:T(8,128)(2,1)S(1)} %collective-permute-done.18.refs_8_), channel_id=1, source_target_pairs={{0,1},{1,0},{2,3},{3,2},{4,5},{5,4},{6,7},{7,6},{8,9},{9,8},{10,11... | collective-permute-start | bytes 786440 | tf_op jit(solution)/shard_map/ppermute | solution.py:35
  94.9 10.9 %collective-permute-start.19 = (bf16[128,1024]{1,0:T(8,128)(2,1)}, bf16[128,1024]{1,0:T(8,128)(2,1)S(1)}, u32[]{:S(2)}, u32[]{:S(2)}) collective-permute-start(bf16[128,1024]{1,0:T(8,128)(2,1)} %copy-done.26), channel_id=1, source_target_pairs={{0,1},{1,0},{2,3},{3,2},{4,5},{5,4},{6,7},{7,6},{8,9},{9,8},{10,11... | collective-permute-start | bytes 786440 | tf_op jit(solution)/shard_map/ppermute | solution.py:35
  113.4 9.4 %collective-permute-start.41 = (bf16[64,2048]{1,0:T(8,128)(2,1)}, bf16[64,2048]{1,0:T(8,128)(2,1)S(1)}, u32[]{:S(2)}, u32[]{:S(2)}) collective-permute-start(bf16[64,2048]{1,0:T(8,128)(2,1)} %get-tuple-element.11.refs_5_), channel_id=1, source_target_pairs={{0,4},{1,5},{2,6},{3,7},{4,0},{5,1},{6,2},{7,3},{8,12},{9,13},{10,... | collective-permute-start | bytes 786440 | tf_op jit(solution)/shard_map/ppermute | solution.py:35
  114.9 9.4 %collective-permute-start.37 = (bf16[64,2048]{1,0:T(8,128)(2,1)}, bf16[64,2048]{1,0:T(8,128)(2,1)S(1)}, u32[]{:S(2)}, u32[]{:S(2)}) collective-permute-start(bf16[64,2048]{1,0:T(8,128)(2,1)} %get-tuple-element.11.refs_5_), channel_id=1, source_target_pairs={{0,2},{1,3},{2,0},{3,1},{4,6},{5,7},{6,4},{7,5},{8,10},{9,11},{10,... | collective-permute-start | bytes 786440 | tf_op jit(solution)/shard_map/ppermute | solution.py:35
  116.4 7.9 %collective-permute-start.35 = (bf16[64,2048]{1,0:T(8,128)(2,1)}, bf16[64,2048]{1,0:T(8,128)(2,1)S(1)}, u32[]{:S(2)}, u32[]{:S(2)}) collective-permute-start(bf16[64,2048]{1,0:T(8,128)(2,1)} %get-tuple-element.11.refs_5_), channel_id=1, source_target_pairs={{0,1},{1,0},{2,3},{3,2},{4,5},{5,4},{6,7},{7,6},{8,9},{9,8},{10,11... | collective-permute-start | bytes 786440 | tf_op jit(solution)/shard_map/ppermute | solution.py:35
  116.4 11.7 %collective-permute-start.42 = (bf16[64,2048]{1,0:T(8,128)(2,1)}, bf16[64,2048]{1,0:T(8,128)(2,1)S(1)}, u32[]{:S(2)}, u32[]{:S(2)}) collective-permute-start(bf16[64,2048]{1,0:T(8,128)(2,1)} %get-tuple-element.12.refs_6_), channel_id=1, source_target_pairs={{0,4},{1,5},{2,6},{3,7},{4,0},{5,1},{6,2},{7,3},{8,12},{9,13},{10,... | collective-permute-start | bytes 786440 | tf_op jit(solution)/shard_map/ppermute | solution.py:35
  116.9 23.7 %collective-permute-start.38 = (bf16[64,2048]{1,0:T(8,128)(2,1)}, bf16[64,2048]{1,0:T(8,128)(2,1)S(1)}, u32[]{:S(2)}, u32[]{:S(2)}) collective-permute-start(bf16[64,2048]{1,0:T(8,128)(2,1)} %get-tuple-element.12.refs_6_), channel_id=1, source_target_pairs={{0,2},{1,3},{2,0},{3,1},{4,6},{5,7},{6,4},{7,5},{8,10},{9,11},{10,... | collective-permute-start | bytes 786440 | tf_op jit(solution)/shard_map/ppermute | solution.py:35
  122.7 18.3 %collective-permute-start.36 = (bf16[64,2048]{1,0:T(8,128)(2,1)}, bf16[64,2048]{1,0:T(8,128)(2,1)S(1)}, u32[]{:S(2)}, u32[]{:S(2)}) collective-permute-start(bf16[64,2048]{1,0:T(8,128)(2,1)} %get-tuple-element.12.refs_6_), channel_id=1, source_target_pairs={{0,1},{1,0},{2,3},{3,2},{4,5},{5,4},{6,7},{7,6},{8,9},{9,8},{10,11... | collective-permute-start | bytes 786440 | tf_op jit(solution)/shard_map/ppermute | solution.py:35
  124.3 16.9 %collective-permute-start.43 = (bf16[64,2048]{1,0:T(8,128)(2,1)S(1)}, bf16[64,2048]{1,0:T(8,128)(2,1)S(1)}, u32[]{:S(2)}, u32[]{:S(2)}) collective-permute-start(bf16[64,2048]{1,0:T(8,128)(2,1)S(1)} %collective-permute-done.41.refs_13_), channel_id=1, source_target_pairs={{0,1},{1,0},{2,3},{3,2},{4,5},{5,4},{6,7},{7,6},{8,9},{9,8},{10,11... | collective-permute-start | bytes 786440 | tf_op jit(solution)/shard_map/ppermute | solution.py:35
  124.3 17.2 %collective-permute-start.45 = (bf16[64,2048]{1,0:T(8,128)(2,1)S(1)}, bf16[64,2048]{1,0:T(8,128)(2,1)S(1)}, u32[]{:S(2)}, u32[]{:S(2)}) collective-permute-start(bf16[64,2048]{1,0:T(8,128)(2,1)S(1)} %collective-permute-done.37.refs_9_), channel_id=1, source_target_pairs={{0,4},{1,5},{2,6},{3,7},{4,0},{5,1},{6,2},{7,3},{8,12},{9,13},{10,... | collective-permute-start | bytes 786440 | tf_op jit(solution)/shard_map/ppermute | solution.py:35
  128.1 13.7 %collective-permute-start.46 = (bf16[64,2048]{1,0:T(8,128)(2,1)S(1)}, bf16[64,2048]{1,0:T(8,128)(2,1)S(1)}, u32[]{:S(2)}, u32[]{:S(2)}) collective-permute-start(bf16[64,2048]{1,0:T(8,128)(2,1)S(1)} %collective-permute-done.42.refs_14_), channel_id=1, source_target_pairs={{0,2},{1,3},{2,0},{3,1},{4,6},{5,7},{6,4},{7,5},{8,10},{9,11},{10,... | collective-permute-start | bytes 786440 | tf_op jit(solution)/shard_map/ppermute | solution.py:35
  170.6 16.7 %collective-permute-start.50 = (bf16[64,2048]{1,0:T(8,128)(2,1)S(1)}, bf16[64,2048]{1,0:T(8,128)(2,1)S(1)}, u32[]{:S(2)}, u32[]{:S(2)}) collective-permute-start(bf16[64,2048]{1,0:T(8,128)(2,1)S(1)} %slice_bitcast_fusion.6), channel_id=1, source_target_pairs={{0,2},{1,3},{2,0},{3,1},{4,6},{5,7},{6,4},{7,5},{8,10},{9,11},{10,... | collective-permute-start | bytes 786440 | tf_op jit(solution)/shard_map/ppermute | solution.py:35
  171.5 13.4 %collective-permute-start.53 = (bf16[64,2048]{1,0:T(8,128)(2,1)S(1)}, bf16[64,2048]{1,0:T(8,128)(2,1)S(1)}, u32[]{:S(2)}, u32[]{:S(2)}) collective-permute-start(bf16[64,2048]{1,0:T(8,128)(2,1)S(1)} %get-tuple-element.22), channel_id=1, source_target_pairs={{0,2},{1,3},{2,0},{3,1},{4,6},{5,7},{6,4},{7,5},{8,10},{9,11},{10,... | collective-permute-start | bytes 786440 | tf_op jit(solution)/shard_map/ppermute | solution.py:35
  172.7 14.6 %collective-permute-start.55 = (bf16[64,2048]{1,0:T(8,128)(2,1)S(1)}, bf16[64,2048]{1,0:T(8,128)(2,1)S(1)}, u32[]{:S(2)}, u32[]{:S(2)}) collective-permute-start(bf16[64,2048]{1,0:T(8,128)(2,1)S(1)} %slice_bitcast_fusion.1), channel_id=1, source_target_pairs={{0,4},{1,5},{2,6},{3,7},{4,0},{5,1},{6,2},{7,3},{8,12},{9,13},{10,... | collective-permute-start | bytes 786440 | tf_op jit(solution)/shard_map/ppermute | solution.py:35
  173.6 12.8 %collective-permute-start.51 = (bf16[64,2048]{1,0:T(8,128)(2,1)S(1)}, bf16[64,2048]{1,0:T(8,128)(2,1)S(1)}, u32[]{:S(2)}, u32[]{:S(2)}) collective-permute-start(bf16[64,2048]{1,0:T(8,128)(2,1)S(1)} %get-tuple-element.23), channel_id=1, source_target_pairs={{0,4},{1,5},{2,6},{3,7},{4,0},{5,1},{6,2},{7,3},{8,12},{9,13},{10,... | collective-permute-start | bytes 786440 | tf_op jit(solution)/shard_map/ppermute | solution.py:35
  184.9 7.8 %collective-permute-start.54 = (bf16[64,2048]{1,0:T(8,128)(2,1)S(1)}, bf16[64,2048]{1,0:T(8,128)(2,1)S(1)}, u32[]{:S(2)}, u32[]{:S(2)}) collective-permute-start(bf16[64,2048]{1,0:T(8,128)(2,1)S(1)} %fusion.4), channel_id=1, source_target_pairs={{0,4},{1,5},{2,6},{3,7},{4,0},{5,1},{6,2},{7,3},{8,12},{9,13},{10,... | collective-permute-start | bytes 786440 | tf_op jit(solution)/shard_map/ppermute | solution.py:35
  186.5 7.2 %collective-permute-start.52 = (bf16[64,2048]{1,0:T(8,128)(2,1)S(1)}, bf16[64,2048]{1,0:T(8,128)(2,1)S(1)}, u32[]{:S(2)}, u32[]{:S(2)}) collective-permute-start(bf16[64,2048]{1,0:T(8,128)(2,1)S(1)} %fusion.5), channel_id=1, source_target_pairs={{0,2},{1,3},{2,0},{3,1},{4,6},{5,7},{6,4},{7,5},{8,10},{9,11},{10,... | collective-permute-start | bytes 786440 | tf_op jit(solution)/shard_map/ppermute | solution.py:35
  (59 other events, 837.7 us)

commit v2 on v0

v2 whole, which is shorter than its diff:
```python
import math

import jax
import jax.numpy as jnp
from jax import lax
from jax.experimental import pallas as pl
from jax.experimental.pallas import tpu as pltpu
from jax.sharding import PartitionSpec as P

HEADS = 16
HEAD_DIM = 128
CAP = 40

NEG_FILL = -1e30
EPSILON = 1e-05
VMEM_LIMIT = 56 * 1024 * 1024

F32 = jnp.float32
BF16 = jnp.bfloat16


def flip(value, bits, size):
    return lax.ppermute(value, "ep", [(i, i ^ bits) for i in range(size)])


def in_hbm(value):
    return pltpu.with_memory_space_constraint(value, pltpu.HBM)


def in_vmem(value):
    return pltpu.with_memory_space_constraint(value, pltpu.VMEM)


def after(value, *done):
    return lax.optimization_barrier((value, done))[0]


def everywhere(shape, dtype):
    return jax.ShapeDtypeStruct(shape, dtype)


IN_VMEM = pl.BlockSpec(memory_space=pltpu.VMEM)
IN_SMEM = pl.BlockSpec(memory_space=pltpu.SMEM)
IN_PLACE = pl.BlockSpec(memory_space=pl.ANY)


def pack_body(core, *refs):
    sources, (ids, gates), (send, send_prompts, mine, prompts), held, sems = refs[:5], refs[5:7], refs[7:11], refs[11:16], refs[16]
    copies = [pltpu.make_async_copy(sources[i], held[i], sems.at[i]) for i in range(5)]
    for copy in copies:
        copy.start()
    for copy in copies:
        copy.wait()
    queries, keys, values, prompt_keys, prompt_values = held
    rows, features = queries.shape
    shards = features // (4 * HEAD_DIM)
    width = 2 * HEAD_DIM
    for shard in range(shards):
        lanes = slice(shard * width, (shard + 1) * width)
        for target, which in ((0, core[0]), (1, 1 - core[0])):
            start = pl.multiple_of(shard * 2 * width + which * width, width)
            low = 0
            for part in (queries, keys, values, prompt_keys, prompt_values):
                high = low + part.shape[0]
                taken = part[:, pl.ds(start, width)]
                if high <= 3 * rows:
                    (mine, send)[target][low:high, lanes] = taken
                else:
                    (prompts, send_prompts)[target][low - 3 * rows : high - 3 * rows, lanes] = taken
                low = high
    top = ids.shape[0]
    high_part = gates[...].astype(BF16)
    low_part = (gates[...] - high_part.astype(F32)).astype(BF16)
    blank = jnp.zeros((top, rows), F32)
    first = jnp.concatenate([ids[...], high_part.astype(F32)], axis=0).astype(BF16)
    second = jnp.concatenate([blank, low_part.astype(F32)], axis=0).astype(BF16)
    base = 2 * prompt_keys.shape[0]
    for target in (send_prompts, prompts):
        target[base : base + 2 * top, :] = jnp.zeros((2 * top, target.shape[1]), BF16)
        target[base : base + 2 * top, :rows] = first
        target[base : base + 2 * top, rows : 2 * rows] = second


def pack(core, queries, keys, values, prompt_keys, prompt_values, ids, gates):
    rows, features = queries.shape
    tail = 2 * prompt_keys.shape[0] + 2 * ids.shape[0]
    return pl.pallas_call(
        pack_body,
        out_shape=(
            everywhere((3 * rows, features // 2), BF16),
            everywhere((tail, features // 2), BF16),
            everywhere((3 * rows, features // 2), BF16),
            everywhere((tail, features // 2), BF16),
        ),
        in_specs=[IN_SMEM] + [IN_PLACE] * 5 + [IN_VMEM] * 2,
        out_specs=(IN_VMEM,) * 4,
        scratch_shapes=[pltpu.VMEM(part.shape, BF16) for part in (queries, keys, values, prompt_keys, prompt_values)]
        + [pltpu.SemaphoreType.DMA((5,))],
        compiler_params=pltpu.CompilerParams(vmem_limit_bytes=12 * 2**20),
        name="pack",
    )(core, *[in_hbm(part) for part in (queries, keys, values, prompt_keys, prompt_values)], ids, gates)


def attend(queries, all_keys, all_values, bias):
    scores = lax.dot_general(queries, all_keys, (((1,), (1,)), ((), ())), preferred_element_type=F32)
    scores = scores * (1.0 / math.sqrt(HEAD_DIM)) + bias
    weights = jnp.exp(scores - jnp.max(scores, axis=-1, keepdims=True))
    total = jnp.sum(weights, axis=-1, keepdims=True)
    mixed = jnp.dot(weights.astype(BF16), all_values, preferred_element_type=F32)
    return (mixed / total).astype(BF16)


def fill_bias(bias, prompt_rows, tree_len, parents, prompts, lengths, prompt_of, position):
    tokens = bias.shape[0]
    for request in range(tokens // tree_len):
        prompt = prompts[request]
        seen = (prompt_of == prompt) & (position < lengths[prompt])
        row = jnp.where(seen, 0.0, NEG_FILL)
        bias[request * tree_len : (request + 1) * tree_len, :prompt_rows] = jnp.broadcast_to(
            row, (tree_len, prompt_rows)
        )
    node = lax.broadcasted_iota(jnp.int32, (tokens, tokens), 0)
    other = lax.broadcasted_iota(jnp.int32, (tokens, tokens), 1)
    reach = jnp.where((other == parents) | (other == node), 1.0, 0.0)
    for _ in range((tree_len - 1).bit_length()):
        reach = reach.astype(BF16)
        reach = jnp.minimum(jnp.dot(reach, reach, preferred_element_type=F32), 1.0)
    bias[:, prompt_rows:] = jnp.where(reach > 0.5, 0.0, NEG_FILL)


def accepted_body(accepted, tree_keys, tree_values, cache):
    rows, features = tree_keys.shape
    chosen = accepted[...] == lax.broadcasted_iota(jnp.int32, (accepted.shape[0], rows), 1)
    chosen = jnp.where(chosen, 1.0, 0.0).astype(BF16)
    cache[:, :features] = jnp.dot(chosen, tree_keys[...], preferred_element_type=F32).astype(BF16)
    cache[:, features:] = jnp.dot(chosen, tree_values[...], preferred_element_type=F32).astype(BF16)


def chip_attention_body(
    me, my_prompts, sibling, lengths, columns, parents, accepted, *refs
):
    copies = [pltpu.make_async_copy(refs[i], refs[17 + i], refs[29].at[i]) for i in range(12)]
    for copy in copies:
        copy.start()
    (attended, cache, ids, gates, bias), (tree_keys, tree_values, mine, got, *holders) = refs[12:17], refs[17:29]
    rows = tree_keys.shape[0]
    requests = my_prompts.shape[0]
    tree_len = rows // requests
    block = (holders[0].shape[0] - 16) // 2
    prompts = [my_prompts[i] for i in range(requests)] + [sibling[requests + i, 0] for i in range(requests)]
    position = (columns[0:1, :] ^ me[0]) * (block // lengths.shape[0]) + columns[2:3, :]
    fill_bias(bias, columns.shape[1], tree_len, parents[...], prompts, lengths, columns[1:2, :], position)
    for copy in copies:
        copy.wait()
    for head in range(mine.shape[1] // HEAD_DIM):
        lanes = slice(head * HEAD_DIM, (head + 1) * HEAD_DIM)
        queries = jnp.concatenate([mine[:rows, lanes], got[:rows, lanes]], axis=0)
        all_keys = jnp.concatenate(
            [ref[:block, lanes] for ref in holders]
            + [mine[rows : 2 * rows, lanes], got[rows : 2 * rows, lanes]],
            axis=0,
        )
        all_values = jnp.concatenate(
            [ref[block : 2 * block, lanes] for ref in holders]
            + [mine[2 * rows :, lanes], got[2 * rows : 3 * rows, lanes]],
            axis=0,
        )
        attended[head] = attend(queries, all_keys, all_values, bias[...])
    accepted_body(accepted, tree_keys, tree_values, cache)
    for index, ref in enumerate(holders):
        first = ref[2 * block :, :rows].astype(F32)
        second = ref[2 * block :, rows : 2 * rows].astype(F32)
        lanes = slice(index % 2 * rows, (index % 2 + 1) * rows)
        ids[index // 2, :, lanes] = first[:8]
        gates[index // 2, :, lanes] = first[8:] + second[8:]


def chip_attention(scalars, columns, parents, accepted, tree_keys, tree_values, blocks):
    rows, features = tree_keys.shape
    width = columns.shape[1] + 2 * rows
    heads = features // HEAD_DIM // 2
    copied = [in_hbm(part) for part in (tree_keys, tree_values, *blocks)]
    return pl.pallas_call(
        chip_attention_body,
        out_shape=(
            everywhere((heads, 2 * rows, HEAD_DIM), BF16),
            everywhere((accepted.shape[0], 2 * features), BF16),
            everywhere((4, 8, 2 * rows), F32),
            everywhere((4, 8, 2 * rows), F32),
        ),
        in_specs=[IN_SMEM] * 4 + [IN_VMEM] * 3 + [IN_PLACE] * len(copied),
        out_specs=(IN_VMEM,) * 4,
        scratch_shapes=[pltpu.VMEM((2 * rows, width), F32)]
        + [pltpu.VMEM(part.shape, BF16) for part in copied]
        + [pltpu.SemaphoreType.DMA((len(copied),))],
        compiler_params=pltpu.CompilerParams(vmem_limit_bytes=14 * 2**20),
        name="attention",
    )(*scalars, columns, parents, accepted, *copied)


def plain_attention_body(
    prompts, lengths, columns, parents, accepted, queries, tree_keys, tree_values, keys, values, attended, cache, bias
):
    rows, features = queries.shape
    tree_len = rows // prompts.shape[0]
    requests = [prompts[i] for i in range(prompts.shape[0])]
    fill_bias(bias, columns.shape[1], tree_len, parents[...], requests, lengths, columns[0:1, :], columns[1:2, :])
    for head in range(features // HEAD_DIM):
        lanes = slice(head * HEAD_DIM, (head + 1) * HEAD_DIM)
        all_keys = jnp.concatenate([keys[:, lanes], tree_keys[:, lanes]], axis=0)
        all_values = jnp.concatenate([values[:, lanes], tree_values[:, lanes]], axis=0)
        attended[:, lanes] = attend(queries[:, lanes], all_keys, all_values, bias[...])
    accepted_body(accepted, tree_keys, tree_values, cache)


def plain_attention(prompts, lengths, columns, parents, accepted, queries, tree_keys, tree_values, keys, values):
    rows, features = queries.shape
    return pl.pallas_call(
        plain_attention_body,
        out_shape=(everywhere((rows, features), BF16), everywhere((accepted.shape[0], 2 * features), BF16)),
        in_specs=[IN_SMEM] * 2 + [IN_VMEM] * 8,
        out_specs=(IN_VMEM,) * 2,
        scratch_shapes=[pltpu.VMEM((rows, columns.shape[1] + rows), F32)],
        compiler_params=pltpu.CompilerParams(vmem_limit_bytes=VMEM_LIMIT),
        name="attention",
    )(prompts, lengths, columns, parents, accepted, queries, tree_keys, tree_values, keys, values)


def fetch_projection(out_proj, packed, before_shared):
    me, place = lax.axis_index("rep"), lax.axis_index("ep")
    core, parity = place % 2, (place // 2 + place // 4) % 2
    block = lax.dynamic_slice_in_dim(out_proj, (2 * core + parity) * HEAD_DIM, HEAD_DIM, 0)
    own = lax.dynamic_slice_in_dim(out_proj, core * 2 * HEAD_DIM, 2 * HEAD_DIM, 0)
    block = after(block, packed)

    def shifted(value, by):
        return lax.ppermute(value, "rep", [(i, (i + by) % 4) for i in range(4)])

    came1, came3 = shifted(block, 1), shifted(block, 3)
    up = lax.ppermute(came1, "rep", [(1, 2), (2, 3)])
    down = lax.ppermute(came3, "rep", [(2, 1), (1, 0)])
    order = [2 * me, 2 * me + 1]
    for by in (1, 3, 2):
        shard = (me + 4 - by) % 4
        order += [2 * shard + parity, 2 * shard + 1 - parity]
    half = HEAD_DIM // 2
    came1, came3 = after((came1, came3), before_shared)
    first = jnp.concatenate([came1[:half], came3[:half]], axis=0)
    second = jnp.concatenate([came1[half:], came3[half:]], axis=0)
    from_x, from_y = flip(first, 2, 8), flip(second, 4, 8)
    weights = [own, first, second, from_x, from_y]
    pieces = [(0, 0, 2 * HEAD_DIM)]
    for low in (0, half):
        pieces += [(index, low, low + half) for index in (1, 2, 3, 4)]
    pieces += [(5, 0, HEAD_DIM), (6, 0, half), (7, 0, half)]
    up, down = after((up, down), from_x, from_y)
    came2 = jnp.where(me >= 2, up, down)
    return weights, pieces, jnp.stack(order).astype(jnp.int32), came2


def chip_project_body(pieces, order, attended, *refs):
    weights, (mine, other, ordered) = refs[: len(refs) - 3], refs[len(refs) - 3 :]
    rows, features = mine.shape
    for index in range(attended.shape[0]):
        ordered[:, index * HEAD_DIM : (index + 1) * HEAD_DIM] = attended[order[index]]
    step = 256
    for column in range(0, features, step):
        joined = jnp.concatenate(
            [weights[ref][low:high, column : column + step] for ref, low, high in pieces], axis=0
        )
        total = jnp.dot(ordered[...], joined, preferred_element_type=F32)
        mine[:, column : column + step] = total[:rows]
        other[:, column : column + step] = total[rows:].astype(BF16)


def chip_project(order, attended, weights, pieces):
    heads, rows, _ = attended.shape
    features = weights[0].shape[1]
    return pl.pallas_call(
        lambda *refs: chip_project_body(pieces, *refs),
        out_shape=(everywhere((rows // 2, features), F32), everywhere((rows // 2, features), BF16)),
        in_specs=[IN_SMEM] + [IN_VMEM] * (1 + len(weights)),
        out_specs=(IN_VMEM,) * 2,
        scratch_shapes=[pltpu.VMEM((rows, heads * HEAD_DIM), BF16)],
        compiler_params=pltpu.CompilerParams(vmem_limit_bytes=14 * 2**20),
        name="project",
    )(order, attended, *weights)


def norm_body(hidden, mine, other, gain, residual, normed):
    total = hidden[...].astype(F32) + mine[...] + other[...].astype(F32)
    residual[...] = total
    factor = lax.rsqrt(jnp.mean(total * total, axis=-1, keepdims=True) + EPSILON)
    normed[...] = (total * factor * gain[...]).astype(BF16)


def norm(hidden, mine, other, gain):
    return pl.pallas_call(
        norm_body,
        out_shape=(everywhere(hidden.shape, F32), everywhere(hidden.shape, BF16)),
        in_specs=[IN_VMEM] * 4,
        out_specs=(IN_VMEM,) * 2,
        compiler_params=pltpu.CompilerParams(vmem_limit_bytes=8 * 2**20),
        name="norm",
    )(hidden, mine, other, gain)


def experts_body(per_pair, first_expert, ids, gates, gate_up_hbm, down_hbm, *refs):
    pairs, top, tokens = ids.shape
    sources = refs[: pairs * per_pair]
    same_core, other_core, picked, produced, hidden, chosen, slot_gates, gate_up, down, sems = refs[pairs * per_pair :]
    local_experts, features, _ = gate_up.shape
    units = down.shape[1]
    copies = [
        (
            pltpu.make_async_copy(gate_up_hbm.at[expert], gate_up.at[expert], sems.at[0, expert]),
            pltpu.make_async_copy(down_hbm.at[expert], down.at[expert], sems.at[1, expert]),
        )
        for expert in range(local_experts)
    ]
    for first, second in copies[:2]:
        first.start()
        second.start()
    slots = 2 * CAP
    earlier = lax.broadcasted_iota(jnp.int32, (tokens, tokens), 0)
    later = lax.broadcasted_iota(jnp.int32, (tokens, tokens), 1)
    before = jnp.where(earlier < later, 1.0, 0.0).astype(BF16)
    slot_ids = lax.broadcasted_iota(jnp.int32, (slots, tokens), 0).astype(F32)
    for pair in range(pairs):
        hits, shares = [], []
        for expert in range(local_experts):
            match = ids[pair] == (first_expert[0] + expert).astype(F32)
            hits.append(jnp.max(jnp.where(match, 1.0, 0.0), axis=0, keepdims=True))
            shares.append(jnp.sum(jnp.where(match, gates[pair], 0.0), axis=0, keepdims=True))
        stacked = jnp.concatenate(hits + [jnp.zeros((16 - local_experts, tokens), F32)], axis=0)
        places = jnp.dot(stacked.astype(BF16), before, preferred_element_type=F32)
        for expert in range(local_experts):
            place = jnp.where(hits[expert] > 0.5, places[expert : expert + 1], -1.0)
            taken = jnp.where(slot_ids == place, 1.0, 0.0)
            chosen[pair, expert * slots : (expert + 1) * slots, :] = taken.astype(BF16)
            slot_gates[expert, pair * slots : (pair + 1) * slots, :] = jnp.sum(
                taken * shares[expert], axis=1, keepdims=True
            )
        group = sources[pair * per_pair : (pair + 1) * per_pair]
        step = 512
        for column in range(0, features, step):
            rows = jnp.concatenate([ref[:, column : column + step] for ref in group], axis=0)
            found = jnp.dot(chosen[pair], rows, preferred_element_type=F32).astype(BF16)
            for expert in range(local_experts):
                picked[expert, pair * slots : (pair + 1) * slots, column : column + step] = found[
                    expert * slots : (expert + 1) * slots
                ]
    chunk = slots * min(pairs, 4)
    for expert in range(local_experts):
        copies[expert][0].wait()
        for later_copy in copies[expert + 2 : expert + 3]:
            later_copy[0].start()
            later_copy[1].start()
        for low in range(0, pairs * slots, chunk):
            rows = picked[expert, low : low + chunk, :]
            gate_rows = slot_gates[expert, low : low + chunk, :]
            for column in range(0, units, 256):
                gate = jnp.dot(rows, gate_up[expert, :, column : column + 256], preferred_element_type=F32)
                up = jnp.dot(
                    rows, gate_up[expert, :, units + column : units + column + 256], preferred_element_type=F32
                )
                active = gate / (1.0 + jnp.exp(-gate)) * up * gate_rows
                hidden[low : low + chunk, column : column + 256] = active.astype(BF16)
            if low == 0:
                copies[expert][1].wait()
            for column in range(0, features, 512):
                result = jnp.dot(
                    hidden[low : low + chunk, :], down[expert, :, column : column + 512], preferred_element_type=F32
                ).astype(BF16)
                for inner in range(chunk // slots):
                    produced[
                        low // slots + inner, expert * slots : (expert + 1) * slots, column : column + 512
                    ] = result[inner * slots : (inner + 1) * slots]
    for pair in range(pairs):
        for column in range(0, features, 512):
            mixture = lax.dot_general(
                chosen[pair], produced[pair, :, column : column + 512], (((0,), (0,)), ((), ())),
                preferred_element_type=F32,
            ).astype(BF16)
            same_core[pair, :, column : column + 512] = mixture[: tokens // 2]
            other_core[pair, :, column : column + 512] = mixture[tokens // 2 :]


def experts(first_expert, ids, gates, gate_up, down, sources, limit):
    pairs, top, tokens = ids.shape
    local_experts, features, _ = gate_up.shape
    units = down.shape[1]
    slots = 2 * CAP
    return pl.pallas_call(
        lambda *refs: experts_body(len(sources) // pairs, *refs),
        out_shape=(everywhere((pairs, tokens // 2, features), BF16),) * 2,
        in_specs=[IN_SMEM] + [IN_VMEM] * 2 + [IN_PLACE] * 2 + [IN_VMEM] * len(sources),
        out_specs=(IN_VMEM,) * 2,
        scratch_shapes=[
            pltpu.VMEM((local_experts, pairs * slots, features), BF16),
            pltpu.VMEM((pairs, local_experts * slots, features), BF16),
            pltpu.VMEM((pairs * slots, units), BF16),
            pltpu.VMEM((pairs, local_experts * slots, tokens), BF16),
            pltpu.VMEM((local_experts, pairs * slots, 1), F32),
            pltpu.VMEM(gate_up.shape, BF16),
            pltpu.VMEM(down.shape, BF16),
            pltpu.SemaphoreType.DMA((2, local_experts)),
        ],
        compiler_params=pltpu.CompilerParams(vmem_limit_bytes=limit),
        name="experts",
    )(first_expert, ids, gates, in_hbm(gate_up), in_hbm(down), *sources)


def add_rows(left, right):
    return (left.astype(F32) + right.astype(F32)).astype(BF16)


def on_planes(
    hidden_in, tree_queries, tree_keys, tree_values, parents, accepted, tree_parents, request_prompt, prompt_lengths,
    prompt_keys, prompt_values, out_proj, gain, expert_ids, gate_weights, gate_up, down,
):
    tok_rows, features = hidden_in.shape
    prompt_count, rows_here, _ = prompt_keys.shape
    me = lax.axis_index("ep").astype(jnp.int32)

    flat = (prompt_count * rows_here, features)
    send, send_prompts, mine, prompts = pack(
        (me % 2).reshape(1), tree_queries, tree_keys, tree_values, prompt_keys.reshape(flat),
        prompt_values.reshape(flat), expert_ids.astype(F32).T, gate_weights.T,
    )
    x_mine, y_mine = flip(prompts, 2, 8), flip(prompts, 4, 8)
    theirs = flip(send_prompts, 1, 8)
    x_theirs, y_theirs = flip(theirs, 2, 8), flip(theirs, 4, 8)
    far_a, far_b = flip(x_mine, 4, 8), flip(y_theirs, 2, 8)
    weights, pieces, order, last = fetch_projection(out_proj, prompts, (x_mine, y_mine, x_theirs, y_theirs, far_a, far_b))
    got = flip(send, 1, 8)
    small = jnp.concatenate(
        [tree_parents, jnp.broadcast_to(request_prompt[:, None], tree_parents.shape)], axis=0
    )
    sibling = flip(small, 1, 8)

    column = jnp.arange(8 * flat[0], dtype=jnp.int32)
    columns = jnp.stack([column // flat[0], column % flat[0] // rows_here, column % rows_here])
    chip_parents = jnp.concatenate([tree_parents, sibling[: tree_parents.shape[0]]], axis=0)
    first_node = jnp.arange(chip_parents.shape[0], dtype=jnp.int32)[:, None] * tree_parents.shape[1]
    chip_parents = jnp.where(chip_parents < 0, -1, chip_parents + first_node).reshape(-1, 1)
    attended, cache, ids, gates = chip_attention(
        (me.reshape(1), request_prompt, sibling, prompt_lengths), columns, chip_parents, accepted,
        tree_keys, tree_values, (mine, got, prompts, theirs, x_mine, x_theirs, y_mine, y_theirs, far_a, far_b),
    )
    last = after(last, attended, *weights[3:5])
    edge = last.shape[0] // 2
    weights += [last, flip(last[:edge], 2, 8), flip(last[edge:], 4, 8)]
    mine, other = chip_project(order, attended, weights, pieces)
    residual, normed = norm(hidden_in, mine, flip(other, 1, 8), gain)

    across = flip(normed, 6, 8)
    sibling_rows = flip(normed, 1, 8)
    first_expert = (me * gate_up.shape[0]).reshape(1)

    def run(low, high, sources, *done):
        limit = (34 + 8 * (high - low)) * 2**20
        return experts(first_expert, after(ids[low:high], done), gates[low:high], gate_up, down, sources, limit)

    near_same, near_other = run(0, 1, [normed, sibling_rows])
    sent, across = after((normed, across), near_same)
    from_x, from_y = flip(sent, 2, 8), flip(sent, 4, 8)
    far_same, far_other = run(3, 4, [across, flip(across, 1, 8)])
    far = add_rows(far_same, flip(after(far_other, from_x, from_y), 1, 8))
    back = flip(far[0], 6, 8)
    from_x, from_y = after((from_x, from_y), far)
    beside = [from_x, flip(from_x, 1, 8), from_y, flip(from_y, 1, 8)]
    side_same, side_other = run(1, 3, beside)
    side = add_rows(side_same, flip(after(side_other, back), 1, 8))
    terms = [near_same[0], flip(near_other, 1, 8)[0], back, flip(side[0], 2, 8), flip(side[1], 4, 8)]
    return residual, terms, cache


def on_any_mesh(
    hidden_in, tree_queries, tree_keys, tree_values, parents, accepted, tree_parents, request_prompt, prompt_lengths,
    prompt_keys, prompt_values, out_proj, gain, expert_ids, gate_weights, gate_up, down,
):
    tok_rows, features = hidden_in.shape
    prompt_count, rows_here, _ = prompt_keys.shape
    ep_size = lax.axis_size("ep")
    me = lax.axis_index("ep").astype(jnp.int32)
    keys = lax.all_gather(prompt_keys, "ep", axis=1, tiled=True).reshape(-1, features)
    values = lax.all_gather(prompt_values, "ep", axis=1, tiled=True).reshape(-1, features)
    column = jnp.arange(keys.shape[0], dtype=jnp.int32)
    columns = jnp.stack([column // (rows_here * ep_size), column % (rows_here * ep_size)])
    attended, cache = plain_attention(
        request_prompt, prompt_lengths, columns, parents, accepted, tree_queries, tree_keys, tree_values, keys, values
    )
    joined = lax.all_gather(out_proj, "rep", axis=0, tiled=True)
    projected = jnp.dot(attended, joined, preferred_element_type=F32)
    residual, normed = norm(hidden_in, projected, jnp.zeros(hidden_in.shape, BF16), gain)
    routing = jnp.concatenate([expert_ids.astype(F32).T, gate_weights.T], axis=0)
    routing = lax.all_gather(routing, "ep", axis=0).reshape(ep_size // 2, 2, -1, tok_rows)
    routing = jnp.concatenate([routing[:, 0], routing[:, 1]], axis=-1)
    top = expert_ids.shape[1]
    everyone = lax.all_gather(normed, "ep", axis=0, tiled=True)
    sources = [everyone[i * 2 * tok_rows : (i + 1) * 2 * tok_rows] for i in range(ep_size // 2)]
    same_core, other_core = experts(
        (me * gate_up.shape[0]).reshape(1), routing[:, :top], routing[:, top:], gate_up, down, sources, VMEM_LIMIT
    )
    shares = jnp.stack([same_core, other_core], axis=1).reshape(ep_size, tok_rows, features)
    shares = lax.all_to_all(shares, "ep", split_axis=0, concat_axis=0, tiled=True)
    return residual, [shares[i] for i in range(ep_size)], cache


def per_device(
    hidden_in,
    tree_queries,
    tree_keys,
    tree_values,
    tree_parents,
    accepted_nodes,
    request_prompt,
    prompt_lengths,
    prompt_keys,
    prompt_values,
    out_proj,
    norm_gain,
    expert_ids,
    gate_weights,
    expert_gate_up,
    expert_down,
):
    tok_rows, features = hidden_in.shape
    req_count, tree_len = tree_parents.shape
    first_node = jnp.arange(req_count, dtype=jnp.int32)[:, None] * tree_len
    accepted = (first_node + accepted_nodes).reshape(-1, 1)
    parents = jnp.where(tree_parents < 0, -1, tree_parents + first_node).reshape(-1, 1)
    planes = lax.axis_size("ep") == 8 and lax.axis_size("rep") == 4 and out_proj.shape[0] == 4 * HEAD_DIM
    plan = on_planes if planes else on_any_mesh
    residual, terms, cache = plan(
        hidden_in, tree_queries, tree_keys, tree_values, parents, accepted, tree_parents, request_prompt,
        prompt_lengths, prompt_keys, prompt_values, out_proj, norm_gain.reshape(1, features), expert_ids,
        gate_weights, expert_gate_up, expert_down,
    )
    layer_out = residual
    for term in terms:
        layer_out = layer_out + term.astype(F32)
    accepted_cache = cache.reshape(req_count, accepted_nodes.shape[1], 2 * features)
    return (layer_out.astype(BF16), accepted_cache)


def solution(mesh):
    in_specs = (
        P(("rep", "ep"), None),
        P(("rep", "ep"), None),
        P(("rep", "ep"), None),
        P(("rep", "ep"), None),
        P(("rep", "ep"), None),
        P(("rep", "ep"), None),
        P(("rep", "ep")),
        P("rep"),
        P("rep", "ep", None),
        P("rep", "ep", None),
        P("rep", None),
        P(),
        P(("rep", "ep"), None),
        P(("rep", "ep"), None),
        P("ep", None, None),
        P("ep", None, None),
    )
    out_specs = (P(("rep", "ep"), None), P(("rep", "ep"), None, None))
    return jax.shard_map(
        per_device, mesh=mesh, in_specs=in_specs, out_specs=out_specs, check_vma=False
    )
```

time: 438 us -> 142 us (0.32)
  waiting for transfers between devices: 237 us -> 53.5 us
  blocking collectives: 64.5 us -> 0 us
  local copies, waits for them, and re-layouts: 56.7 us -> 5.62 us
  Pallas kernels: 0 us -> 49.8 us
  matrix products: 28.3 us -> 0 us
  other arithmetic: 28.8 us -> 4.08 us
  starting transfers between devices: 5.15 us -> 26.9 us
  between operations: 14.6 us -> 0.98 us
    all_gather x3 -> x0, waiting for transfers between devices: 176 us -> none  [the longest x1 144 us: per_device(): lax.all_gather(out_proj, 'rep', axis=0, tiled=True)]
    all_to_all x1 -> x0, blocking collectives: 64.5 us -> none  [per_device(): lax.all_to_all(outgoing, 'ep', split_axis=0, concat_axis=0, tiled=True)]
    all_to_all x1 -> x0, waiting for transfers between devices: 58 us -> none  [per_device(): lax.all_to_all(replies, 'ep', split_axis=0, concat_axis=0, tiled=True)]
    ppermute x0 -> x31, waiting for transfers between devices: none -> 53.5 us  [the longest x27 46.9 us: flip(): return lax.ppermute(value, 'ep', [(i, i ^ bits) for i in range(size)])]
    pallas_call x0 -> x7, Pallas kernels: none -> 49.8 us  [the longest x3 34.7 us: experts(): pl.pallas_call(lambda *refs: experts_body(len(sources) // pairs, *refs),...]
    dot_general x19 -> x0, matrix products: 27.3 us -> none  [the longest x4 8.75 us: per_device(): jnp.dot(rows_in, expert_gate_up[expert], preferred_element_type=jnp.float32)]
    ppermute x0 -> x31, starting transfers between devices: none -> 26.9 us  [the longest x27 20.3 us: flip(): return lax.ppermute(value, 'ep', [(i, i ^ bits) for i in range(size)])]
    scatter x1 -> x0, local copies, waits for them, and re-layouts: 23.3 us -> none  [per_device(): outgoing = jnp.zeros((expert_total * CAP, feature_count), jnp.bfloat16).a...]
  transfers between devices with their start and end apart: 4 -> 31, of which waited for: 4 -> 22; matrix products, arithmetic and copies ran while one was open for 11% -> 2% of each run, Pallas kernels for 0% -> 31%
where the time goes in v2:
time: 142 us; the launch traced here: 141 us
  waiting for transfers between devices  53.5 us (38%)
  Pallas kernels  49.8 us (35%)
  starting transfers between devices  26.9 us (19%)
  local copies, waits for them, and re-layouts  5.62 us (4%)
  other arithmetic  4.08 us (3%)
    ppermute x27, waiting for transfers between devices, flip(): return lax.ppermute(value, 'ep', [(i, i ^ bits) for i in range(size)])  46.9 us
    pallas_call x3, Pallas kernels, experts(): pl.pallas_call(lambda *refs: experts_body(len(sources) // pairs, *refs),...  34.7 us
    ppermute x27, starting transfers between devices, flip(): return lax.ppermute(value, 'ep', [(i, i ^ bits) for i in range(size)])  20.3 us
    pallas_call x1, Pallas kernels, chip_attention(): pl.pallas_call(chip_attention_body, out_shape=(everywhere((heads, 2 * row...  9.36 us
    ppermute x2, waiting for transfers between devices, shifted(): return lax.ppermute(value, 'rep', [(i, (i + by) % 4) for i in range(4)])  5.24 us
    ppermute x2, starting transfers between devices, shifted(): return lax.ppermute(value, 'rep', [(i, (i + by) % 4) for i in range(4)])  3.88 us
    unnamed x30, local copies, waits for them, and re-layouts  2.86 us
  transfers between devices with their start and end apart: 31, of which 22 were waited for; matrix products, arithmetic and copies ran while one was open for 2% of the time, Pallas kernels for 31%

profile of v2, /device:TPU:0, one launch (start us, length us, event | category | flops | bytes accessed | tf_op | source)
XLA Modules:
  0.0 140.9 jit_solution(5336692167581812757)
XLA Ops:
  0.7 0.8 convert_bitcast_fusion.refs_5_
  1.5 0.7 copy-done.9
  2.2 2.0 %pack.1 = (bf16[384,1024]{1,0:T(8,128)(2,1)S(1)}, bf16[208,1024]{1,0:T(8,128)(2,1)S(1)}, bf16[384,1024]{1,0:T(8,128)(2,1)S(1)}, bf16[208,1024]{1,0:T(8,128)(2,1)S(1)}) custom-call(s32[1]{0:T(128)} %bitcast.9.core, bf16[128,2048]{1,0:T(8,128)(2,1)} %refs_0_.2, bf16[128,2048]{1,0:T(8,128)(2,1)} %refs_0_.3, bf16[128,2048]{1,0:T(8,128)(2,1)} %refs_1_.3, ...), custom_call_target="tpu_custom_call" | custom-call | tf_op jit(solution)/shard_map/pack/pallas_call | solution.py:87
  4.2 0.9 copy-done.3
  6.0 2.9 %collective-permute-start.3 = (bf16[208,1024]{1,0:T(8,128)(2,1)S(1)}, bf16[208,1024]{1,0:T(8,128)(2,1)}, u32[]{:S(2)}, u32[]{:S(2)}) collective-permute-start(bf16[208,1024]{1,0:T(8,128)(2,1)S(1)} %get-tuple-element.34.refs_4_), channel_id=1, source_target_pairs={{0,2},{1,3},{2,0},{3,1},{4,6},{5,7},{6,4},{7,5},{8,10},{9,11},{10,... | collective-permute-start | bytes 1277960 | tf_op jit(solution)/shard_map/ppermute | solution.py:23
  8.9 1.5 %collective-permute-start.5 = (bf16[208,1024]{1,0:T(8,128)(2,1)S(1)}, bf16[208,1024]{1,0:T(8,128)(2,1)}, u32[]{:S(2)}, u32[]{:S(2)}) collective-permute-start(bf16[208,1024]{1,0:T(8,128)(2,1)S(1)} %get-tuple-element.34.refs_4_), channel_id=1, source_target_pairs={{0,4},{1,5},{2,6},{3,7},{4,0},{5,1},{6,2},{7,3},{8,12},{9,13},{10,... | collective-permute-start | bytes 1277960 | tf_op jit(solution)/shard_map/ppermute | solution.py:23
  11.0 1.6 %collective-permute-start.9 = (bf16[128,2048]{1,0:T(8,128)(2,1)S(1)}, bf16[128,2048]{1,0:T(8,128)(2,1)}, u32[]{:S(2)}, u32[]{:S(2)}) collective-permute-start(bf16[128,2048]{1,0:T(8,128)(2,1)S(1)} %constant_dynamic-slice_fusion), channel_id=1, source_target_pairs={{0,8},{8,16},{16,24},{24,0},{1,9},{9,17},{17,25},{25,1},{2,10},{10... | collective-permute-start | bytes 1572872 | tf_op jit(solution)/shard_map/ppermute | solution.py:237
  12.6 2.2 %collective-permute-start.10 = (bf16[128,2048]{1,0:T(8,128)(2,1)S(1)}, bf16[128,2048]{1,0:T(8,128)(2,1)}, u32[]{:S(2)}, u32[]{:S(2)}) collective-permute-start(bf16[128,2048]{1,0:T(8,128)(2,1)S(1)} %constant_dynamic-slice_fusion), channel_id=1, source_target_pairs={{0,24},{8,0},{16,8},{24,16},{1,25},{9,1},{17,9},{25,17},{2,26},{10... | collective-permute-start | bytes 1572872 | tf_op jit(solution)/shard_map/ppermute | solution.py:237
  14.9 4.0 %collective-permute-done.3.refs_6_ = bf16[208,1024]{1,0:T(8,128)(2,1)} collective-permute-done((bf16[208,1024]{1,0:T(8,128)(2,1)S(1)}, bf16[208,1024]{1,0:T(8,128)(2,1)}, u32[]{:S(2)}, u32[]{:S(2)}) %collective-permute-start.3) | collective-permute-done | bytes 426016 | tf_op jit(solution)/shard_map/ppermute | solution.py:23
  18.8 1.7 %collective-permute-start.4 = (bf16[208,1024]{1,0:T(8,128)(2,1)}, bf16[208,1024]{1,0:T(8,128)(2,1)}, u32[]{:S(2)}, u32[]{:S(2)}) collective-permute-start(bf16[208,1024]{1,0:T(8,128)(2,1)} %collective-permute-done.2.refs_5_), channel_id=1, source_target_pairs={{0,2},{1,3},{2,0},{3,1},{4,6},{5,7},{6,4},{7,5},{8,10},{9,11},{10,... | collective-permute-start | bytes 1277960 | tf_op jit(solution)/shard_map/ppermute | solution.py:23
  20.6 1.2 collective-permute-done.5.refs_8_
  21.8 1.5 %collective-permute-start.7 = (bf16[208,1024]{1,0:T(8,128)(2,1)}, bf16[208,1024]{1,0:T(8,128)(2,1)}, u32[]{:S(2)}, u32[]{:S(2)}) collective-permute-start(bf16[208,1024]{1,0:T(8,128)(2,1)} %collective-permute-done.3.refs_6_), channel_id=1, source_target_pairs={{0,4},{1,5},{2,6},{3,7},{4,0},{5,1},{6,2},{7,3},{8,12},{9,13},{10,... | collective-permute-start | bytes 1277960 | tf_op jit(solution)/shard_map/ppermute | solution.py:23
  23.3 7.6 %collective-permute-done.6.refs_9_ = bf16[208,1024]{1,0:T(8,128)(2,1)} collective-permute-done((bf16[208,1024]{1,0:T(8,128)(2,1)}, bf16[208,1024]{1,0:T(8,128)(2,1)}, u32[]{:S(2)}, u32[]{:S(2)}) %collective-permute-start.6) | collective-permute-done | bytes 426016 | tf_op jit(solution)/shard_map/ppermute | solution.py:23
  31.3 5.2 %collective-permute-done.10 = bf16[128,2048]{1,0:T(8,128)(2,1)} collective-permute-done((bf16[128,2048]{1,0:T(8,128)(2,1)S(1)}, bf16[128,2048]{1,0:T(8,128)(2,1)}, u32[]{:S(2)}, u32[]{:S(2)}) %collective-permute-start.10) | collective-permute-done | bytes 524320 | tf_op jit(solution)/shard_map/ppermute | solution.py:237
  36.5 1.5 %collective-permute-start.13 = (bf16[128,2048]{1,0:T(8,128)(2,1)}, bf16[128,2048]{1,0:T(8,128)(2,1)}, u32[]{:S(2)}, u32[]{:S(2)}) collective-permute-start(bf16[128,2048]{1,0:T(8,128)(2,1)} %collective-permute-done.9), channel_id=1, source_target_pairs={{8,16},{16,24},{9,17},{17,25},{10,18},{18,26},{11,19},{19,27},{12,... | collective-permute-start | bytes 1572872 | tf_op jit(solution)/shard_map/ppermute | solution.py:240
  38.6 1.3 collective-permute-start.14
  40.1 1.3 fusion.5
  41.5 0.7 collective-permute-start.11
  42.2 1.6 %collective-permute-start.12 = (bf16[128,2048]{1,0:T(8,128)(2,1)S(1)}, bf16[128,2048]{1,0:T(8,128)(2,1)}, u32[]{:S(2)}, u32[]{:S(2)}) collective-permute-start(bf16[128,2048]{1,0:T(8,128)(2,1)S(1)} %pad_maximum_fusion.1.refs_4_), channel_id=1, source_target_pairs={{0,4},{1,5},{2,6},{3,7},{4,0},{5,1},{6,2},{7,3},{8,12},{9,13},{10,... | collective-permute-start | bytes 1572872 | tf_op jit(solution)/shard_map/ppermute | solution.py:23
  44.1 9.4 %attention.1 = (bf16[8,256,128]{2,1,0:T(8,128)(2,1)S(1)}, bf16[32,4096]{1,0:T(8,128)(2,1)}, f32[4,8,256]{2,1,0:T(8,128)S(1)}, f32[4,8,256]{2,1,0:T(8,128)S(1)}) custom-call(s32[1]{0:T(128)} %bitcast.8.me, s32[2]{0:T(128)S(1)} %copy-done.10, s32[4,64]{1,0:T(4,128)S(1)} %collective-permute-done.sibling, s32[4]{0:T(128)S(1)} %copy-done.11, ...), custom_call_target="tpu_custom_call" | custom-call | tf_op jit(solution)/shard_map/attention/pallas_call | solution.py:183
  53.5 0.8 copy-done.4
  54.3 1.4 %collective-permute-done.14 = bf16[128,2048]{1,0:T(8,128)(2,1)} collective-permute-done((bf16[128,2048]{1,0:T(8,128)(2,1)}, bf16[128,2048]{1,0:T(8,128)(2,1)}, u32[]{:S(2)}, u32[]{:S(2)}) %collective-permute-start.14) | collective-permute-done | bytes 524320 | tf_op jit(solution)/shard_map/ppermute | solution.py:241
  55.7 0.7 collective-permute-done.12.refs_6_
  56.4 1.1 broadcast_select_fusion.refs_7_
  57.5 0.9 fusion.4
  58.3 0.7 collective-permute-start.15
  59.0 1.5 %collective-permute-start.16 = (bf16[64,2048]{1,0:T(8,128)(2,1)}, bf16[64,2048]{1,0:T(8,128)(2,1)}, u32[]{:S(2)}, u32[]{:S(2)}) collective-permute-start(bf16[64,2048]{1,0:T(8,128)(2,1)} %get-tuple-element.64), channel_id=1, source_target_pairs={{0,4},{1,5},{2,6},{3,7},{4,0},{5,1},{6,2},{7,3},{8,12},{9,13},{10,... | collective-permute-start | bytes 786440 | tf_op jit(solution)/shard_map/ppermute | solution.py:23
  60.7 5.4 %collective-permute-done.15.refs_8_ = bf16[64,2048]{1,0:T(8,128)(2,1)S(1)} collective-permute-done((bf16[64,2048]{1,0:T(8,128)(2,1)}, bf16[64,2048]{1,0:T(8,128)(2,1)S(1)}, u32[]{:S(2)}, u32[]{:S(2)}) %collective-permute-start.15) | collective-permute-done | bytes 262176 | tf_op jit(solution)/shard_map/ppermute | solution.py:23
  66.5 2.5 %project.1 = (f32[128,2048]{1,0:T(8,128)S(1)}, bf16[128,2048]{1,0:T(8,128)(2,1)S(1)}) custom-call(s32[8]{0:T(128)S(1)} %stack.41.refs_0_, bf16[8,256,128]{2,1,0:T(8,128)(2,1)S(1)} %copy-done.5, bf16[256,2048]{1,0:T(8,128)(2,1)S(1)} %constant_dynamic-slice_fusion.1.refs_2_, bf16[128,2048]{1,0:T(8,128)(2,1)S(1)} %pad_maximum_fusion.refs_3_, ...), custom_call_target="tpu_custom_call" | custom-call | tf_op jit(solution)/shard_map/project/pallas_call | solution.py:279
  69.2 1.9 %collective-permute-done.17.other = bf16[128,2048]{1,0:T(8,128)(2,1)S(1)} collective-permute-done((bf16[128,2048]{1,0:T(8,128)(2,1)S(1)}, bf16[128,2048]{1,0:T(8,128)(2,1)S(1)}, u32[]{:S(2)}, u32[]{:S(2)}) %collective-permute-start.17) | collective-permute-done | bytes 524320 | tf_op jit(solution)/shard_map/ppermute | solution.py:23
  71.1 1.2 norm.1
  72.4 1.6 %collective-permute-start.20 = (bf16[128,2048]{1,0:T(8,128)(2,1)}, bf16[128,2048]{1,0:T(8,128)(2,1)}, u32[]{:S(2)}, u32[]{:S(2)}) collective-permute-start(bf16[128,2048]{1,0:T(8,128)(2,1)} %get-tuple-element.54.refs_5_), channel_id=1, source_target_pairs={{0,6},{1,7},{2,4},{3,5},{4,2},{5,3},{6,0},{7,1},{8,14},{9,15},{10,... | collective-permute-start | bytes 1572872 | tf_op jit(solution)/shard_map/ppermute | solution.py:23
  74.5 11.1 %experts.3 = (bf16[1,128,2048]{2,1,0:T(8,128)(2,1)S(1)}, bf16[1,128,2048]{2,1,0:T(8,128)(2,1)S(1)}) custom-call(s32[1]{0:T(128)} %bitcast.15.refs_0_, f32[1,8,256]{2,1,0:T(8,128)S(1)} %get-tuple-element.73.refs_1_, f32[1,8,256]{2,1,0:T(8,128)S(1)} %get-tuple-element.71.refs_2_, bf16[4,2048,1024]{2,1,0:T(8,128)(2,1)} %refs_3_.5, ...), custom_call_target="tpu_custom_call" | custom-call | tf_op jit(solution)/shard_map/experts/pallas_call | solution.py:394
  85.6 2.2 %collective-permute-done.20.refs_5_ = bf16[128,2048]{1,0:T(8,128)(2,1)} collective-permute-done((bf16[128,2048]{1,0:T(8,128)(2,1)}, bf16[128,2048]{1,0:T(8,128)(2,1)}, u32[]{:S(2)}, u32[]{:S(2)}) %collective-permute-start.20) | collective-permute-done | bytes 524320 | tf_op jit(solution)/shard_map/ppermute | solution.py:23
  87.8 1.4 %collective-permute-start.22 = (bf16[128,2048]{1,0:T(8,128)(2,1)}, bf16[128,2048]{1,0:T(8,128)(2,1)S(1)}, u32[]{:S(2)}, u32[]{:S(2)}) collective-permute-start(bf16[128,2048]{1,0:T(8,128)(2,1)} %get-tuple-element.54.refs_5_), channel_id=1, source_target_pairs={{0,2},{1,3},{2,0},{3,1},{4,6},{5,7},{6,4},{7,5},{8,10},{9,11},{10,... | collective-permute-start | bytes 1572872 | tf_op jit(solution)/shard_map/ppermute | solution.py:23
  89.2 0.7 collective-permute-start.23
  90.0 11.3 %experts.4 = (bf16[1,128,2048]{2,1,0:T(8,128)(2,1)S(1)}, bf16[1,128,2048]{2,1,0:T(8,128)(2,1)S(1)}) custom-call(s32[1]{0:T(128)} %bitcast.15.refs_0_, f32[1,8,256]{2,1,0:T(8,128)S(1)} %get-tuple-element.72.refs_1_, f32[1,8,256]{2,1,0:T(8,128)S(1)} %get-tuple-element.70.refs_2_, bf16[4,2048,1024]{2,1,0:T(8,128)(2,1)} %refs_3_.5, ...), custom_call_target="tpu_custom_call" | custom-call | tf_op jit(solution)/shard_map/experts/pallas_call | solution.py:394
  101.3 1.1 collective-permute-done.22.refs_5_
  102.3 1.1 collective-permute-done.23.refs_7_
  103.5 1.9 %collective-permute-done.24 = bf16[1,128,2048]{2,1,0:T(8,128)(2,1)S(1)} collective-permute-done((bf16[1,128,2048]{2,1,0:T(8,128)(2,1)S(1)}, bf16[1,128,2048]{2,1,0:T(8,128)(2,1)S(1)}, u32[]{:S(2)}, u32[]{:S(2)}) %collective-permute-start.24) | collective-permute-done | bytes 524320 | tf_op jit(solution)/shard_map/ppermute | solution.py:23
  106.1 0.7 collective-permute-start.25
  106.9 0.6 collective-permute-done.26.refs_6_
  107.5 0.7 collective-permute-done.27.refs_8_
  108.3 12.3 %experts.5 = (bf16[2,128,2048]{2,1,0:T(8,128)(2,1)S(1)}, bf16[2,128,2048]{2,1,0:T(8,128)(2,1)}) custom-call(s32[1]{0:T(128)} %bitcast.15.refs_0_, f32[2,8,256]{2,1,0:T(8,128)S(1)} %slice.56.refs_1_, f32[2,8,256]{2,1,0:T(8,128)S(1)} %slice.57.refs_2_, bf16[4,2048,1024]{2,1,0:T(8,128)(2,1)} %refs_3_.5, bf16[4,512,2048]{2,1,0:T(8,128)(2,1)} %refs_4_.5, ...), custom_call_target="tpu_custom_call" | custom-call | tf_op jit(solution)/shard_map/experts/pallas_call | solution.py:394
  121.5 3.1 %collective-permute-done.28 = bf16[2,128,2048]{2,1,0:T(8,128)(2,1)S(1)} collective-permute-done((bf16[2,128,2048]{2,1,0:T(8,128)(2,1)}, bf16[2,128,2048]{2,1,0:T(8,128)(2,1)S(1)}, u32[]{:S(2)}, u32[]{:S(2)}) %collective-permute-start.28) | collective-permute-done | bytes 1048608 | tf_op jit(solution)/shard_map/ppermute | solution.py:23
  125.1 0.8 collective-permute-start.30
  126.5 12.7 %collective-permute-done.30 = bf16[128,2048]{1,0:T(8,128)(2,1)S(1)} collective-permute-done((bf16[128,2048]{1,0:T(8,128)(2,1)S(1)}, bf16[128,2048]{1,0:T(8,128)(2,1)S(1)}, u32[]{:S(2)}, u32[]{:S(2)}) %collective-permute-start.30) | collective-permute-done | bytes 524320 | tf_op jit(solution)/shard_map/ppermute | solution.py:23
  139.6 1.3 fusion.3
  (80 shorter events, 7.5 us)
Async XLA Ops:
  0.6 10.3 %copy-start = (bf16[512,2048]{1,0:T(8,128)(2,1)S(1)}, bf16[512,2048]{1,0:T(8,128)(2,1)}, u32[]{:S(2)}) copy-start(bf16[512,2048]{1,0:T(8,128)(2,1)} %param.26) | copy-start | bytes 6291460
  0.6 30.3 %copy-start.14 = (s32[2,16]{1,0:T(2,128)S(1)}, s32[2,16]{1,0:T(2,128)}, u32[]{:S(2)}) copy-start(s32[2,16]{1,0:T(2,128)} %param.21) | copy-start | bytes 388
  0.7 30.3 %copy-start.10 = (s32[2]{0:T(128)S(1)}, s32[2]{0:T(128)}, u32[]{:S(2)}) copy-start(s32[2]{0:T(128)} %my_prompts.1) | copy-start | bytes 28
  0.7 30.5 %copy-start.13 = (s32[2,64]{1,0:T(2,128)S(1)}, s32[2,64]{1,0:T(2,128)}, u32[]{:S(2)}) copy-start(s32[2,64]{1,0:T(2,128)} %param.20) | copy-start | bytes 1540
  1.5 0.7 copy-start.9
  4.2 0.9 copy-start.3
  5.1 0.9 copy-start.12
  5.1 36.3 %copy-start.7 = (bf16[208,1024]{1,0:T(8,128)(2,1)}, bf16[208,1024]{1,0:T(8,128)(2,1)S(1)}, u32[]{:S(2)}) copy-start(bf16[208,1024]{1,0:T(8,128)(2,1)S(1)} %get-tuple-element.34.refs_4_) | copy-start | bytes 1277956
  5.1 5.3 %collective-permute-start.2 = (bf16[208,1024]{1,0:T(8,128)(2,1)S(1)}, bf16[208,1024]{1,0:T(8,128)(2,1)}, u32[]{:S(2)}, u32[]{:S(2)}) collective-permute-start(bf16[208,1024]{1,0:T(8,128)(2,1)S(1)} %get-tuple-element.35), channel_id=1, source_target_pairs={{0,1},{1,0},{2,3},{3,2},{4,5},{5,4},{6,7},{7,6},{8,9},{9,8},{10,11... | collective-permute-start | bytes 1277960 | tf_op jit(solution)/shard_map/ppermute | solution.py:23
  6.0 12.9 %collective-permute-start.3 = (bf16[208,1024]{1,0:T(8,128)(2,1)S(1)}, bf16[208,1024]{1,0:T(8,128)(2,1)}, u32[]{:S(2)}, u32[]{:S(2)}) collective-permute-start(bf16[208,1024]{1,0:T(8,128)(2,1)S(1)} %get-tuple-element.34.refs_4_), channel_id=1, source_target_pairs={{0,2},{1,3},{2,0},{3,1},{4,6},{5,7},{6,4},{7,5},{8,10},{9,11},{10,... | collective-permute-start | bytes 1277960 | tf_op jit(solution)/shard_map/ppermute | solution.py:23
  8.9 12.9 %collective-permute-start.5 = (bf16[208,1024]{1,0:T(8,128)(2,1)S(1)}, bf16[208,1024]{1,0:T(8,128)(2,1)}, u32[]{:S(2)}, u32[]{:S(2)}) collective-permute-start(bf16[208,1024]{1,0:T(8,128)(2,1)S(1)} %get-tuple-element.34.refs_4_), channel_id=1, source_target_pairs={{0,4},{1,5},{2,6},{3,7},{4,0},{5,1},{6,2},{7,3},{8,12},{9,13},{10,... | collective-permute-start | bytes 1277960 | tf_op jit(solution)/shard_map/ppermute | solution.py:23
  10.4 20.5 %collective-permute-start.6 = (bf16[208,1024]{1,0:T(8,128)(2,1)}, bf16[208,1024]{1,0:T(8,128)(2,1)}, u32[]{:S(2)}, u32[]{:S(2)}) collective-permute-start(bf16[208,1024]{1,0:T(8,128)(2,1)} %collective-permute-done.2.refs_5_), channel_id=1, source_target_pairs={{0,4},{1,5},{2,6},{3,7},{4,0},{5,1},{6,2},{7,3},{8,12},{9,13},{10,... | collective-permute-start | bytes 1277960 | tf_op jit(solution)/shard_map/ppermute | solution.py:23
  11.0 20.2 %collective-permute-start.9 = (bf16[128,2048]{1,0:T(8,128)(2,1)S(1)}, bf16[128,2048]{1,0:T(8,128)(2,1)}, u32[]{:S(2)}, u32[]{:S(2)}) collective-permute-start(bf16[128,2048]{1,0:T(8,128)(2,1)S(1)} %constant_dynamic-slice_fusion), channel_id=1, source_target_pairs={{0,8},{8,16},{16,24},{24,0},{1,9},{9,17},{17,25},{25,1},{2,10},{10... | collective-permute-start | bytes 1572872 | tf_op jit(solution)/shard_map/ppermute | solution.py:237
  12.6 23.9 %collective-permute-start.10 = (bf16[128,2048]{1,0:T(8,128)(2,1)S(1)}, bf16[128,2048]{1,0:T(8,128)(2,1)}, u32[]{:S(2)}, u32[]{:S(2)}) collective-permute-start(bf16[128,2048]{1,0:T(8,128)(2,1)S(1)} %constant_dynamic-slice_fusion), channel_id=1, source_target_pairs={{0,24},{8,0},{16,8},{24,16},{1,25},{9,1},{17,9},{25,17},{2,26},{10... | collective-permute-start | bytes 1572872 | tf_op jit(solution)/shard_map/ppermute | solution.py:237
  18.8 17.7 %collective-permute-start.4 = (bf16[208,1024]{1,0:T(8,128)(2,1)}, bf16[208,1024]{1,0:T(8,128)(2,1)}, u32[]{:S(2)}, u32[]{:S(2)}) collective-permute-start(bf16[208,1024]{1,0:T(8,128)(2,1)} %collective-permute-done.2.refs_5_), channel_id=1, source_target_pairs={{0,2},{1,3},{2,0},{3,1},{4,6},{5,7},{6,4},{7,5},{8,10},{9,11},{10,... | collective-permute-start | bytes 1277960 | tf_op jit(solution)/shard_map/ppermute | solution.py:23
  21.8 16.8 %collective-permute-start.7 = (bf16[208,1024]{1,0:T(8,128)(2,1)}, bf16[208,1024]{1,0:T(8,128)(2,1)}, u32[]{:S(2)}, u32[]{:S(2)}) collective-permute-start(bf16[208,1024]{1,0:T(8,128)(2,1)} %collective-permute-done.3.refs_6_), channel_id=1, source_target_pairs={{0,4},{1,5},{2,6},{3,7},{4,0},{5,1},{6,2},{7,3},{8,12},{9,13},{10,... | collective-permute-start | bytes 1277960 | tf_op jit(solution)/shard_map/ppermute | solution.py:23
  30.9 9.2 %collective-permute-start.8 = (bf16[208,1024]{1,0:T(8,128)(2,1)}, bf16[208,1024]{1,0:T(8,128)(2,1)}, u32[]{:S(2)}, u32[]{:S(2)}) collective-permute-start(bf16[208,1024]{1,0:T(8,128)(2,1)} %collective-permute-done.6.refs_9_), channel_id=1, source_target_pairs={{0,2},{1,3},{2,0},{3,1},{4,6},{5,7},{6,4},{7,5},{8,10},{9,11},{10,... | collective-permute-start | bytes 1277960 | tf_op jit(solution)/shard_map/ppermute | solution.py:23
  31.2 11.0 %collective-permute-start = (s32[4,64]{1,0:T(4,128)S(1)}, s32[4,64]{1,0:T(4,128)S(1)}, u32[]{:S(2)}, u32[]{:S(2)}) collective-permute-start(s32[4,64]{1,0:T(4,128)S(1)} %pad_add_fusion.2), channel_id=1, source_target_pairs={{0,1},{1,0},{2,3},{3,2},{4,5},{5,4},{6,7},{7,6},{8,9},{9,8},{10,11... | collective-permute-start | bytes 3080 | tf_op jit(solution)/shard_map/ppermute | solution.py:23
  36.5 7.6 %copy-start.11 = (s32[4]{0:T(128)S(1)}, s32[4]{0:T(128)}, u32[]{:S(2)}) copy-start(s32[4]{0:T(128)} %lengths.1) | copy-start | bytes 52
  36.5 7.5 %collective-permute-start.1 = (bf16[384,1024]{1,0:T(8,128)(2,1)}, bf16[384,1024]{1,0:T(8,128)(2,1)}, u32[]{:S(2)}, u32[]{:S(2)}) collective-permute-start(bf16[384,1024]{1,0:T(8,128)(2,1)} %copy-done.12), channel_id=1, source_target_pairs={{0,1},{1,0},{2,3},{3,2},{4,5},{5,4},{6,7},{7,6},{8,9},{9,8},{10,11... | collective-permute-start | bytes 2359304 | tf_op jit(solution)/shard_map/ppermute | solution.py:23
  36.5 17.7 %collective-permute-start.13 = (bf16[128,2048]{1,0:T(8,128)(2,1)}, bf16[128,2048]{1,0:T(8,128)(2,1)}, u32[]{:S(2)}, u32[]{:S(2)}) collective-permute-start(bf16[128,2048]{1,0:T(8,128)(2,1)} %collective-permute-done.9), channel_id=1, source_target_pairs={{8,16},{16,24},{9,17},{17,25},{10,18},{18,26},{11,19},{19,27},{12,... | collective-permute-start | bytes 1572872 | tf_op jit(solution)/shard_map/ppermute | solution.py:240
  38.6 17.1 %collective-permute-start.14 = (bf16[128,2048]{1,0:T(8,128)(2,1)}, bf16[128,2048]{1,0:T(8,128)(2,1)}, u32[]{:S(2)}, u32[]{:S(2)}) collective-permute-start(bf16[128,2048]{1,0:T(8,128)(2,1)} %collective-permute-done.10), channel_id=1, source_target_pairs={{16,8},{8,0},{17,9},{9,1},{18,10},{10,2},{19,11},{11,3},{20,12},{1... | collective-permute-start | bytes 1572872 | tf_op jit(solution)/shard_map/ppermute | solution.py:241
  41.5 14.2 %collective-permute-start.11 = (bf16[128,2048]{1,0:T(8,128)(2,1)S(1)}, bf16[128,2048]{1,0:T(8,128)(2,1)}, u32[]{:S(2)}, u32[]{:S(2)}) collective-permute-start(bf16[128,2048]{1,0:T(8,128)(2,1)S(1)} %pad_maximum_fusion.refs_3_), channel_id=1, source_target_pairs={{0,2},{1,3},{2,0},{3,1},{4,6},{5,7},{6,4},{7,5},{8,10},{9,11},{10,... | collective-permute-start | bytes 1572872 | tf_op jit(solution)/shard_map/ppermute | solution.py:23
  42.2 11.3 %copy-start.1 = (bf16[128,2048]{1,0:T(8,128)(2,1)}, bf16[128,2048]{1,0:T(8,128)(2,1)S(1)}, u32[]{:S(2)}) copy-start(bf16[128,2048]{1,0:T(8,128)(2,1)S(1)} %pad_maximum_fusion.1.refs_4_) | copy-start | bytes 1572868
  42.2 14.2 %collective-permute-start.12 = (bf16[128,2048]{1,0:T(8,128)(2,1)S(1)}, bf16[128,2048]{1,0:T(8,128)(2,1)}, u32[]{:S(2)}, u32[]{:S(2)}) collective-permute-start(bf16[128,2048]{1,0:T(8,128)(2,1)S(1)} %pad_maximum_fusion.1.refs_4_), channel_id=1, source_target_pairs={{0,4},{1,5},{2,6},{3,7},{4,0},{5,1},{6,2},{7,3},{8,12},{9,13},{10,... | collective-permute-start | bytes 1572872 | tf_op jit(solution)/shard_map/ppermute | solution.py:23
  53.5 0.8 copy-start.4
  58.3 7.8 %collective-permute-start.15 = (bf16[64,2048]{1,0:T(8,128)(2,1)}, bf16[64,2048]{1,0:T(8,128)(2,1)S(1)}, u32[]{:S(2)}, u32[]{:S(2)}) collective-permute-start(bf16[64,2048]{1,0:T(8,128)(2,1)} %get-tuple-element.65), channel_id=1, source_target_pairs={{0,2},{1,3},{2,0},{3,1},{4,6},{5,7},{6,4},{7,5},{8,10},{9,11},{10,... | collective-permute-start | bytes 786440 | tf_op jit(solution)/shard_map/ppermute | solution.py:23
  59.0 7.5 %collective-permute-start.16 = (bf16[64,2048]{1,0:T(8,128)(2,1)}, bf16[64,2048]{1,0:T(8,128)(2,1)}, u32[]{:S(2)}, u32[]{:S(2)}) collective-permute-start(bf16[64,2048]{1,0:T(8,128)(2,1)} %get-tuple-element.64), channel_id=1, source_target_pairs={{0,4},{1,5},{2,6},{3,7},{4,0},{5,1},{6,2},{7,3},{8,12},{9,13},{10,... | collective-permute-start | bytes 786440 | tf_op jit(solution)/shard_map/ppermute | solution.py:23
  60.6 5.9 %copy-start.2 = (bf16[128,2048]{1,0:T(8,128)(2,1)S(1)}, bf16[128,2048]{1,0:T(8,128)(2,1)}, u32[]{:S(2)}) copy-start(bf16[128,2048]{1,0:T(8,128)(2,1)} %copy-done.1) | copy-start | bytes 1572868
  60.6 5.9 %copy-start.5 = (bf16[8,256,128]{2,1,0:T(8,128)(2,1)S(1)}, bf16[8,256,128]{2,1,0:T(8,128)(2,1)}, u32[]{:S(2)}) copy-start(bf16[8,256,128]{2,1,0:T(8,128)(2,1)} %copy-done.4) | copy-start | bytes 1572868
  60.7 10.4 %copy-start.6 = (bf16[128,2048]{1,0:T(8,128)(2,1)S(1)}, bf16[128,2048]{1,0:T(8,128)(2,1)}, u32[]{:S(2)}) copy-start(bf16[128,2048]{1,0:T(8,128)(2,1)} %hidden.1) | copy-start | bytes 1572868
  60.7 10.4 %copy-start.8 = (f32[2048]{0:T(1024)S(1)}, f32[2048]{0:T(1024)}, u32[]{:S(2)}) copy-start(f32[2048]{0:T(1024)} %param.27) | copy-start | bytes 24580
  69.1 2.0 %collective-permute-start.17 = (bf16[128,2048]{1,0:T(8,128)(2,1)S(1)}, bf16[128,2048]{1,0:T(8,128)(2,1)S(1)}, u32[]{:S(2)}, u32[]{:S(2)}) collective-permute-start(bf16[128,2048]{1,0:T(8,128)(2,1)S(1)} %get-tuple-element.44), channel_id=1, source_target_pairs={{0,1},{1,0},{2,3},{3,2},{4,5},{5,4},{6,7},{7,6},{8,9},{9,8},{10,11... | collective-permute-start | bytes 1572872 | tf_op jit(solution)/shard_map/ppermute | solution.py:23
  72.2 2.3 %collective-permute-start.18 = (bf16[128,2048]{1,0:T(8,128)(2,1)}, bf16[128,2048]{1,0:T(8,128)(2,1)}, u32[]{:S(2)}, u32[]{:S(2)}) collective-permute-start(bf16[128,2048]{1,0:T(8,128)(2,1)} %get-tuple-element.54.refs_5_), channel_id=1, source_target_pairs={{0,1},{1,0},{2,3},{3,2},{4,5},{5,4},{6,7},{7,6},{8,9},{9,8},{10,11... | collective-permute-start | bytes 1572872 | tf_op jit(solution)/shard_map/ppermute | solution.py:23
  72.4 15.4 %collective-permute-start.20 = (bf16[128,2048]{1,0:T(8,128)(2,1)}, bf16[128,2048]{1,0:T(8,128)(2,1)}, u32[]{:S(2)}, u32[]{:S(2)}) collective-permute-start(bf16[128,2048]{1,0:T(8,128)(2,1)} %get-tuple-element.54.refs_5_), channel_id=1, source_target_pairs={{0,6},{1,7},{2,4},{3,5},{4,2},{5,3},{6,0},{7,1},{8,14},{9,15},{10,... | collective-permute-start | bytes 1572872 | tf_op jit(solution)/shard_map/ppermute | solution.py:23
  87.8 2.2 %collective-permute-start.21 = (bf16[128,2048]{1,0:T(8,128)(2,1)}, bf16[128,2048]{1,0:T(8,128)(2,1)S(1)}, u32[]{:S(2)}, u32[]{:S(2)}) collective-permute-start(bf16[128,2048]{1,0:T(8,128)(2,1)} %collective-permute-done.20.refs_5_), channel_id=1, source_target_pairs={{0,1},{1,0},{2,3},{3,2},{4,5},{5,4},{6,7},{7,6},{8,9},{9,8},{10,11... | collective-permute-start | bytes 1572872 | tf_op jit(solution)/shard_map/ppermute | solution.py:23
  87.8 14.5 %collective-permute-start.22 = (bf16[128,2048]{1,0:T(8,128)(2,1)}, bf16[128,2048]{1,0:T(8,128)(2,1)S(1)}, u32[]{:S(2)}, u32[]{:S(2)}) collective-permute-start(bf16[128,2048]{1,0:T(8,128)(2,1)} %get-tuple-element.54.refs_5_), channel_id=1, source_target_pairs={{0,2},{1,3},{2,0},{3,1},{4,6},{5,7},{6,4},{7,5},{8,10},{9,11},{10,... | collective-permute-start | bytes 1572872 | tf_op jit(solution)/shard_map/ppermute | solution.py:23
  89.2 14.3 %collective-permute-start.23 = (bf16[128,2048]{1,0:T(8,128)(2,1)}, bf16[128,2048]{1,0:T(8,128)(2,1)S(1)}, u32[]{:S(2)}, u32[]{:S(2)}) collective-permute-start(bf16[128,2048]{1,0:T(8,128)(2,1)} %get-tuple-element.54.refs_5_), channel_id=1, source_target_pairs={{0,4},{1,5},{2,6},{3,7},{4,0},{5,1},{6,2},{7,3},{8,12},{9,13},{10,... | collective-permute-start | bytes 1572872 | tf_op jit(solution)/shard_map/ppermute | solution.py:23
  103.5 1.9 %collective-permute-start.24 = (bf16[1,128,2048]{2,1,0:T(8,128)(2,1)S(1)}, bf16[1,128,2048]{2,1,0:T(8,128)(2,1)S(1)}, u32[]{:S(2)}, u32[]{:S(2)}) collective-permute-start(bf16[1,128,2048]{2,1,0:T(8,128)(2,1)S(1)} %get-tuple-element.55), channel_id=1, source_target_pairs={{0,1},{1,0},{2,3},{3,2},{4,5},{5,4},{6,7},{7,6},{8,9},{9,8},{10,11... | collective-permute-start | bytes 1572872 | tf_op jit(solution)/shard_map/ppermute | solution.py:23
  105.5 2.0 %collective-permute-start.26 = (bf16[128,2048]{1,0:T(8,128)(2,1)S(1)}, bf16[128,2048]{1,0:T(8,128)(2,1)S(1)}, u32[]{:S(2)}, u32[]{:S(2)}) collective-permute-start(bf16[128,2048]{1,0:T(8,128)(2,1)S(1)} %collective-permute-done.22.refs_5_), channel_id=1, source_target_pairs={{0,1},{1,0},{2,3},{3,2},{4,5},{5,4},{6,7},{7,6},{8,9},{9,8},{10,11... | collective-permute-start | bytes 1572872 | tf_op jit(solution)/shard_map/ppermute | solution.py:23
  105.7 2.5 %collective-permute-start.27 = (bf16[128,2048]{1,0:T(8,128)(2,1)S(1)}, bf16[128,2048]{1,0:T(8,128)(2,1)S(1)}, u32[]{:S(2)}, u32[]{:S(2)}) collective-permute-start(bf16[128,2048]{1,0:T(8,128)(2,1)S(1)} %collective-permute-done.23.refs_7_), channel_id=1, source_target_pairs={{0,1},{1,0},{2,3},{3,2},{4,5},{5,4},{6,7},{7,6},{8,9},{9,8},{10,11... | collective-permute-start | bytes 1572872 | tf_op jit(solution)/shard_map/ppermute | solution.py:23
  106.1 14.9 %collective-permute-start.25 = (bf16[128,2048]{1,0:T(8,128)(2,1)S(1)}, bf16[128,2048]{1,0:T(8,128)(2,1)S(1)}, u32[]{:S(2)}, u32[]{:S(2)}) collective-permute-start(bf16[128,2048]{1,0:T(8,128)(2,1)S(1)} %bitcast.31), channel_id=1, source_target_pairs={{0,6},{1,7},{2,4},{3,5},{4,2},{5,3},{6,0},{7,1},{8,14},{9,15},{10,... | collective-permute-start | bytes 1572872 | tf_op jit(solution)/shard_map/ppermute | solution.py:23
  121.0 3.6 %collective-permute-start.28 = (bf16[2,128,2048]{2,1,0:T(8,128)(2,1)}, bf16[2,128,2048]{2,1,0:T(8,128)(2,1)S(1)}, u32[]{:S(2)}, u32[]{:S(2)}) collective-permute-start(bf16[2,128,2048]{2,1,0:T(8,128)(2,1)} %get-tuple-element.60), channel_id=1, source_target_pairs={{0,1},{1,0},{2,3},{3,2},{4,5},{5,4},{6,7},{7,6},{8,9},{9,8},{10,11... | collective-permute-start | bytes 3145736 | tf_op jit(solution)/shard_map/ppermute | solution.py:23
  121.0 5.5 %collective-permute-start.19 = (bf16[1,128,2048]{2,1,0:T(8,128)(2,1)S(1)}, bf16[1,128,2048]{2,1,0:T(8,128)(2,1)S(1)}, u32[]{:S(2)}, u32[]{:S(2)}) collective-permute-start(bf16[1,128,2048]{2,1,0:T(8,128)(2,1)S(1)} %get-tuple-element.50), channel_id=1, source_target_pairs={{0,1},{1,0},{2,3},{3,2},{4,5},{5,4},{6,7},{7,6},{8,9},{9,8},{10,11... | collective-permute-start | bytes 1572872 | tf_op jit(solution)/shard_map/ppermute | solution.py:23
  125.1 14.0 %collective-permute-start.30 = (bf16[128,2048]{1,0:T(8,128)(2,1)S(1)}, bf16[128,2048]{1,0:T(8,128)(2,1)S(1)}, u32[]{:S(2)}, u32[]{:S(2)}) collective-permute-start(bf16[128,2048]{1,0:T(8,128)(2,1)S(1)} %get-tuple-element.63), channel_id=1, source_target_pairs={{0,4},{1,5},{2,6},{3,7},{4,0},{5,1},{6,2},{7,3},{8,12},{9,13},{10,... | collective-permute-start | bytes 1572872 | tf_op jit(solution)/shard_map/ppermute | solution.py:23
  125.9 13.7 %collective-permute-start.29 = (bf16[128,2048]{1,0:T(8,128)(2,1)S(1)}, bf16[128,2048]{1,0:T(8,128)(2,1)S(1)}, u32[]{:S(2)}, u32[]{:S(2)}) collective-permute-start(bf16[128,2048]{1,0:T(8,128)(2,1)S(1)} %get-tuple-element.62), channel_id=1, source_target_pairs={{0,2},{1,3},{2,0},{3,1},{4,6},{5,7},{6,4},{7,5},{8,10},{9,11},{10,... | collective-permute-start | bytes 1572872 | tf_op jit(solution)/shard_map/ppermute | solution.py:23

commit v3 on v2

--- a/solution.py
+++ b/solution.py
@@ -45,13 +45,13 @@
 
 
 def pack_body(core, *refs):
-    sources, (ids, gates), (send, send_prompts, mine, prompts), held, sems = refs[:5], refs[5:7], refs[7:11], refs[11:16], refs[16]
-    copies = [pltpu.make_async_copy(sources[i], held[i], sems.at[i]) for i in range(5)]
+    sources, (send, send_prompts, mine, prompts), held, sems = refs[:7], refs[7:11], refs[11:18], refs[18]
+    copies = [pltpu.make_async_copy(sources[i], held[i], sems.at[i]) for i in range(7)]
     for copy in copies:
         copy.start()
     for copy in copies:
         copy.wait()
-    queries, keys, values, prompt_keys, prompt_values = held
+    queries, keys, values, prompt_keys, prompt_values, ids, gates = held
     rows, features = queries.shape
     shards = features // (4 * HEAD_DIM)
     width = 2 * HEAD_DIM
@@ -72,7 +72,7 @@
     high_part = gates[...].astype(BF16)
     low_part = (gates[...] - high_part.astype(F32)).astype(BF16)
     blank = jnp.zeros((top, rows), F32)
-    first = jnp.concatenate([ids[...], high_part.astype(F32)], axis=0).astype(BF16)
+    first = jnp.concatenate([ids[...].astype(F32), high_part.astype(F32)], axis=0).astype(BF16)
     second = jnp.concatenate([blank, low_part.astype(F32)], axis=0).astype(BF16)
     base = 2 * prompt_keys.shape[0]
     for target in (send_prompts, prompts):
@@ -84,6 +84,7 @@
 def pack(core, queries, keys, values, prompt_keys, prompt_values, ids, gates):
     rows, features = queries.shape
     tail = 2 * prompt_keys.shape[0] + 2 * ids.shape[0]
+    parts = (queries, keys, values, prompt_keys, prompt_values, ids, gates)
     return pl.pallas_call(
         pack_body,
         out_shape=(
@@ -92,13 +93,12 @@
             everywhere((3 * rows, features // 2), BF16),
             everywhere((tail, features // 2), BF16),
         ),
-        in_specs=[IN_SMEM] + [IN_PLACE] * 5 + [IN_VMEM] * 2,
+        in_specs=[IN_SMEM] + [IN_PLACE] * 7,
         out_specs=(IN_VMEM,) * 4,
-        scratch_shapes=[pltpu.VMEM(part.shape, BF16) for part in (queries, keys, values, prompt_keys, prompt_values)]
-        + [pltpu.SemaphoreType.DMA((5,))],
+        scratch_shapes=[pltpu.VMEM(part.shape, part.dtype) for part in parts] + [pltpu.SemaphoreType.DMA((7,))],
         compiler_params=pltpu.CompilerParams(vmem_limit_bytes=12 * 2**20),
         name="pack",
-    )(core, *[in_hbm(part) for part in (queries, keys, values, prompt_keys, prompt_values)], ids, gates)
+    )(core, *[in_hbm(part) for part in parts])
 
 
 def attend(queries, all_keys, all_values, bias):
@@ -137,12 +137,13 @@
 
 
 def chip_attention_body(
-    me, my_prompts, sibling, lengths, columns, parents, accepted, *refs
+    me, my_prompts, sibling, lengths, columns, parents, accepted, mine, prompts_here, *refs
 ):
-    copies = [pltpu.make_async_copy(refs[i], refs[17 + i], refs[29].at[i]) for i in range(12)]
+    copies = [pltpu.make_async_copy(refs[i], refs[15 + i], refs[25].at[i]) for i in range(10)]
     for copy in copies:
         copy.start()
-    (attended, cache, ids, gates, bias), (tree_keys, tree_values, mine, got, *holders) = refs[12:17], refs[17:29]
+    (attended, cache, ids, gates, bias), (tree_keys, tree_values, got, *holders) = refs[10:15], refs[15:25]
+    holders = [prompts_here, *holders]
     rows = tree_keys.shape[0]
     requests = my_prompts.shape[0]
     tree_len = rows // requests
@@ -175,11 +176,12 @@
         gates[index // 2, :, lanes] = first[8:] + second[8:]
 
 
-def chip_attention(scalars, columns, parents, accepted, tree_keys, tree_values, blocks):
+def chip_attention(scalars, columns, parents, accepted, tree_keys, tree_values, mine, prompts, blocks):
     rows, features = tree_keys.shape
     width = columns.shape[1] + 2 * rows
     heads = features // HEAD_DIM // 2
     copied = [in_hbm(part) for part in (tree_keys, tree_values, *blocks)]
+    kept = (mine, prompts)
     return pl.pallas_call(
         chip_attention_body,
         out_shape=(
@@ -188,14 +190,14 @@
             everywhere((4, 8, 2 * rows), F32),
             everywhere((4, 8, 2 * rows), F32),
         ),
-        in_specs=[IN_SMEM] * 4 + [IN_VMEM] * 3 + [IN_PLACE] * len(copied),
+        in_specs=[IN_SMEM] * 4 + [IN_VMEM] * 5 + [IN_PLACE] * len(copied),
         out_specs=(IN_VMEM,) * 4,
         scratch_shapes=[pltpu.VMEM((2 * rows, width), F32)]
         + [pltpu.VMEM(part.shape, BF16) for part in copied]
         + [pltpu.SemaphoreType.DMA((len(copied),))],
         compiler_params=pltpu.CompilerParams(vmem_limit_bytes=14 * 2**20),
         name="attention",
-    )(*scalars, columns, parents, accepted, *copied)
+    )(*scalars, columns, parents, accepted, *kept, *copied)
 
 
 def plain_attention_body(
@@ -252,36 +254,33 @@
     pieces = [(0, 0, 2 * HEAD_DIM)]
     for low in (0, half):
         pieces += [(index, low, low + half) for index in (1, 2, 3, 4)]
-    pieces += [(5, 0, HEAD_DIM), (6, 0, half), (7, 0, half)]
-    up, down = after((up, down), from_x, from_y)
-    came2 = jnp.where(me >= 2, up, down)
-    return weights, pieces, jnp.stack(order).astype(jnp.int32), came2
-
-
-def chip_project_body(pieces, order, attended, *refs):
-    weights, (mine, other, ordered) = refs[: len(refs) - 3], refs[len(refs) - 3 :]
-    rows, features = mine.shape
+    pieces += [(index, 0, half) for index in (5, 6, 7, 8)]
+    return weights, pieces, jnp.stack(order).astype(jnp.int32), up, down
+
+
+def chip_project_body(pieces, low_row, order, attended, *refs):
+    weights, (result, ordered) = refs[: len(refs) - 2], refs[len(refs) - 2 :]
+    rows, features = result.shape
     for index in range(attended.shape[0]):
-        ordered[:, index * HEAD_DIM : (index + 1) * HEAD_DIM] = attended[order[index]]
+        ordered[:, index * HEAD_DIM : (index + 1) * HEAD_DIM] = attended[order[index], low_row : low_row + rows, :]
     step = 256
     for column in range(0, features, step):
         joined = jnp.concatenate(
             [weights[ref][low:high, column : column + step] for ref, low, high in pieces], axis=0
         )
         total = jnp.dot(ordered[...], joined, preferred_element_type=F32)
-        mine[:, column : column + step] = total[:rows]
-        other[:, column : column + step] = total[rows:].astype(BF16)
-
-
-def chip_project(order, attended, weights, pieces):
+        result[:, column : column + step] = total.astype(result.dtype)
+
+
+def chip_project(order, attended, weights, pieces, low_row, dtype):
     heads, rows, _ = attended.shape
     features = weights[0].shape[1]
     return pl.pallas_call(
-        lambda *refs: chip_project_body(pieces, *refs),
-        out_shape=(everywhere((rows // 2, features), F32), everywhere((rows // 2, features), BF16)),
+        lambda *refs: chip_project_body(pieces, low_row, *refs),
+        out_shape=everywhere((rows // 2, features), dtype),
         in_specs=[IN_SMEM] + [IN_VMEM] * (1 + len(weights)),
-        out_specs=(IN_VMEM,) * 2,
-        scratch_shapes=[pltpu.VMEM((rows, heads * HEAD_DIM), BF16)],
+        out_specs=IN_VMEM,
+        scratch_shapes=[pltpu.VMEM((rows // 2, heads * HEAD_DIM), BF16)],
         compiler_params=pltpu.CompilerParams(vmem_limit_bytes=14 * 2**20),
         name="project",
     )(order, attended, *weights)
@@ -305,22 +304,40 @@
     )(hidden, mine, other, gain)
 
 
-def experts_body(per_pair, first_expert, ids, gates, gate_up_hbm, down_hbm, *refs):
+def stage_body(gate_up, down, *refs):
+    count = gate_up.shape[0]
+    sems = refs[2 * count]
+    copies = []
+    for expert in range(count):
+        copies.append(pltpu.make_async_copy(gate_up.at[expert], refs[expert], sems.at[expert]))
+        copies.append(pltpu.make_async_copy(down.at[expert], refs[count + expert], sems.at[count + expert]))
+    for copy in copies:
+        copy.start()
+    for copy in copies:
+        copy.wait()
+
+
+def stage(gate_up, down):
+    count = gate_up.shape[0]
+    staged = pl.pallas_call(
+        stage_body,
+        out_shape=[pltpu.VMEM(gate_up.shape[1:], BF16)] * count + [pltpu.VMEM(down.shape[1:], BF16)] * count,
+        in_specs=[IN_PLACE] * 2,
+        out_specs=[IN_PLACE] * (2 * count),
+        scratch_shapes=[pltpu.SemaphoreType.DMA((2 * count,))],
+        compiler_params=pltpu.CompilerParams(vmem_limit_bytes=2**20),
+        cost_estimate=pl.CostEstimate(flops=0, bytes_accessed=2 * (gate_up.size + down.size), transcendentals=0),
+        name="stage",
+    )(in_hbm(gate_up), in_hbm(down))
+    return staged[:count], staged[count:]
+
+
+def experts_body(per_pair, local_experts, first_expert, ids, gates, *refs):
     pairs, top, tokens = ids.shape
+    gate_up, down, refs = refs[:local_experts], refs[local_experts : 2 * local_experts], refs[2 * local_experts :]
     sources = refs[: pairs * per_pair]
-    same_core, other_core, picked, produced, hidden, chosen, slot_gates, gate_up, down, sems = refs[pairs * per_pair :]
-    local_experts, features, _ = gate_up.shape
-    units = down.shape[1]
-    copies = [
-        (
-            pltpu.make_async_copy(gate_up_hbm.at[expert], gate_up.at[expert], sems.at[0, expert]),
-            pltpu.make_async_copy(down_hbm.at[expert], down.at[expert], sems.at[1, expert]),
-        )
-        for expert in range(local_experts)
-    ]
-    for first, second in copies[:2]:
-        first.start()
-        second.start()
+    same_core, other_core, picked, produced, hidden, chosen, slot_gates = refs[pairs * per_pair :]
+    features, units = gate_up[0].shape[0], down[0].shape[0]
     slots = 2 * CAP
     earlier = lax.broadcasted_iota(jnp.int32, (tokens, tokens), 0)
     later = lax.broadcasted_iota(jnp.int32, (tokens, tokens), 1)
@@ -352,25 +369,19 @@
                 ]
     chunk = slots * min(pairs, 4)
     for expert in range(local_experts):
-        copies[expert][0].wait()
-        for later_copy in copies[expert + 2 : expert + 3]:
-            later_copy[0].start()
-            later_copy[1].start()
         for low in range(0, pairs * slots, chunk):
             rows = picked[expert, low : low + chunk, :]
             gate_rows = slot_gates[expert, low : low + chunk, :]
             for column in range(0, units, 256):
-                gate = jnp.dot(rows, gate_up[expert, :, column : column + 256], preferred_element_type=F32)
+                gate = jnp.dot(rows, gate_up[expert][:, column : column + 256], preferred_element_type=F32)
                 up = jnp.dot(
-                    rows, gate_up[expert, :, units + column : units + column + 256], preferred_element_type=F32
+                    rows, gate_up[expert][:, units + column : units + column + 256], preferred_element_type=F32
                 )
                 active = gate / (1.0 + jnp.exp(-gate)) * up * gate_rows
                 hidden[low : low + chunk, column : column + 256] = active.astype(BF16)
-            if low == 0:
-                copies[expert][1].wait()
             for column in range(0, features, 512):
                 result = jnp.dot(
-                    hidden[low : low + chunk, :], down[expert, :, column : column + 512], preferred_element_type=F32
+                    hidden[low : low + chunk, :], down[expert][:, column : column + 512], preferred_element_type=F32
                 ).astype(BF16)
                 for inner in range(chunk // slots):
                     produced[
@@ -386,15 +397,18 @@
             other_core[pair, :, column : column + 512] = mixture[tokens // 2 :]
 
 
-def experts(first_expert, ids, gates, gate_up, down, sources, limit):
+def experts(first_expert, ids, gates, gate_up, down, sources, limit, pin=False):
     pairs, top, tokens = ids.shape
-    local_experts, features, _ = gate_up.shape
-    units = down.shape[1]
+    local_experts, (features, _) = len(gate_up), gate_up[0].shape
+    units = down[0].shape[0]
     slots = 2 * CAP
+    matrices = [*gate_up, *down]
+    if pin:
+        matrices = [in_vmem(part) for part in matrices]
     return pl.pallas_call(
-        lambda *refs: experts_body(len(sources) // pairs, *refs),
+        lambda *refs: experts_body(len(sources) // pairs, local_experts, *refs),
         out_shape=(everywhere((pairs, tokens // 2, features), BF16),) * 2,
-        in_specs=[IN_SMEM] + [IN_VMEM] * 2 + [IN_PLACE] * 2 + [IN_VMEM] * len(sources),
+        in_specs=[IN_SMEM] + [IN_VMEM] * (2 + 2 * local_experts + len(sources)),
         out_specs=(IN_VMEM,) * 2,
         scratch_shapes=[
             pltpu.VMEM((local_experts, pairs * slots, features), BF16),
@@ -402,13 +416,13 @@
             pltpu.VMEM((pairs * slots, units), BF16),
             pltpu.VMEM((pairs, local_experts * slots, tokens), BF16),
             pltpu.VMEM((local_experts, pairs * slots, 1), F32),
-            pltpu.VMEM(gate_up.shape, BF16),
-            pltpu.VMEM(down.shape, BF16),
-            pltpu.SemaphoreType.DMA((2, local_experts)),
         ],
         compiler_params=pltpu.CompilerParams(vmem_limit_bytes=limit),
+        cost_estimate=pl.CostEstimate(
+            flops=12 * local_experts * pairs * slots * features * units, bytes_accessed=16 * 2**20, transcendentals=0
+        ),
         name="experts",
-    )(first_expert, ids, gates, in_hbm(gate_up), in_hbm(down), *sources)
+    )(first_expert, ids, gates, *matrices, *sources)
 
 
 def add_rows(left, right):
@@ -426,13 +440,13 @@
     flat = (prompt_count * rows_here, features)
     send, send_prompts, mine, prompts = pack(
         (me % 2).reshape(1), tree_queries, tree_keys, tree_values, prompt_keys.reshape(flat),
-        prompt_values.reshape(flat), expert_ids.astype(F32).T, gate_weights.T,
+        prompt_values.reshape(flat), expert_ids.T, gate_weights.T,
     )
     x_mine, y_mine = flip(prompts, 2, 8), flip(prompts, 4, 8)
     theirs = flip(send_prompts, 1, 8)
     x_theirs, y_theirs = flip(theirs, 2, 8), flip(theirs, 4, 8)
     far_a, far_b = flip(x_mine, 4, 8), flip(y_theirs, 2, 8)
-    weights, pieces, order, last = fetch_projection(out_proj, prompts, (x_mine, y_mine, x_theirs, y_theirs, far_a, far_b))
+    weights, pieces, order, up, down_rows = fetch_projection(out_proj, prompts, (x_mine, y_mine, x_theirs, y_theirs, far_a, far_b))
     got = flip(send, 1, 8)
     small = jnp.concatenate(
         [tree_parents, jnp.broadcast_to(request_prompt[:, None], tree_parents.shape)], axis=0
@@ -446,33 +460,42 @@
     chip_parents = jnp.where(chip_parents < 0, -1, chip_parents + first_node).reshape(-1, 1)
     attended, cache, ids, gates = chip_attention(
         (me.reshape(1), request_prompt, sibling, prompt_lengths), columns, chip_parents, accepted,
-        tree_keys, tree_values, (mine, got, prompts, theirs, x_mine, x_theirs, y_mine, y_theirs, far_a, far_b),
-    )
-    last = after(last, attended, *weights[3:5])
-    edge = last.shape[0] // 2
-    weights += [last, flip(last[:edge], 2, 8), flip(last[edge:], 4, 8)]
-    mine, other = chip_project(order, attended, weights, pieces)
-    residual, normed = norm(hidden_in, mine, flip(other, 1, 8), gain)
-
-    across = flip(normed, 6, 8)
+        tree_keys, tree_values, mine, prompts, (got, theirs, x_mine, x_theirs, y_mine, y_theirs, far_a, far_b),
+    )
+    up, down_rows = after((up, down_rows), attended)
+    edge = up.shape[0] // 2
+    last_first, last_second = [
+        jnp.where(lax.axis_index("rep") >= 2, up[rows], down_rows[rows]) for rows in (slice(0, edge), slice(edge, None))
+    ]
+    weights += [last_first, last_second, flip(last_first, 2, 8), flip(last_second, 4, 8)]
+    other = flip(chip_project(order, attended, weights, pieces, tok_rows, BF16), 1, 8)
+    mine = chip_project(order, attended, weights, pieces, 0, F32)
+    residual, normed = norm(hidden_in, mine, other, gain)
+
+    across, from_x, from_y = flip(normed, 6, 8), flip(normed, 2, 8), flip(normed, 4, 8)
     sibling_rows = flip(normed, 1, 8)
     first_expert = (me * gate_up.shape[0]).reshape(1)
-
-    def run(low, high, sources, *done):
-        limit = (34 + 8 * (high - low)) * 2**20
-        return experts(first_expert, after(ids[low:high], done), gates[low:high], gate_up, down, sources, limit)
-
-    near_same, near_other = run(0, 1, [normed, sibling_rows])
-    sent, across = after((normed, across), near_same)
-    from_x, from_y = flip(sent, 2, 8), flip(sent, 4, 8)
-    far_same, far_other = run(3, 4, [across, flip(across, 1, 8)])
-    far = add_rows(far_same, flip(after(far_other, from_x, from_y), 1, 8))
-    back = flip(far[0], 6, 8)
-    from_x, from_y = after((from_x, from_y), far)
+    gate_up, down = stage(*after((gate_up, down), normed))
+
+    def run(low, high, sources, megabytes, *done):
+        return experts(
+            first_expert, after(ids[low:high], done), gates[low:high], gate_up, down, sources, megabytes * 2**20, True
+        )
+
+    near_same, near_other = run(0, 1, [normed, sibling_rows], 12)
+    across = after(across, near_same)
+    far_same, far_other = run(3, 4, [across, flip(across, 1, 8)], 12)
+    far = add_rows(far_same, flip(far_other, 1, 8))[0]
+
+    half = tok_rows // 2
+    far_first, far_second = flip(far[:half], 2, 8), flip(far[half:], 4, 8)
     beside = [from_x, flip(from_x, 1, 8), from_y, flip(from_y, 1, 8)]
-    side_same, side_other = run(1, 3, beside)
-    side = add_rows(side_same, flip(after(side_other, back), 1, 8))
-    terms = [near_same[0], flip(near_other, 1, 8)[0], back, flip(side[0], 2, 8), flip(side[1], 4, 8)]
+    side_same, side_other = run(1, 3, beside, 16, far)
+    side = [part.astype(F32) for part in (side_same, flip(after(side_other, far_first, far_second), 1, 8))]
+    side = side[0] + side[1]
+    to_x = jnp.concatenate([side[0, :half], side[0, half:] + far_second.astype(F32)], axis=0).astype(BF16)
+    to_y = jnp.concatenate([side[1, :half] + far_first.astype(F32), side[1, half:]], axis=0).astype(BF16)
+    terms = [near_same[0], flip(near_other, 1, 8)[0], flip(to_x, 2, 8), flip(to_y, 4, 8)]
     return residual, terms, cache
 
 
@@ -501,7 +524,8 @@
     everyone = lax.all_gather(normed, "ep", axis=0, tiled=True)
     sources = [everyone[i * 2 * tok_rows : (i + 1) * 2 * tok_rows] for i in range(ep_size // 2)]
     same_core, other_core = experts(
-        (me * gate_up.shape[0]).reshape(1), routing[:, :top], routing[:, top:], gate_up, down, sources, VMEM_LIMIT
+        (me * gate_up.shape[0]).reshape(1), routing[:, :top], routing[:, top:], list(gate_up), list(down), sources,
+        VMEM_LIMIT
     )
     shares = jnp.stack([same_core, other_core], axis=1).reshape(ep_size, tok_rows, features)
     shares = lax.all_to_all(shares, "ep", split_axis=0, concat_axis=0, tiled=True)

time: 142 us -> 130 us (0.915)
  Pallas kernels: 49.8 us -> 42.9 us
  waiting for transfers between devices: 53.5 us -> 50.7 us
    ppermute x27 -> x28, waiting for transfers between devices: 46.9 us -> 39.5 us  [flip(): return lax.ppermute(value, 'ep', [(i, i ^ bits) for i in range(size)])]
    pallas_call x4 -> x6, Pallas kernels: 37.2 us -> 31.4 us  [the longest x3 18.7 us: experts(): pl.pallas_call(lambda *refs: experts_body(len(sources) // pairs, local_ex...]
    ppermute x2, waiting for transfers between devices: 5.24 us -> 8.02 us  [shifted(): return lax.ppermute(value, 'rep', [(i, (i + by) % 4) for i in range(4)])]
    ppermute x1, waiting for transfers between devices: 1.41 us -> 3.17 us  [fetch_projection(): down = lax.ppermute(came3, 'rep', [(2, 1), (1, 0)])]
    ppermute x27 -> x28, starting transfers between devices: 20.3 us -> 21.3 us  [flip(): return lax.ppermute(value, 'ep', [(i, i ^ bits) for i in range(size)])]
    unnamed x30 -> x34, local copies, waits for them, and re-layouts: 2.86 us -> 1.89 us
  transfers between devices with their start and end apart: 31 -> 32, of which waited for: 22 -> 11; matrix products, arithmetic and copies ran while one was open for 2% -> 3% of each run, Pallas kernels for 31% -> 29%
where the time goes in v3:
time: 130 us
  waiting for transfers between devices  50.7 us (39%)
  Pallas kernels  42.9 us (33%)
  starting transfers between devices  27.3 us (21%)
  local copies, waits for them, and re-layouts  4.53 us (3%)
  other arithmetic  3.05 us (2%)
    ppermute x28, waiting for transfers between devices, flip(): return lax.ppermute(value, 'ep', [(i, i ^ bits) for i in range(size)])  39.5 us
    ppermute x28, starting transfers between devices, flip(): return lax.ppermute(value, 'ep', [(i, i ^ bits) for i in range(size)])  21.3 us
    pallas_call x3, Pallas kernels, experts(): pl.pallas_call(lambda *refs: experts_body(len(sources) // pairs, local_ex...  18.7 us
    pallas_call x1, Pallas kernels, chip_attention(): pl.pallas_call(chip_attention_body, out_shape=(everywhere((heads, 2 * row...  8.97 us
    pallas_call x1, Pallas kernels, stage(): pl.pallas_call(stage_body, out_shape=[pltpu.VMEM(gate_up.shape[1:], BF16)...  8.32 us
    ppermute x2, waiting for transfers between devices, shifted(): return lax.ppermute(value, 'rep', [(i, (i + by) % 4) for i in range(4)])  8.02 us
    pallas_call x2, Pallas kernels, chip_project(): pl.pallas_call(lambda *refs: chip_project_body(pieces, low_row, *refs), o...  4.4 us
    ppermute x2, starting transfers between devices, shifted(): return lax.ppermute(value, 'rep', [(i, (i + by) % 4) for i in range(4)])  4.05 us
  transfers between devices with their start and end apart: 32, of which 11 were waited for; matrix products, arithmetic and copies ran while one was open for 3% of the time, Pallas kernels for 29%

profile of v3, /device:TPU:0, one launch (start us, length us, event | category | flops | bytes accessed | tf_op | source)
XLA Modules:
  0.0 129.7 jit_solution(12663595888941932605)
XLA Ops:
  0.7 2.1 %pack.1 = (bf16[384,1024]{1,0:T(8,128)(2,1)S(1)}, bf16[208,1024]{1,0:T(8,128)(2,1)S(1)}, bf16[384,1024]{1,0:T(8,128)(2,1)S(1)}, bf16[208,1024]{1,0:T(8,128)(2,1)S(1)}) custom-call(s32[1]{0:T(128)} %bitcast.9.core, bf16[128,2048]{1,0:T(8,128)(2,1)} %refs_0_.2, bf16[128,2048]{1,0:T(8,128)(2,1)} %refs_0_.3, bf16[128,2048]{1,0:T(8,128)(2,1)} %refs_1_.3, ...), custom_call_target="tpu_custom_call" | custom-call | tf_op jit(solution)/shard_map/pack/pallas_call | solution.py:88
  2.8 0.9 copy-done.4
  3.8 2.9 %collective-permute-start.3 = (bf16[208,1024]{1,0:T(8,128)(2,1)S(1)}, bf16[208,1024]{1,0:T(8,128)(2,1)}, u32[]{:S(2)}, u32[]{:S(2)}) collective-permute-start(bf16[208,1024]{1,0:T(8,128)(2,1)S(1)} %get-tuple-element.36.prompts_here), channel_id=1, source_target_pairs={{0,2},{1,3},{2,0},{3,1},{4,6},{5,7},{6,4},{7,5},{8,10},{9,11},{10,... | collective-permute-start | bytes 1277960 | tf_op jit(solution)/shard_map/ppermute | solution.py:23
  6.7 1.5 %collective-permute-start.5 = (bf16[208,1024]{1,0:T(8,128)(2,1)S(1)}, bf16[208,1024]{1,0:T(8,128)(2,1)}, u32[]{:S(2)}, u32[]{:S(2)}) collective-permute-start(bf16[208,1024]{1,0:T(8,128)(2,1)S(1)} %get-tuple-element.36.prompts_here), channel_id=1, source_target_pairs={{0,4},{1,5},{2,6},{3,7},{4,0},{5,1},{6,2},{7,3},{8,12},{9,13},{10,... | collective-permute-start | bytes 1277960 | tf_op jit(solution)/shard_map/ppermute | solution.py:23
  8.4 0.5 collective-permute-start
  8.9 0.8 constant_dynamic-slice_fusion
  9.7 1.6 %collective-permute-start.9 = (bf16[128,2048]{1,0:T(8,128)(2,1)}, bf16[128,2048]{1,0:T(8,128)(2,1)}, u32[]{:S(2)}, u32[]{:S(2)}) collective-permute-start(bf16[128,2048]{1,0:T(8,128)(2,1)} %constant_dynamic-slice_fusion), channel_id=1, source_target_pairs={{0,8},{8,16},{16,24},{24,0},{1,9},{9,17},{17,25},{25,1},{2,10},{10... | collective-permute-start | bytes 1572872 | tf_op jit(solution)/shard_map/ppermute | solution.py:239
  11.3 0.5 collective-permute-start.6
  12.0 2.5 %collective-permute-start.10 = (bf16[128,2048]{1,0:T(8,128)(2,1)}, bf16[128,2048]{1,0:T(8,128)(2,1)}, u32[]{:S(2)}, u32[]{:S(2)}) collective-permute-start(bf16[128,2048]{1,0:T(8,128)(2,1)} %constant_dynamic-slice_fusion), channel_id=1, source_target_pairs={{0,24},{8,0},{16,8},{24,16},{1,25},{9,1},{17,9},{25,17},{2,26},{10... | collective-permute-start | bytes 1572872 | tf_op jit(solution)/shard_map/ppermute | solution.py:239
  14.5 2.1 %collective-permute-done.3.refs_4_ = bf16[208,1024]{1,0:T(8,128)(2,1)} collective-permute-done((bf16[208,1024]{1,0:T(8,128)(2,1)S(1)}, bf16[208,1024]{1,0:T(8,128)(2,1)}, u32[]{:S(2)}, u32[]{:S(2)}) %collective-permute-start.3) | collective-permute-done | bytes 426016 | tf_op jit(solution)/shard_map/ppermute | solution.py:23
  16.6 1.7 %collective-permute-start.4 = (bf16[208,1024]{1,0:T(8,128)(2,1)}, bf16[208,1024]{1,0:T(8,128)(2,1)}, u32[]{:S(2)}, u32[]{:S(2)}) collective-permute-start(bf16[208,1024]{1,0:T(8,128)(2,1)} %collective-permute-done.2.refs_3_), channel_id=1, source_target_pairs={{0,2},{1,3},{2,0},{3,1},{4,6},{5,7},{6,4},{7,5},{8,10},{9,11},{10,... | collective-permute-start | bytes 1277960 | tf_op jit(solution)/shard_map/ppermute | solution.py:23
  18.4 1.2 collective-permute-done.5.refs_6_
  19.6 1.5 %collective-permute-start.7 = (bf16[208,1024]{1,0:T(8,128)(2,1)}, bf16[208,1024]{1,0:T(8,128)(2,1)}, u32[]{:S(2)}, u32[]{:S(2)}) collective-permute-start(bf16[208,1024]{1,0:T(8,128)(2,1)} %collective-permute-done.3.refs_4_), channel_id=1, source_target_pairs={{0,4},{1,5},{2,6},{3,7},{4,0},{5,1},{6,2},{7,3},{8,12},{9,13},{10,... | collective-permute-start | bytes 1277960 | tf_op jit(solution)/shard_map/ppermute | solution.py:23
  21.1 7.5 %collective-permute-done.6.refs_7_ = bf16[208,1024]{1,0:T(8,128)(2,1)S(1)} collective-permute-done((bf16[208,1024]{1,0:T(8,128)(2,1)}, bf16[208,1024]{1,0:T(8,128)(2,1)S(1)}, u32[]{:S(2)}, u32[]{:S(2)}) %collective-permute-start.6) | collective-permute-done | bytes 426016 | tf_op jit(solution)/shard_map/ppermute | solution.py:23
  28.9 8.0 %collective-permute-done.10 = bf16[128,2048]{1,0:T(8,128)(2,1)} collective-permute-done((bf16[128,2048]{1,0:T(8,128)(2,1)}, bf16[128,2048]{1,0:T(8,128)(2,1)}, u32[]{:S(2)}, u32[]{:S(2)}) %collective-permute-start.10) | collective-permute-done | bytes 524320 | tf_op jit(solution)/shard_map/ppermute | solution.py:239
  37.0 0.7 collective-permute-start.13
  37.7 1.3 collective-permute-start.14
  39.0 1.3 fusion.8
  40.4 0.6 collective-permute-start.11
  41.0 0.6 collective-permute-start.12
  41.6 0.9 copy-done.13
  42.5 9.0 %attention.1 = (bf16[8,256,128]{2,1,0:T(8,128)(2,1)S(1)}, bf16[32,4096]{1,0:T(8,128)(2,1)}, f32[4,8,256]{2,1,0:T(8,128)S(1)}, f32[4,8,256]{2,1,0:T(8,128)S(1)}) custom-call(s32[1]{0:T(128)} %bitcast.8.me, s32[2]{0:T(128)S(1)} %copy-done.10, s32[4,64]{1,0:T(4,128)S(1)} %collective-permute-done.sibling, s32[4]{0:T(128)S(1)} %copy-done.11, ...), custom_call_target="tpu_custom_call" | custom-call | tf_op jit(solution)/shard_map/attention/pallas_call | solution.py:185
  51.5 3.2 %collective-permute-done.14 = bf16[128,2048]{1,0:T(8,128)(2,1)S(1)} collective-permute-done((bf16[128,2048]{1,0:T(8,128)(2,1)}, bf16[128,2048]{1,0:T(8,128)(2,1)S(1)}, u32[]{:S(2)}, u32[]{:S(2)}) %collective-permute-start.14) | collective-permute-done | bytes 524320 | tf_op jit(solution)/shard_map/ppermute | solution.py:243
  54.7 0.8 slice_select_fusion
  55.5 0.5 collective-permute-start.15
  56.0 0.5 collective-permute-start.16
  56.7 7.0 %collective-permute-done.15.refs_9_ = bf16[64,2048]{1,0:T(8,128)(2,1)} collective-permute-done((bf16[64,2048]{1,0:T(8,128)(2,1)}, bf16[64,2048]{1,0:T(8,128)(2,1)}, u32[]{:S(2)}, u32[]{:S(2)}) %collective-permute-start.15) | collective-permute-done | bytes 262176 | tf_op jit(solution)/shard_map/ppermute | solution.py:23
  63.7 2.2 %project.3 = bf16[128,2048]{1,0:T(8,128)(2,1)S(1)} custom-call(s32[8]{0:T(128)S(1)} %stack.41.refs_0_, bf16[8,256,128]{2,1,0:T(8,128)(2,1)S(1)} %copy-done.3, bf16[256,2048]{1,0:T(8,128)(2,1)S(1)} %constant_dynamic-slice_fusion.1.refs_2_, bf16[128,2048]{1,0:T(8,128)(2,1)S(1)} %pad_maximum_fusion.refs_3_, bf16[128,2048]{1,0:T(8,128)(2,1)S(1)} %pad_maximum_fusion.1.refs_4_, ...), custom_call_target="tpu_custom_call" | custom-call | tf_op jit(solution)/shard_map/project/pallas_call | solution.py:278
  66.0 2.2 %project.2.mine = f32[128,2048]{1,0:T(8,128)S(1)} custom-call(s32[8]{0:T(128)S(1)} %stack.41.refs_0_, bf16[8,256,128]{2,1,0:T(8,128)(2,1)S(1)} %copy-done.3, bf16[256,2048]{1,0:T(8,128)(2,1)S(1)} %constant_dynamic-slice_fusion.1.refs_2_, bf16[128,2048]{1,0:T(8,128)(2,1)S(1)} %pad_maximum_fusion.refs_3_, bf16[128,2048]{1,0:T(8,128)(2,1)S(1)} %pad_maximum_fusion.1.refs_4_, ...), custom_call_target="tpu_custom_call" | custom-call | tf_op jit(solution)/shard_map/project/pallas_call | solution.py:278
  68.3 0.4 norm.1
  68.7 0.5 collective-permute-start.18
  69.2 1.4 %collective-permute-start.24 = (bf16[128,2048]{1,0:T(8,128)(2,1)S(1)}, bf16[128,2048]{1,0:T(8,128)(2,1)S(1)}, u32[]{:S(2)}, u32[]{:S(2)}) collective-permute-start(bf16[128,2048]{1,0:T(8,128)(2,1)S(1)} %get-tuple-element.48.refs_11_), channel_id=1, source_target_pairs={{0,6},{1,7},{2,4},{3,5},{4,2},{5,3},{6,0},{7,1},{8,14},{9,15},{10,... | collective-permute-start | bytes 1572872 | tf_op jit(solution)/shard_map/ppermute | solution.py:23
  70.7 8.3 %stage.1 = (bf16[2048,1024]{1,0:T(8,128)(2,1)S(1)}, bf16[2048,1024]{1,0:T(8,128)(2,1)S(1)}, bf16[2048,1024]{1,0:T(8,128)(2,1)S(1)}, bf16[2048,1024]{1,0:T(8,128)...) custom-call(bf16[4,2048,1024]{2,1,0:T(8,128)(2,1)} %gate_up, ...), custom_call_target="tpu_custom_call" | custom-call | bytes 25165824 | tf_op jit(solution)/shard_map/stage/pallas_call | solution.py:322
  79.0 5.9 %experts.3 = (bf16[1,128,2048]{2,1,0:T(8,128)(2,1)S(1)}, bf16[1,128,2048]{2,1,0:T(8,128)(2,1)S(1)}) custom-call(s32[1]{0:T(128)} %bitcast.15.refs_0_, f32[1,8,256]{2,1,0:T(8,128)S(1)} %get-tuple-element.84.refs_1_, f32[1,8,256]{2,1,0:T(8,128)S(1)} %get-tuple-element.82.refs_2_, bf16[2048,1024]{1,0:T(8,128)(2,1)S(1)} %get-tuple-element.51.refs_3_, ...), custom_call_target="tpu_custom_call" | custom-call | flops 4026531840 | bytes 16777216 | tf_op jit(solution)/shard_map/experts/pallas_call | solution.py:408
  85.0 0.8 collective-permute-start.20
  85.8 1.5 %collective-permute-start.22 = (bf16[128,2048]{1,0:T(8,128)(2,1)S(1)}, bf16[128,2048]{1,0:T(8,128)(2,1)S(1)}, u32[]{:S(2)}, u32[]{:S(2)}) collective-permute-start(bf16[128,2048]{1,0:T(8,128)(2,1)S(1)} %get-tuple-element.48.refs_11_), channel_id=1, source_target_pairs={{0,4},{1,5},{2,6},{3,7},{4,0},{5,1},{6,2},{7,3},{8,12},{9,13},{10,... | collective-permute-start | bytes 1572872 | tf_op jit(solution)/shard_map/ppermute | solution.py:23
  87.3 5.9 %experts.5 = (bf16[1,128,2048]{2,1,0:T(8,128)(2,1)S(1)}, bf16[1,128,2048]{2,1,0:T(8,128)(2,1)S(1)}) custom-call(s32[1]{0:T(128)} %bitcast.15.refs_0_, f32[1,8,256]{2,1,0:T(8,128)S(1)} %get-tuple-element.85.refs_1_, f32[1,8,256]{2,1,0:T(8,128)S(1)} %get-tuple-element.83.refs_2_, bf16[2048,1024]{1,0:T(8,128)(2,1)S(1)} %get-tuple-element.51.refs_3_, ...), custom_call_target="tpu_custom_call" | custom-call | flops 4026531840 | bytes 16777216 | tf_op jit(solution)/shard_map/experts/pallas_call | solution.py:408
  93.3 6.0 %collective-permute-done.20.refs_11_ = bf16[128,2048]{1,0:T(8,128)(2,1)S(1)} collective-permute-done((bf16[128,2048]{1,0:T(8,128)(2,1)S(1)}, bf16[128,2048]{1,0:T(8,128)(2,1)S(1)}, u32[]{:S(2)}, u32[]{:S(2)}) %collective-permute-start.20) | collective-permute-done | bytes 524320 | tf_op jit(solution)/shard_map/ppermute | solution.py:23
  100.0 1.3 %collective-permute-start.27 = (bf16[64,2048]{1,0:T(8,128)(2,1)S(1)}, bf16[64,2048]{1,0:T(8,128)(2,1)S(1)}, u32[]{:S(2)}, u32[]{:S(2)}) collective-permute-start(bf16[64,2048]{1,0:T(8,128)(2,1)S(1)} %get-tuple-element.77), channel_id=1, source_target_pairs={{0,2},{1,3},{2,0},{3,1},{4,6},{5,7},{6,4},{7,5},{8,10},{9,11},{10,... | collective-permute-start | bytes 786440 | tf_op jit(solution)/shard_map/ppermute | solution.py:23
  101.3 1.5 %collective-permute-start.28 = (bf16[64,2048]{1,0:T(8,128)(2,1)S(1)}, bf16[64,2048]{1,0:T(8,128)(2,1)S(1)}, u32[]{:S(2)}, u32[]{:S(2)}) collective-permute-start(bf16[64,2048]{1,0:T(8,128)(2,1)S(1)} %get-tuple-element.76), channel_id=1, source_target_pairs={{0,4},{1,5},{2,6},{3,7},{4,0},{5,1},{6,2},{7,3},{8,12},{9,13},{10,... | collective-permute-start | bytes 786440 | tf_op jit(solution)/shard_map/ppermute | solution.py:23
  102.8 6.9 %experts.4 = (bf16[2,128,2048]{2,1,0:T(8,128)(2,1)S(1)}, bf16[2,128,2048]{2,1,0:T(8,128)(2,1)S(1)}) custom-call(s32[1]{0:T(128)} %bitcast.15.refs_0_, f32[2,8,256]{2,1,0:T(8,128)S(1)} %slice.82.refs_1_, f32[2,8,256]{2,1,0:T(8,128)S(1)} %slice.83.refs_2_, bf16[2048,1024]{1,0:T(8,128)(2,1)S(1)} %get-tuple-element.51.refs_3_, ...), custom_call_target="tpu_custom_call" | custom-call | flops 8053063680 | bytes 16777216 | tf_op jit(solution)/shard_map/experts/pallas_call | solution.py:408
  109.8 0.5 collective-permute-start.19
  110.3 2.1 %collective-permute-done.29 = bf16[2,128,2048]{2,1,0:T(8,128)(2,1)S(1)} collective-permute-done((bf16[2,128,2048]{2,1,0:T(8,128)(2,1)S(1)}, bf16[2,128,2048]{2,1,0:T(8,128)(2,1)S(1)}, u32[]{:S(2)}, u32[]{:S(2)}) %collective-permute-start.29) | collective-permute-done | bytes 1048608 | tf_op jit(solution)/shard_map/ppermute | solution.py:23
  113.1 1.5 %collective-permute-start.31 = (bf16[128,2048]{1,0:T(8,128)(2,1)S(1)}, bf16[128,2048]{1,0:T(8,128)(2,1)S(1)}, u32[]{:S(2)}, u32[]{:S(2)}) collective-permute-start(bf16[128,2048]{1,0:T(8,128)(2,1)S(1)} %pad_maximum_fusion.3), channel_id=1, source_target_pairs={{0,4},{1,5},{2,6},{3,7},{4,0},{5,1},{6,2},{7,3},{8,12},{9,13},{10,... | collective-permute-start | bytes 1572872 | tf_op jit(solution)/shard_map/ppermute | solution.py:23
  114.7 0.6 collective-permute-start.30
  115.3 11.9 %collective-permute-done.31 = bf16[128,2048]{1,0:T(8,128)(2,1)S(1)} collective-permute-done((bf16[128,2048]{1,0:T(8,128)(2,1)S(1)}, bf16[128,2048]{1,0:T(8,128)(2,1)S(1)}, u32[]{:S(2)}, u32[]{:S(2)}) %collective-permute-start.31) | collective-permute-done | bytes 524320 | tf_op jit(solution)/shard_map/ppermute | solution.py:23
  127.2 1.3 collective-permute-done.30
  128.5 1.2 fusion.2
  (90 shorter events, 2.7 us)
Async XLA Ops:
  0.6 8.3 %copy-start = (bf16[512,2048]{1,0:T(8,128)(2,1)S(1)}, bf16[512,2048]{1,0:T(8,128)(2,1)}, u32[]{:S(2)}) copy-start(bf16[512,2048]{1,0:T(8,128)(2,1)} %param.26) | copy-start | bytes 6291460
  0.7 7.6 %copy-start.10 = (s32[2]{0:T(128)S(1)}, s32[2]{0:T(128)}, u32[]{:S(2)}) copy-start(s32[2]{0:T(128)} %my_prompts.1) | copy-start | bytes 28
  0.7 7.6 %copy-start.15 = (s32[2,64]{1,0:T(2,128)S(1)}, s32[2,64]{1,0:T(2,128)}, u32[]{:S(2)}) copy-start(s32[2,64]{1,0:T(2,128)} %param.20) | copy-start | bytes 1540
  0.7 11.1 %copy-start.16 = (s32[2,16]{1,0:T(2,128)S(1)}, s32[2,16]{1,0:T(2,128)}, u32[]{:S(2)}) copy-start(s32[2,16]{1,0:T(2,128)} %param.21) | copy-start | bytes 388
  2.8 0.9 copy-start.4
  3.8 4.5 %copy-start.12 = (bf16[384,1024]{1,0:T(8,128)(2,1)}, bf16[384,1024]{1,0:T(8,128)(2,1)S(1)}, u32[]{:S(2)}) copy-start(bf16[384,1024]{1,0:T(8,128)(2,1)S(1)} %get-tuple-element.37) | copy-start | bytes 2359300
  3.8 36.5 %copy-start.7 = (bf16[208,1024]{1,0:T(8,128)(2,1)}, bf16[208,1024]{1,0:T(8,128)(2,1)S(1)}, u32[]{:S(2)}) copy-start(bf16[208,1024]{1,0:T(8,128)(2,1)S(1)} %get-tuple-element.36.prompts_here) | copy-start | bytes 1277956
  3.8 12.9 %collective-permute-start.3 = (bf16[208,1024]{1,0:T(8,128)(2,1)S(1)}, bf16[208,1024]{1,0:T(8,128)(2,1)}, u32[]{:S(2)}, u32[]{:S(2)}) collective-permute-start(bf16[208,1024]{1,0:T(8,128)(2,1)S(1)} %get-tuple-element.36.prompts_here), channel_id=1, source_target_pairs={{0,2},{1,3},{2,0},{3,1},{4,6},{5,7},{6,4},{7,5},{8,10},{9,11},{10,... | collective-permute-start | bytes 1277960 | tf_op jit(solution)/shard_map/ppermute | solution.py:23
  6.7 12.8 %collective-permute-start.5 = (bf16[208,1024]{1,0:T(8,128)(2,1)S(1)}, bf16[208,1024]{1,0:T(8,128)(2,1)}, u32[]{:S(2)}, u32[]{:S(2)}) collective-permute-start(bf16[208,1024]{1,0:T(8,128)(2,1)S(1)} %get-tuple-element.36.prompts_here), channel_id=1, source_target_pairs={{0,4},{1,5},{2,6},{3,7},{4,0},{5,1},{6,2},{7,3},{8,12},{9,13},{10,... | collective-permute-start | bytes 1277960 | tf_op jit(solution)/shard_map/ppermute | solution.py:23
  8.2 3.1 %collective-permute-start.2 = (bf16[208,1024]{1,0:T(8,128)(2,1)S(1)}, bf16[208,1024]{1,0:T(8,128)(2,1)}, u32[]{:S(2)}, u32[]{:S(2)}) collective-permute-start(bf16[208,1024]{1,0:T(8,128)(2,1)S(1)} %get-tuple-element.38), channel_id=1, source_target_pairs={{0,1},{1,0},{2,3},{3,2},{4,5},{5,4},{6,7},{7,6},{8,9},{9,8},{10,11... | collective-permute-start | bytes 1277960 | tf_op jit(solution)/shard_map/ppermute | solution.py:23
  8.4 3.6 %collective-permute-start = (s32[4,64]{1,0:T(4,128)S(1)}, s32[4,64]{1,0:T(4,128)S(1)}, u32[]{:S(2)}, u32[]{:S(2)}) collective-permute-start(s32[4,64]{1,0:T(4,128)S(1)} %pad_add_fusion.2), channel_id=1, source_target_pairs={{0,1},{1,0},{2,3},{3,2},{4,5},{5,4},{6,7},{7,6},{8,9},{9,8},{10,11... | collective-permute-start | bytes 3080 | tf_op jit(solution)/shard_map/ppermute | solution.py:23
  9.7 19.1 %collective-permute-start.9 = (bf16[128,2048]{1,0:T(8,128)(2,1)}, bf16[128,2048]{1,0:T(8,128)(2,1)}, u32[]{:S(2)}, u32[]{:S(2)}) collective-permute-start(bf16[128,2048]{1,0:T(8,128)(2,1)} %constant_dynamic-slice_fusion), channel_id=1, source_target_pairs={{0,8},{8,16},{16,24},{24,0},{1,9},{9,17},{17,25},{25,1},{2,10},{10... | collective-permute-start | bytes 1572872 | tf_op jit(solution)/shard_map/ppermute | solution.py:239
  11.3 17.3 %collective-permute-start.6 = (bf16[208,1024]{1,0:T(8,128)(2,1)}, bf16[208,1024]{1,0:T(8,128)(2,1)S(1)}, u32[]{:S(2)}, u32[]{:S(2)}) collective-permute-start(bf16[208,1024]{1,0:T(8,128)(2,1)} %collective-permute-done.2.refs_3_), channel_id=1, source_target_pairs={{0,4},{1,5},{2,6},{3,7},{4,0},{5,1},{6,2},{7,3},{8,12},{9,13},{10,... | collective-permute-start | bytes 1277960 | tf_op jit(solution)/shard_map/ppermute | solution.py:23
  12.0 24.9 %collective-permute-start.10 = (bf16[128,2048]{1,0:T(8,128)(2,1)}, bf16[128,2048]{1,0:T(8,128)(2,1)}, u32[]{:S(2)}, u32[]{:S(2)}) collective-permute-start(bf16[128,2048]{1,0:T(8,128)(2,1)} %constant_dynamic-slice_fusion), channel_id=1, source_target_pairs={{0,24},{8,0},{16,8},{24,16},{1,25},{9,1},{17,9},{25,17},{2,26},{10... | collective-permute-start | bytes 1572872 | tf_op jit(solution)/shard_map/ppermute | solution.py:239
  16.6 21.0 %collective-permute-start.4 = (bf16[208,1024]{1,0:T(8,128)(2,1)}, bf16[208,1024]{1,0:T(8,128)(2,1)}, u32[]{:S(2)}, u32[]{:S(2)}) collective-permute-start(bf16[208,1024]{1,0:T(8,128)(2,1)} %collective-permute-done.2.refs_3_), channel_id=1, source_target_pairs={{0,2},{1,3},{2,0},{3,1},{4,6},{5,7},{6,4},{7,5},{8,10},{9,11},{10,... | collective-permute-start | bytes 1277960 | tf_op jit(solution)/shard_map/ppermute | solution.py:23
  19.6 19.4 %collective-permute-start.7 = (bf16[208,1024]{1,0:T(8,128)(2,1)}, bf16[208,1024]{1,0:T(8,128)(2,1)}, u32[]{:S(2)}, u32[]{:S(2)}) collective-permute-start(bf16[208,1024]{1,0:T(8,128)(2,1)} %collective-permute-done.3.refs_4_), channel_id=1, source_target_pairs={{0,4},{1,5},{2,6},{3,7},{4,0},{5,1},{6,2},{7,3},{8,12},{9,13},{10,... | collective-permute-start | bytes 1277960 | tf_op jit(solution)/shard_map/ppermute | solution.py:23
  28.6 10.4 %copy-start.14 = (bf16[208,1024]{1,0:T(8,128)(2,1)}, bf16[208,1024]{1,0:T(8,128)(2,1)S(1)}, u32[]{:S(2)}) copy-start(bf16[208,1024]{1,0:T(8,128)(2,1)S(1)} %collective-permute-done.6.refs_7_) | copy-start | bytes 1277956
  28.6 10.4 %collective-permute-start.8 = (bf16[208,1024]{1,0:T(8,128)(2,1)S(1)}, bf16[208,1024]{1,0:T(8,128)(2,1)}, u32[]{:S(2)}, u32[]{:S(2)}) collective-permute-start(bf16[208,1024]{1,0:T(8,128)(2,1)S(1)} %collective-permute-done.6.refs_7_), channel_id=1, source_target_pairs={{0,2},{1,3},{2,0},{3,1},{4,6},{5,7},{6,4},{7,5},{8,10},{9,11},{10,... | collective-permute-start | bytes 1277960 | tf_op jit(solution)/shard_map/ppermute | solution.py:23
  28.8 13.7 %copy-start.5 = (bf16[384,1024]{1,0:T(8,128)(2,1)S(1)}, bf16[384,1024]{1,0:T(8,128)(2,1)}, u32[]{:S(2)}) copy-start(bf16[384,1024]{1,0:T(8,128)(2,1)} %copy-done.4) | copy-start | bytes 2359300
  28.9 13.7 %copy-start.11 = (s32[4]{0:T(128)S(1)}, s32[4]{0:T(128)}, u32[]{:S(2)}) copy-start(s32[4]{0:T(128)} %lengths.1) | copy-start | bytes 52
  28.9 12.8 %collective-permute-start.1 = (bf16[384,1024]{1,0:T(8,128)(2,1)}, bf16[384,1024]{1,0:T(8,128)(2,1)S(1)}, u32[]{:S(2)}, u32[]{:S(2)}) collective-permute-start(bf16[384,1024]{1,0:T(8,128)(2,1)} %copy-done.12), channel_id=1, source_target_pairs={{0,1},{1,0},{2,3},{3,2},{4,5},{5,4},{6,7},{7,6},{8,9},{9,8},{10,11... | collective-permute-start | bytes 2359304 | tf_op jit(solution)/shard_map/ppermute | solution.py:23
  37.0 14.6 %collective-permute-start.13 = (bf16[128,2048]{1,0:T(8,128)(2,1)}, bf16[128,2048]{1,0:T(8,128)(2,1)S(1)}, u32[]{:S(2)}, u32[]{:S(2)}) collective-permute-start(bf16[128,2048]{1,0:T(8,128)(2,1)} %collective-permute-done.9), channel_id=1, source_target_pairs={{8,16},{16,24},{9,17},{17,25},{10,18},{18,26},{11,19},{19,27},{12,... | collective-permute-start | bytes 1572872 | tf_op jit(solution)/shard_map/ppermute | solution.py:242
  37.7 17.0 %collective-permute-start.14 = (bf16[128,2048]{1,0:T(8,128)(2,1)}, bf16[128,2048]{1,0:T(8,128)(2,1)S(1)}, u32[]{:S(2)}, u32[]{:S(2)}) collective-permute-start(bf16[128,2048]{1,0:T(8,128)(2,1)} %collective-permute-done.10), channel_id=1, source_target_pairs={{16,8},{8,0},{17,9},{9,1},{18,10},{10,2},{19,11},{11,3},{20,12},{1... | collective-permute-start | bytes 1572872 | tf_op jit(solution)/shard_map/ppermute | solution.py:243
  40.3 2.2 %copy-start.8 = (bf16[208,1024]{1,0:T(8,128)(2,1)S(1)}, bf16[208,1024]{1,0:T(8,128)(2,1)}, u32[]{:S(2)}) copy-start(bf16[208,1024]{1,0:T(8,128)(2,1)} %copy-done.7) | copy-start | bytes 1277956
  40.4 23.3 %collective-permute-start.11 = (bf16[128,2048]{1,0:T(8,128)(2,1)S(1)}, bf16[128,2048]{1,0:T(8,128)(2,1)}, u32[]{:S(2)}, u32[]{:S(2)}) collective-permute-start(bf16[128,2048]{1,0:T(8,128)(2,1)S(1)} %pad_maximum_fusion.refs_3_), channel_id=1, source_target_pairs={{0,2},{1,3},{2,0},{3,1},{4,6},{5,7},{6,4},{7,5},{8,10},{9,11},{10,... | collective-permute-start | bytes 1572872 | tf_op jit(solution)/shard_map/ppermute | solution.py:23
  41.0 22.7 %collective-permute-start.12 = (bf16[128,2048]{1,0:T(8,128)(2,1)S(1)}, bf16[128,2048]{1,0:T(8,128)(2,1)}, u32[]{:S(2)}, u32[]{:S(2)}) collective-permute-start(bf16[128,2048]{1,0:T(8,128)(2,1)S(1)} %pad_maximum_fusion.1.refs_4_), channel_id=1, source_target_pairs={{0,4},{1,5},{2,6},{3,7},{4,0},{5,1},{6,2},{7,3},{8,12},{9,13},{10,... | collective-permute-start | bytes 1572872 | tf_op jit(solution)/shard_map/ppermute | solution.py:23
  51.5 4.5 %copy-start.2 = (bf16[8,256,128]{2,1,0:T(8,128)(2,1)}, bf16[8,256,128]{2,1,0:T(8,128)(2,1)S(1)}, u32[]{:S(2)}) copy-start(bf16[8,256,128]{2,1,0:T(8,128)(2,1)S(1)} %get-tuple-element.39.refs_1_) | copy-start | bytes 1572868
  55.5 8.2 %collective-permute-start.15 = (bf16[64,2048]{1,0:T(8,128)(2,1)}, bf16[64,2048]{1,0:T(8,128)(2,1)}, u32[]{:S(2)}, u32[]{:S(2)}) collective-permute-start(bf16[64,2048]{1,0:T(8,128)(2,1)} %get-tuple-element.75.refs_7_), channel_id=1, source_target_pairs={{0,2},{1,3},{2,0},{3,1},{4,6},{5,7},{6,4},{7,5},{8,10},{9,11},{10,... | collective-permute-start | bytes 786440 | tf_op jit(solution)/shard_map/ppermute | solution.py:23
  56.0 7.7 %collective-permute-start.16 = (bf16[64,2048]{1,0:T(8,128)(2,1)S(1)}, bf16[64,2048]{1,0:T(8,128)(2,1)}, u32[]{:S(2)}, u32[]{:S(2)}) collective-permute-start(bf16[64,2048]{1,0:T(8,128)(2,1)S(1)} %get-tuple-element.74.refs_8_), channel_id=1, source_target_pairs={{0,4},{1,5},{2,6},{3,7},{4,0},{5,1},{6,2},{7,3},{8,12},{9,13},{10,... | collective-permute-start | bytes 786440 | tf_op jit(solution)/shard_map/ppermute | solution.py:23
  56.6 7.1 %copy-start.3 = (bf16[8,256,128]{2,1,0:T(8,128)(2,1)S(1)}, bf16[8,256,128]{2,1,0:T(8,128)(2,1)}, u32[]{:S(2)}) copy-start(bf16[8,256,128]{2,1,0:T(8,128)(2,1)} %copy-done.2) | copy-start | bytes 1572868
  65.9 2.3 %copy-start.6 = (bf16[128,2048]{1,0:T(8,128)(2,1)S(1)}, bf16[128,2048]{1,0:T(8,128)(2,1)}, u32[]{:S(2)}) copy-start(bf16[128,2048]{1,0:T(8,128)(2,1)} %hidden.1) | copy-start | bytes 1572868
  65.9 2.3 %copy-start.9 = (f32[2048]{0:T(1024)S(1)}, f32[2048]{0:T(1024)}, u32[]{:S(2)}) copy-start(f32[2048]{0:T(1024)} %param.27) | copy-start | bytes 24580
  65.9 2.3 %collective-permute-start.17 = (bf16[128,2048]{1,0:T(8,128)(2,1)S(1)}, bf16[128,2048]{1,0:T(8,128)(2,1)S(1)}, u32[]{:S(2)}, u32[]{:S(2)}) collective-permute-start(bf16[128,2048]{1,0:T(8,128)(2,1)S(1)} %project.3), channel_id=1, source_target_pairs={{0,1},{1,0},{2,3},{3,2},{4,5},{5,4},{6,7},{7,6},{8,9},{9,8},{10,11... | collective-permute-start | bytes 1572872 | tf_op jit(solution)/shard_map/ppermute | solution.py:23
  68.7 10.3 %collective-permute-start.18 = (bf16[128,2048]{1,0:T(8,128)(2,1)S(1)}, bf16[128,2048]{1,0:T(8,128)(2,1)S(1)}, u32[]{:S(2)}, u32[]{:S(2)}) collective-permute-start(bf16[128,2048]{1,0:T(8,128)(2,1)S(1)} %get-tuple-element.48.refs_11_), channel_id=1, source_target_pairs={{0,1},{1,0},{2,3},{3,2},{4,5},{5,4},{6,7},{7,6},{8,9},{9,8},{10,11... | collective-permute-start | bytes 1572872 | tf_op jit(solution)/shard_map/ppermute | solution.py:23
  69.2 15.7 %collective-permute-start.24 = (bf16[128,2048]{1,0:T(8,128)(2,1)S(1)}, bf16[128,2048]{1,0:T(8,128)(2,1)S(1)}, u32[]{:S(2)}, u32[]{:S(2)}) collective-permute-start(bf16[128,2048]{1,0:T(8,128)(2,1)S(1)} %get-tuple-element.48.refs_11_), channel_id=1, source_target_pairs={{0,6},{1,7},{2,4},{3,5},{4,2},{5,3},{6,0},{7,1},{8,14},{9,15},{10,... | collective-permute-start | bytes 1572872 | tf_op jit(solution)/shard_map/ppermute | solution.py:23
  84.9 2.4 %collective-permute-start.25 = (bf16[128,2048]{1,0:T(8,128)(2,1)S(1)}, bf16[128,2048]{1,0:T(8,128)(2,1)S(1)}, u32[]{:S(2)}, u32[]{:S(2)}) collective-permute-start(bf16[128,2048]{1,0:T(8,128)(2,1)S(1)} %collective-permute-done.24.refs_11_), channel_id=1, source_target_pairs={{0,1},{1,0},{2,3},{3,2},{4,5},{5,4},{6,7},{7,6},{8,9},{9,8},{10,11... | collective-permute-start | bytes 1572872 | tf_op jit(solution)/shard_map/ppermute | solution.py:23
  85.0 14.3 %collective-permute-start.20 = (bf16[128,2048]{1,0:T(8,128)(2,1)S(1)}, bf16[128,2048]{1,0:T(8,128)(2,1)S(1)}, u32[]{:S(2)}, u32[]{:S(2)}) collective-permute-start(bf16[128,2048]{1,0:T(8,128)(2,1)S(1)} %get-tuple-element.48.refs_11_), channel_id=1, source_target_pairs={{0,2},{1,3},{2,0},{3,1},{4,6},{5,7},{6,4},{7,5},{8,10},{9,11},{10,... | collective-permute-start | bytes 1572872 | tf_op jit(solution)/shard_map/ppermute | solution.py:23
  85.8 13.9 %collective-permute-start.22 = (bf16[128,2048]{1,0:T(8,128)(2,1)S(1)}, bf16[128,2048]{1,0:T(8,128)(2,1)S(1)}, u32[]{:S(2)}, u32[]{:S(2)}) collective-permute-start(bf16[128,2048]{1,0:T(8,128)(2,1)S(1)} %get-tuple-element.48.refs_11_), channel_id=1, source_target_pairs={{0,4},{1,5},{2,6},{3,7},{4,0},{5,1},{6,2},{7,3},{8,12},{9,13},{10,... | collective-permute-start | bytes 1572872 | tf_op jit(solution)/shard_map/ppermute | solution.py:23
  93.2 6.6 %collective-permute-start.26 = (bf16[1,128,2048]{2,1,0:T(8,128)(2,1)S(1)}, bf16[1,128,2048]{2,1,0:T(8,128)(2,1)S(1)}, u32[]{:S(2)}, u32[]{:S(2)}) collective-permute-start(bf16[1,128,2048]{2,1,0:T(8,128)(2,1)S(1)} %get-tuple-element.65), channel_id=1, source_target_pairs={{0,1},{1,0},{2,3},{3,2},{4,5},{5,4},{6,7},{7,6},{8,9},{9,8},{10,11... | collective-permute-start | bytes 1572872 | tf_op jit(solution)/shard_map/ppermute | solution.py:23
  99.3 3.5 %collective-permute-start.21 = (bf16[128,2048]{1,0:T(8,128)(2,1)S(1)}, bf16[128,2048]{1,0:T(8,128)(2,1)S(1)}, u32[]{:S(2)}, u32[]{:S(2)}) collective-permute-start(bf16[128,2048]{1,0:T(8,128)(2,1)S(1)} %collective-permute-done.20.refs_11_), channel_id=1, source_target_pairs={{0,1},{1,0},{2,3},{3,2},{4,5},{5,4},{6,7},{7,6},{8,9},{9,8},{10,11... | collective-permute-start | bytes 1572872 | tf_op jit(solution)/shard_map/ppermute | solution.py:23
  99.6 3.2 %collective-permute-start.23 = (bf16[128,2048]{1,0:T(8,128)(2,1)S(1)}, bf16[128,2048]{1,0:T(8,128)(2,1)S(1)}, u32[]{:S(2)}, u32[]{:S(2)}) collective-permute-start(bf16[128,2048]{1,0:T(8,128)(2,1)S(1)} %collective-permute-done.22.refs_13_), channel_id=1, source_target_pairs={{0,1},{1,0},{2,3},{3,2},{4,5},{5,4},{6,7},{7,6},{8,9},{9,8},{10,11... | collective-permute-start | bytes 1572872 | tf_op jit(solution)/shard_map/ppermute | solution.py:23
  100.0 9.7 %collective-permute-start.27 = (bf16[64,2048]{1,0:T(8,128)(2,1)S(1)}, bf16[64,2048]{1,0:T(8,128)(2,1)S(1)}, u32[]{:S(2)}, u32[]{:S(2)}) collective-permute-start(bf16[64,2048]{1,0:T(8,128)(2,1)S(1)} %get-tuple-element.77), channel_id=1, source_target_pairs={{0,2},{1,3},{2,0},{3,1},{4,6},{5,7},{6,4},{7,5},{8,10},{9,11},{10,... | collective-permute-start | bytes 786440 | tf_op jit(solution)/shard_map/ppermute | solution.py:23
  101.3 8.4 %collective-permute-start.28 = (bf16[64,2048]{1,0:T(8,128)(2,1)S(1)}, bf16[64,2048]{1,0:T(8,128)(2,1)S(1)}, u32[]{:S(2)}, u32[]{:S(2)}) collective-permute-start(bf16[64,2048]{1,0:T(8,128)(2,1)S(1)} %get-tuple-element.76), channel_id=1, source_target_pairs={{0,4},{1,5},{2,6},{3,7},{4,0},{5,1},{6,2},{7,3},{8,12},{9,13},{10,... | collective-permute-start | bytes 786440 | tf_op jit(solution)/shard_map/ppermute | solution.py:23
  109.8 2.7 %collective-permute-start.29 = (bf16[2,128,2048]{2,1,0:T(8,128)(2,1)S(1)}, bf16[2,128,2048]{2,1,0:T(8,128)(2,1)S(1)}, u32[]{:S(2)}, u32[]{:S(2)}) collective-permute-start(bf16[2,128,2048]{2,1,0:T(8,128)(2,1)S(1)} %get-tuple-element.66), channel_id=1, source_target_pairs={{0,1},{1,0},{2,3},{3,2},{4,5},{5,4},{6,7},{7,6},{8,9},{9,8},{10,11... | collective-permute-start | bytes 3145736 | tf_op jit(solution)/shard_map/ppermute | solution.py:23
  109.8 5.5 %collective-permute-start.19 = (bf16[1,128,2048]{2,1,0:T(8,128)(2,1)S(1)}, bf16[1,128,2048]{2,1,0:T(8,128)(2,1)S(1)}, u32[]{:S(2)}, u32[]{:S(2)}) collective-permute-start(bf16[1,128,2048]{2,1,0:T(8,128)(2,1)S(1)} %get-tuple-element.60), channel_id=1, source_target_pairs={{0,1},{1,0},{2,3},{3,2},{4,5},{5,4},{6,7},{7,6},{8,9},{9,8},{10,11... | collective-permute-start | bytes 1572872 | tf_op jit(solution)/shard_map/ppermute | solution.py:23
  113.1 14.0 %collective-permute-start.31 = (bf16[128,2048]{1,0:T(8,128)(2,1)S(1)}, bf16[128,2048]{1,0:T(8,128)(2,1)S(1)}, u32[]{:S(2)}, u32[]{:S(2)}) collective-permute-start(bf16[128,2048]{1,0:T(8,128)(2,1)S(1)} %pad_maximum_fusion.3), channel_id=1, source_target_pairs={{0,4},{1,5},{2,6},{3,7},{4,0},{5,1},{6,2},{7,3},{8,12},{9,13},{10,... | collective-permute-start | bytes 1572872 | tf_op jit(solution)/shard_map/ppermute | solution.py:23
  114.7 15.0 %copy-start.1 = (bf16[512,2048]{1,0:T(8,128)(2,1)S(1)}, bf16[512,2048]{1,0:T(8,128)(2,1)}, u32[]{:S(2)}) copy-start(bf16[512,2048]{1,0:T(8,128)(2,1)} %param.26) | copy-start | bytes 6291460
  114.7 13.8 %collective-permute-start.30 = (bf16[128,2048]{1,0:T(8,128)(2,1)S(1)}, bf16[128,2048]{1,0:T(8,128)(2,1)S(1)}, u32[]{:S(2)}, u32[]{:S(2)}) collective-permute-start(bf16[128,2048]{1,0:T(8,128)(2,1)S(1)} %pad_maximum_fusion.2), channel_id=1, source_target_pairs={{0,2},{1,3},{2,0},{3,1},{4,6},{5,7},{6,4},{7,5},{8,10},{9,11},{10,... | collective-permute-start | bytes 1572872 | tf_op jit(solution)/shard_map/ppermute | solution.py:23
  (1 other events, 0.9 us)

commit v4 on v3

--- a/solution.py
+++ b/solution.py
@@ -44,9 +44,13 @@
 IN_PLACE = pl.BlockSpec(memory_space=pl.ANY)
 
 
-def pack_body(core, *refs):
-    sources, (send, send_prompts, mine, prompts), held, sems = refs[:7], refs[7:11], refs[11:18], refs[18]
+def pack_body(place, *refs):
+    sources, out_proj, (send, send_prompts, prompts, block) = refs[:7], refs[7], refs[8:12]
+    held, sems = refs[12:19], refs[19]
+    core, parity = place[0] % 2, (place[0] // 2 + place[0] // 4) % 2
+    head_rows = pl.ds(pl.multiple_of((2 * core + parity) * HEAD_DIM, HEAD_DIM), HEAD_DIM)
     copies = [pltpu.make_async_copy(sources[i], held[i], sems.at[i]) for i in range(7)]
+    copies.append(pltpu.make_async_copy(out_proj.at[head_rows], block, sems.at[7]))
     for copy in copies:
         copy.start()
     for copy in copies:
@@ -57,16 +61,16 @@
     width = 2 * HEAD_DIM
     for shard in range(shards):
         lanes = slice(shard * width, (shard + 1) * width)
-        for target, which in ((0, core[0]), (1, 1 - core[0])):
+        for target, which in ((0, core), (1, 1 - core)):
             start = pl.multiple_of(shard * 2 * width + which * width, width)
             low = 0
             for part in (queries, keys, values, prompt_keys, prompt_values):
                 high = low + part.shape[0]
-                taken = part[:, pl.ds(start, width)]
-                if high <= 3 * rows:
-                    (mine, send)[target][low:high, lanes] = taken
-                else:
-                    (prompts, send_prompts)[target][low - 3 * rows : high - 3 * rows, lanes] = taken
+                if high > 3 * rows:
+                    kept = slice(low - 3 * rows, high - 3 * rows)
+                    (prompts, send_prompts)[target][kept, lanes] = part[:, pl.ds(start, width)]
+                elif target == 1:
+                    send[low:high, lanes] = part[:, pl.ds(start, width)]
                 low = high
     top = ids.shape[0]
     high_part = gates[...].astype(BF16)
@@ -81,7 +85,7 @@
         target[base : base + 2 * top, rows : 2 * rows] = second
 
 
-def pack(core, queries, keys, values, prompt_keys, prompt_values, ids, gates):
+def pack(place, queries, keys, values, prompt_keys, prompt_values, ids, gates, out_proj):
     rows, features = queries.shape
     tail = 2 * prompt_keys.shape[0] + 2 * ids.shape[0]
     parts = (queries, keys, values, prompt_keys, prompt_values, ids, gates)
@@ -90,15 +94,15 @@
         out_shape=(
             everywhere((3 * rows, features // 2), BF16),
             everywhere((tail, features // 2), BF16),
-            everywhere((3 * rows, features // 2), BF16),
             everywhere((tail, features // 2), BF16),
+            everywhere((HEAD_DIM, features), BF16),
         ),
-        in_specs=[IN_SMEM] + [IN_PLACE] * 7,
+        in_specs=[IN_SMEM] + [IN_PLACE] * 8,
         out_specs=(IN_VMEM,) * 4,
-        scratch_shapes=[pltpu.VMEM(part.shape, part.dtype) for part in parts] + [pltpu.SemaphoreType.DMA((7,))],
+        scratch_shapes=[pltpu.VMEM(part.shape, part.dtype) for part in parts] + [pltpu.SemaphoreType.DMA((8,))],
         compiler_params=pltpu.CompilerParams(vmem_limit_bytes=12 * 2**20),
         name="pack",
-    )(core, *[in_hbm(part) for part in parts])
+    )(place, *[in_hbm(part) for part in (*parts, out_proj)])
 
 
 def attend(queries, all_keys, all_values, bias):
@@ -137,12 +141,12 @@
 
 
 def chip_attention_body(
-    me, my_prompts, sibling, lengths, columns, parents, accepted, mine, prompts_here, *refs
+    me, my_prompts, sibling, lengths, columns, parents, accepted, prompts_here, *refs
 ):
-    copies = [pltpu.make_async_copy(refs[i], refs[15 + i], refs[25].at[i]) for i in range(10)]
+    copies = [pltpu.make_async_copy(refs[i], refs[16 + i], refs[27].at[i]) for i in range(11)]
     for copy in copies:
         copy.start()
-    (attended, cache, ids, gates, bias), (tree_keys, tree_values, got, *holders) = refs[10:15], refs[15:25]
+    (attended, cache, ids, gates, bias), (queries_here, tree_keys, tree_values, got, *holders) = refs[11:16], refs[16:27]
     holders = [prompts_here, *holders]
     rows = tree_keys.shape[0]
     requests = my_prompts.shape[0]
@@ -153,17 +157,19 @@
     fill_bias(bias, columns.shape[1], tree_len, parents[...], prompts, lengths, columns[1:2, :], position)
     for copy in copies:
         copy.wait()
-    for head in range(mine.shape[1] // HEAD_DIM):
+    for head in range(got.shape[1] // HEAD_DIM):
         lanes = slice(head * HEAD_DIM, (head + 1) * HEAD_DIM)
-        queries = jnp.concatenate([mine[:rows, lanes], got[:rows, lanes]], axis=0)
+        place = head // 2 * 4 * HEAD_DIM + me[0] % 2 * 2 * HEAD_DIM + head % 2 * HEAD_DIM
+        mine = pl.ds(pl.multiple_of(place, HEAD_DIM), HEAD_DIM)
+        queries = jnp.concatenate([queries_here[:, mine], got[:rows, lanes]], axis=0)
         all_keys = jnp.concatenate(
             [ref[:block, lanes] for ref in holders]
-            + [mine[rows : 2 * rows, lanes], got[rows : 2 * rows, lanes]],
+            + [tree_keys[:, mine], got[rows : 2 * rows, lanes]],
             axis=0,
         )
         all_values = jnp.concatenate(
             [ref[block : 2 * block, lanes] for ref in holders]
-            + [mine[2 * rows :, lanes], got[2 * rows : 3 * rows, lanes]],
+            + [tree_values[:, mine], got[2 * rows : 3 * rows, lanes]],
             axis=0,
         )
         attended[head] = attend(queries, all_keys, all_values, bias[...])
@@ -176,12 +182,11 @@
         gates[index // 2, :, lanes] = first[8:] + second[8:]
 
 
-def chip_attention(scalars, columns, parents, accepted, tree_keys, tree_values, mine, prompts, blocks):
+def chip_attention(scalars, columns, parents, accepted, queries, tree_keys, tree_values, prompts, blocks):
     rows, features = tree_keys.shape
     width = columns.shape[1] + 2 * rows
     heads = features // HEAD_DIM // 2
-    copied = [in_hbm(part) for part in (tree_keys, tree_values, *blocks)]
-    kept = (mine, prompts)
+    copied = [in_hbm(part) for part in (queries, tree_keys, tree_values, *blocks)]
     return pl.pallas_call(
         chip_attention_body,
         out_shape=(
@@ -190,14 +195,14 @@
             everywhere((4, 8, 2 * rows), F32),
             everywhere((4, 8, 2 * rows), F32),
         ),
-        in_specs=[IN_SMEM] * 4 + [IN_VMEM] * 5 + [IN_PLACE] * len(copied),
+        in_specs=[IN_SMEM] * 4 + [IN_VMEM] * 4 + [IN_PLACE] * len(copied),
         out_specs=(IN_VMEM,) * 4,
         scratch_shapes=[pltpu.VMEM((2 * rows, width), F32)]
         + [pltpu.VMEM(part.shape, BF16) for part in copied]
         + [pltpu.SemaphoreType.DMA((len(copied),))],
         compiler_params=pltpu.CompilerParams(vmem_limit_bytes=14 * 2**20),
         name="attention",
-    )(*scalars, columns, parents, accepted, *kept, *copied)
+    )(*scalars, columns, parents, accepted, prompts, *copied)
 
 
 def plain_attention_body(
@@ -228,12 +233,10 @@
     )(prompts, lengths, columns, parents, accepted, queries, tree_keys, tree_values, keys, values)
 
 
-def fetch_projection(out_proj, packed, before_shared):
+def fetch_projection(out_proj, block, before_shared):
     me, place = lax.axis_index("rep"), lax.axis_index("ep")
     core, parity = place % 2, (place // 2 + place // 4) % 2
-    block = lax.dynamic_slice_in_dim(out_proj, (2 * core + parity) * HEAD_DIM, HEAD_DIM, 0)
     own = lax.dynamic_slice_in_dim(out_proj, core * 2 * HEAD_DIM, 2 * HEAD_DIM, 0)
-    block = after(block, packed)
 
     def shifted(value, by):
         return lax.ppermute(value, "rep", [(i, (i + by) % 4) for i in range(4)])
@@ -438,20 +441,20 @@
     me = lax.axis_index("ep").astype(jnp.int32)
 
     flat = (prompt_count * rows_here, features)
-    send, send_prompts, mine, prompts = pack(
-        (me % 2).reshape(1), tree_queries, tree_keys, tree_values, prompt_keys.reshape(flat),
-        prompt_values.reshape(flat), expert_ids.T, gate_weights.T,
+    send, send_prompts, prompts, block = pack(
+        me.reshape(1), tree_queries, tree_keys, tree_values, prompt_keys.reshape(flat),
+        prompt_values.reshape(flat), expert_ids.T, gate_weights.T, out_proj,
     )
     x_mine, y_mine = flip(prompts, 2, 8), flip(prompts, 4, 8)
     theirs = flip(send_prompts, 1, 8)
     x_theirs, y_theirs = flip(theirs, 2, 8), flip(theirs, 4, 8)
     far_a, far_b = flip(x_mine, 4, 8), flip(y_theirs, 2, 8)
-    weights, pieces, order, up, down_rows = fetch_projection(out_proj, prompts, (x_mine, y_mine, x_theirs, y_theirs, far_a, far_b))
+    weights, pieces, order, up, down_rows = fetch_projection(out_proj, block, (x_mine, y_mine, x_theirs, y_theirs, far_a, far_b))
     got = flip(send, 1, 8)
     small = jnp.concatenate(
         [tree_parents, jnp.broadcast_to(request_prompt[:, None], tree_parents.shape)], axis=0
     )
-    sibling = flip(small, 1, 8)
+    sibling = flip(after(small, x_mine), 1, 8)
 
     column = jnp.arange(8 * flat[0], dtype=jnp.int32)
     columns = jnp.stack([column // flat[0], column % flat[0] // rows_here, column % rows_here])
@@ -460,7 +463,7 @@
     chip_parents = jnp.where(chip_parents < 0, -1, chip_parents + first_node).reshape(-1, 1)
     attended, cache, ids, gates = chip_attention(
         (me.reshape(1), request_prompt, sibling, prompt_lengths), columns, chip_parents, accepted,
-        tree_keys, tree_values, mine, prompts, (got, theirs, x_mine, x_theirs, y_mine, y_theirs, far_a, far_b),
+        tree_queries, tree_keys, tree_values, prompts, (got, theirs, x_mine, x_theirs, y_mine, y_theirs, far_a, far_b),
     )
     up, down_rows = after((up, down_rows), attended)
     edge = up.shape[0] // 2

time: 130 us -> 126 us (0.969)
  waiting for transfers between devices: 50.7 us -> 48.7 us
    ppermute x28, waiting for transfers between devices: 39.5 us -> 43 us  [flip(): return lax.ppermute(value, 'ep', [(i, i ^ bits) for i in range(size)])]
    ppermute x1, waiting for transfers between devices: 3.17 us -> 0.01 us  [fetch_projection(): down = lax.ppermute(came3, 'rep', [(2, 1), (1, 0)])]
    ppermute x2, waiting for transfers between devices: 8.02 us -> 5.68 us  [shifted(): return lax.ppermute(value, 'rep', [(i, (i + by) % 4) for i in range(4)])]
  transfers between devices with their start and end apart: 32 -> 32, of which waited for: 11 -> 14; matrix products, arithmetic and copies ran while one was open for 3% -> 3% of each run, Pallas kernels for 29% -> 30%
where the time goes in v4:
time: 126 us
  waiting for transfers between devices  48.7 us (39%)
  Pallas kernels  43 us (34%)
  starting transfers between devices  27.2 us (22%)
  local copies, waits for them, and re-layouts  3.83 us (3%)
  other arithmetic  2.36 us (2%)
    ppermute x28, waiting for transfers between devices, flip(): return lax.ppermute(value, 'ep', [(i, i ^ bits) for i in range(size)])  43 us
    ppermute x28, starting transfers between devices, flip(): return lax.ppermute(value, 'ep', [(i, i ^ bits) for i in range(size)])  21.4 us
    pallas_call x3, Pallas kernels, experts(): pl.pallas_call(lambda *refs: experts_body(len(sources) // pairs, local_ex...  18.7 us
    pallas_call x1, Pallas kernels, chip_attention(): pl.pallas_call(chip_attention_body, out_shape=(everywhere((heads, 2 * row...  9.11 us
    pallas_call x1, Pallas kernels, stage(): pl.pallas_call(stage_body, out_shape=[pltpu.VMEM(gate_up.shape[1:], BF16)...  8.32 us
    ppermute x2, waiting for transfers between devices, shifted(): return lax.ppermute(value, 'rep', [(i, (i + by) % 4) for i in range(4)])  5.68 us
    ppermute x2, starting transfers between devices, shifted(): return lax.ppermute(value, 'rep', [(i, (i + by) % 4) for i in range(4)])  3.82 us
    pallas_call x2, Pallas kernels, chip_project(): pl.pallas_call(lambda *refs: chip_project_body(pieces, low_row, *refs), o...  3.42 us
  transfers between devices with their start and end apart: 32, of which 14 were waited for; matrix products, arithmetic and copies ran while one was open for 3% of the time, Pallas kernels for 30%

profile of v4, /device:TPU:0, one launch (start us, length us, event | category | flops | bytes accessed | tf_op | source)
XLA Modules:
  0.0 126.1 jit_solution(3734670985541084517)
XLA Ops:
  0.7 3.0 %pack.1 = (bf16[384,1024]{1,0:T(8,128)(2,1)}, bf16[208,1024]{1,0:T(8,128)(2,1)S(1)}, bf16[208,1024]{1,0:T(8,128)(2,1)S(1)}, bf16[128,2048]{1,0:T(8,128)(2,1)S(1)}) custom-call(s32[1]{0:T(128)} %bitcast.8.place.me, bf16[128,2048]{1,0:T(8,128)(2,1)} %refs_0_.3, bf16[128,2048]{1,0:T(8,128)(2,1)} %refs_1_.3, bf16[128,2048]{1,0:T(8,128)(2,1)} %refs_2_.3, ...), custom_call_target="tpu_custom_call" | custom-call | tf_op jit(solution)/shard_map/pack/pallas_call | solution.py:92
  3.7 0.5 collective-permute-start.3
  4.2 2.6 %collective-permute-start = (bf16[208,1024]{1,0:T(8,128)(2,1)S(1)}, bf16[208,1024]{1,0:T(8,128)(2,1)S(1)}, u32[]{:S(2)}, u32[]{:S(2)}) collective-permute-start(bf16[208,1024]{1,0:T(8,128)(2,1)S(1)} %get-tuple-element.35.prompts_here), channel_id=1, source_target_pairs={{0,2},{1,3},{2,0},{3,1},{4,6},{5,7},{6,4},{7,5},{8,10},{9,11},{10,... | collective-permute-start | bytes 1277960 | tf_op jit(solution)/shard_map/ppermute | solution.py:23
  6.8 1.5 %collective-permute-start.5 = (bf16[208,1024]{1,0:T(8,128)(2,1)S(1)}, bf16[208,1024]{1,0:T(8,128)(2,1)}, u32[]{:S(2)}, u32[]{:S(2)}) collective-permute-start(bf16[208,1024]{1,0:T(8,128)(2,1)S(1)} %get-tuple-element.35.prompts_here), channel_id=1, source_target_pairs={{0,4},{1,5},{2,6},{3,7},{4,0},{5,1},{6,2},{7,3},{8,12},{9,13},{10,... | collective-permute-start | bytes 1277960 | tf_op jit(solution)/shard_map/ppermute | solution.py:23
  8.3 1.6 %collective-permute-start.9 = (bf16[128,2048]{1,0:T(8,128)(2,1)S(1)}, bf16[128,2048]{1,0:T(8,128)(2,1)S(1)}, u32[]{:S(2)}, u32[]{:S(2)}) collective-permute-start(bf16[128,2048]{1,0:T(8,128)(2,1)S(1)} %get-tuple-element.40), channel_id=1, source_target_pairs={{0,8},{8,16},{16,24},{24,0},{1,9},{9,17},{17,25},{25,1},{2,10},{10... | collective-permute-start | bytes 1572872 | tf_op jit(solution)/shard_map/ppermute | solution.py:242
  9.9 2.2 %collective-permute-start.10 = (bf16[128,2048]{1,0:T(8,128)(2,1)S(1)}, bf16[128,2048]{1,0:T(8,128)(2,1)}, u32[]{:S(2)}, u32[]{:S(2)}) collective-permute-start(bf16[128,2048]{1,0:T(8,128)(2,1)S(1)} %get-tuple-element.40), channel_id=1, source_target_pairs={{0,24},{8,0},{16,8},{24,16},{1,25},{9,1},{17,9},{25,17},{2,26},{10... | collective-permute-start | bytes 1572872 | tf_op jit(solution)/shard_map/ppermute | solution.py:242
  12.3 0.6 collective-permute-start.6
  13.0 4.2 %collective-permute-done.refs_5_ = bf16[208,1024]{1,0:T(8,128)(2,1)S(1)} collective-permute-done((bf16[208,1024]{1,0:T(8,128)(2,1)S(1)}, bf16[208,1024]{1,0:T(8,128)(2,1)S(1)}, u32[]{:S(2)}, u32[]{:S(2)}) %collective-permute-start) | collective-permute-done | bytes 426016 | tf_op jit(solution)/shard_map/ppermute | solution.py:23
  17.3 2.3 %collective-permute-done.5.refs_7_ = bf16[208,1024]{1,0:T(8,128)(2,1)} collective-permute-done((bf16[208,1024]{1,0:T(8,128)(2,1)S(1)}, bf16[208,1024]{1,0:T(8,128)(2,1)}, u32[]{:S(2)}, u32[]{:S(2)}) %collective-permute-start.5) | collective-permute-done | bytes 426016 | tf_op jit(solution)/shard_map/ppermute | solution.py:23
  19.6 2.0 %collective-permute-start.7 = (bf16[208,1024]{1,0:T(8,128)(2,1)S(1)}, bf16[208,1024]{1,0:T(8,128)(2,1)}, u32[]{:S(2)}, u32[]{:S(2)}) collective-permute-start(bf16[208,1024]{1,0:T(8,128)(2,1)S(1)} %collective-permute-done.refs_5_), channel_id=1, source_target_pairs={{0,4},{1,5},{2,6},{3,7},{4,0},{5,1},{6,2},{7,3},{8,12},{9,13},{10,... | collective-permute-start | bytes 1277960 | tf_op jit(solution)/shard_map/ppermute | solution.py:23
  21.6 7.0 %collective-permute-done.6.refs_8_ = bf16[208,1024]{1,0:T(8,128)(2,1)S(1)} collective-permute-done((bf16[208,1024]{1,0:T(8,128)(2,1)S(1)}, bf16[208,1024]{1,0:T(8,128)(2,1)S(1)}, u32[]{:S(2)}, u32[]{:S(2)}) %collective-permute-start.6) | collective-permute-done | bytes 426016 | tf_op jit(solution)/shard_map/ppermute | solution.py:23
  29.0 5.7 %collective-permute-done.10 = bf16[128,2048]{1,0:T(8,128)(2,1)} collective-permute-done((bf16[128,2048]{1,0:T(8,128)(2,1)S(1)}, bf16[128,2048]{1,0:T(8,128)(2,1)}, u32[]{:S(2)}, u32[]{:S(2)}) %collective-permute-start.10) | collective-permute-done | bytes 524320 | tf_op jit(solution)/shard_map/ppermute | solution.py:242
  34.7 0.7 collective-permute-start.13
  35.4 1.3 %collective-permute-start.14 = (bf16[128,2048]{1,0:T(8,128)(2,1)}, bf16[128,2048]{1,0:T(8,128)(2,1)S(1)}, u32[]{:S(2)}, u32[]{:S(2)}) collective-permute-start(bf16[128,2048]{1,0:T(8,128)(2,1)} %collective-permute-done.10), channel_id=1, source_target_pairs={{16,8},{8,0},{17,9},{9,1},{18,10},{10,2},{19,11},{11,3},{20,12},{1... | collective-permute-start | bytes 1572872 | tf_op jit(solution)/shard_map/ppermute | solution.py:246
  36.7 0.4 collective-permute-done.7.refs_9_
  37.0 2.0 %collective-permute-done.8.refs_10_ = bf16[208,1024]{1,0:T(8,128)(2,1)} collective-permute-done((bf16[208,1024]{1,0:T(8,128)(2,1)S(1)}, bf16[208,1024]{1,0:T(8,128)(2,1)}, u32[]{:S(2)}, u32[]{:S(2)}) %collective-permute-start.8) | collective-permute-done | bytes 426016 | tf_op jit(solution)/shard_map/ppermute | solution.py:23
  39.1 1.1 fusion.8
  40.3 1.6 %collective-permute-start.11 = (bf16[128,2048]{1,0:T(8,128)(2,1)S(1)}, bf16[128,2048]{1,0:T(8,128)(2,1)S(1)}, u32[]{:S(2)}, u32[]{:S(2)}) collective-permute-start(bf16[128,2048]{1,0:T(8,128)(2,1)S(1)} %pad_maximum_fusion.refs_3_), channel_id=1, source_target_pairs={{0,2},{1,3},{2,0},{3,1},{4,6},{5,7},{6,4},{7,5},{8,10},{9,11},{10,... | collective-permute-start | bytes 1572872 | tf_op jit(solution)/shard_map/ppermute | solution.py:23
  41.9 1.6 %collective-permute-start.12 = (bf16[128,2048]{1,0:T(8,128)(2,1)S(1)}, bf16[128,2048]{1,0:T(8,128)(2,1)S(1)}, u32[]{:S(2)}, u32[]{:S(2)}) collective-permute-start(bf16[128,2048]{1,0:T(8,128)(2,1)S(1)} %pad_maximum_fusion.1.refs_4_), channel_id=1, source_target_pairs={{0,4},{1,5},{2,6},{3,7},{4,0},{5,1},{6,2},{7,3},{8,12},{9,13},{10,... | collective-permute-start | bytes 1572872 | tf_op jit(solution)/shard_map/ppermute | solution.py:23
  43.5 0.9 copy-done.6
  44.4 9.1 %attention.1 = (bf16[8,256,128]{2,1,0:T(8,128)(2,1)S(1)}, bf16[32,4096]{1,0:T(8,128)(2,1)}, f32[4,8,256]{2,1,0:T(8,128)S(1)}, f32[4,8,256]{2,1,0:T(8,128)S(1)}) custom-call(s32[1]{0:T(128)} %bitcast.8.place.me, s32[2]{0:T(128)S(1)} %copy-done.4, s32[4,64]{1,0:T(4,128)S(1)} %collective-permute-done.1.sibling, s32[4]{0:T(128)S(1)} %copy-done.5, ...), custom_call_target="tpu_custom_call" | custom-call | tf_op jit(solution)/shard_map/attention/pallas_call | solution.py:190
  53.6 0.6 collective-permute-start.15
  54.2 0.5 collective-permute-start.16
  54.8 1.3 %constant_dynamic-slice_fusion.refs_2_ = bf16[256,2048]{1,0:T(8,128)(2,1)S(1)} fusion(bf16[512,2048]{1,0:T(8,128)(2,1)} %refs_7_.1, s32[]{:T(128)S(6)} %select_n.118), kind=kLoop, calls=%fused_computation.37 | loop fusion | bytes 2097156 | tf_op jit(solution)/shard_map/dynamic_slice | solution.py:239
  56.1 4.8 %collective-permute-done.15.refs_9_ = bf16[64,2048]{1,0:T(8,128)(2,1)S(1)} collective-permute-done((bf16[64,2048]{1,0:T(8,128)(2,1)S(1)}, bf16[64,2048]{1,0:T(8,128)(2,1)S(1)}, u32[]{:S(2)}, u32[]{:S(2)}) %collective-permute-start.15) | collective-permute-done | bytes 262176 | tf_op jit(solution)/shard_map/ppermute | solution.py:23
  60.8 0.4 collective-permute-done.16.refs_10_
  61.2 1.7 %project.3 = bf16[128,2048]{1,0:T(8,128)(2,1)S(1)} custom-call(s32[8]{0:T(128)S(1)} %stack.41.refs_0_, bf16[8,256,128]{2,1,0:T(8,128)(2,1)S(1)} %get-tuple-element.39.refs_1_, bf16[256,2048]{1,0:T(8,128)(2,1)S(1)} %constant_dynamic-slice_fusion.refs_2_, bf16[128,2048]{1,0:T(8,128)(2,1)S(1)} %pad_maximum_fusion.refs_3_, ...), custom_call_target="tpu_custom_call" | custom-call | tf_op jit(solution)/shard_map/project/pallas_call | solution.py:281
  63.0 1.7 %project.2.mine = f32[128,2048]{1,0:T(8,128)S(1)} custom-call(s32[8]{0:T(128)S(1)} %stack.41.refs_0_, bf16[8,256,128]{2,1,0:T(8,128)(2,1)S(1)} %get-tuple-element.39.refs_1_, bf16[256,2048]{1,0:T(8,128)(2,1)S(1)} %constant_dynamic-slice_fusion.refs_2_, bf16[128,2048]{1,0:T(8,128)(2,1)S(1)} %pad_maximum_fusion.refs_3_, ...), custom_call_target="tpu_custom_call" | custom-call | tf_op jit(solution)/shard_map/project/pallas_call | solution.py:281
  64.9 0.4 norm.1
  65.3 0.4 collective-permute-start.18
  65.7 1.4 %collective-permute-start.24 = (bf16[128,2048]{1,0:T(8,128)(2,1)S(1)}, bf16[128,2048]{1,0:T(8,128)(2,1)S(1)}, u32[]{:S(2)}, u32[]{:S(2)}) collective-permute-start(bf16[128,2048]{1,0:T(8,128)(2,1)S(1)} %get-tuple-element.48.refs_11_), channel_id=1, source_target_pairs={{0,6},{1,7},{2,4},{3,5},{4,2},{5,3},{6,0},{7,1},{8,14},{9,15},{10,... | collective-permute-start | bytes 1572872 | tf_op jit(solution)/shard_map/ppermute | solution.py:23
  67.1 8.3 %stage.1 = (bf16[2048,1024]{1,0:T(8,128)(2,1)S(1)}, bf16[2048,1024]{1,0:T(8,128)(2,1)S(1)}, bf16[2048,1024]{1,0:T(8,128)(2,1)S(1)}, bf16[2048,1024]{1,0:T(8,128)...) custom-call(bf16[4,2048,1024]{2,1,0:T(8,128)(2,1)} %gate_up, ...), custom_call_target="tpu_custom_call" | custom-call | bytes 25165824 | tf_op jit(solution)/shard_map/stage/pallas_call | solution.py:325
  75.5 5.9 %experts.3 = (bf16[1,128,2048]{2,1,0:T(8,128)(2,1)S(1)}, bf16[1,128,2048]{2,1,0:T(8,128)(2,1)S(1)}) custom-call(s32[1]{0:T(128)} %bitcast.14.refs_0_, f32[1,8,256]{2,1,0:T(8,128)S(1)} %get-tuple-element.84.refs_1_, f32[1,8,256]{2,1,0:T(8,128)S(1)} %get-tuple-element.82.refs_2_, bf16[2048,1024]{1,0:T(8,128)(2,1)S(1)} %get-tuple-element.51.refs_3_, ...), custom_call_target="tpu_custom_call" | custom-call | flops 4026531840 | bytes 16777216 | tf_op jit(solution)/shard_map/experts/pallas_call | solution.py:411
  81.5 0.6 collective-permute-start.20
  82.1 1.5 %collective-permute-start.22 = (bf16[128,2048]{1,0:T(8,128)(2,1)S(1)}, bf16[128,2048]{1,0:T(8,128)(2,1)S(1)}, u32[]{:S(2)}, u32[]{:S(2)}) collective-permute-start(bf16[128,2048]{1,0:T(8,128)(2,1)S(1)} %get-tuple-element.48.refs_11_), channel_id=1, source_target_pairs={{0,4},{1,5},{2,6},{3,7},{4,0},{5,1},{6,2},{7,3},{8,12},{9,13},{10,... | collective-permute-start | bytes 1572872 | tf_op jit(solution)/shard_map/ppermute | solution.py:23
  83.6 5.9 %experts.5 = (bf16[1,128,2048]{2,1,0:T(8,128)(2,1)S(1)}, bf16[1,128,2048]{2,1,0:T(8,128)(2,1)S(1)}) custom-call(s32[1]{0:T(128)} %bitcast.14.refs_0_, f32[1,8,256]{2,1,0:T(8,128)S(1)} %get-tuple-element.85.refs_1_, f32[1,8,256]{2,1,0:T(8,128)S(1)} %get-tuple-element.83.refs_2_, bf16[2048,1024]{1,0:T(8,128)(2,1)S(1)} %get-tuple-element.51.refs_3_, ...), custom_call_target="tpu_custom_call" | custom-call | flops 4026531840 | bytes 16777216 | tf_op jit(solution)/shard_map/experts/pallas_call | solution.py:411
  89.6 6.2 %collective-permute-done.20.refs_11_ = bf16[128,2048]{1,0:T(8,128)(2,1)S(1)} collective-permute-done((bf16[128,2048]{1,0:T(8,128)(2,1)S(1)}, bf16[128,2048]{1,0:T(8,128)(2,1)S(1)}, u32[]{:S(2)}, u32[]{:S(2)}) %collective-permute-start.20) | collective-permute-done | bytes 524320 | tf_op jit(solution)/shard_map/ppermute | solution.py:23
  96.5 1.3 %collective-permute-start.27 = (bf16[64,2048]{1,0:T(8,128)(2,1)S(1)}, bf16[64,2048]{1,0:T(8,128)(2,1)S(1)}, u32[]{:S(2)}, u32[]{:S(2)}) collective-permute-start(bf16[64,2048]{1,0:T(8,128)(2,1)S(1)} %get-tuple-element.77), channel_id=1, source_target_pairs={{0,2},{1,3},{2,0},{3,1},{4,6},{5,7},{6,4},{7,5},{8,10},{9,11},{10,... | collective-permute-start | bytes 786440 | tf_op jit(solution)/shard_map/ppermute | solution.py:23
  97.8 1.5 %collective-permute-start.28 = (bf16[64,2048]{1,0:T(8,128)(2,1)S(1)}, bf16[64,2048]{1,0:T(8,128)(2,1)S(1)}, u32[]{:S(2)}, u32[]{:S(2)}) collective-permute-start(bf16[64,2048]{1,0:T(8,128)(2,1)S(1)} %get-tuple-element.76), channel_id=1, source_target_pairs={{0,4},{1,5},{2,6},{3,7},{4,0},{5,1},{6,2},{7,3},{8,12},{9,13},{10,... | collective-permute-start | bytes 786440 | tf_op jit(solution)/shard_map/ppermute | solution.py:23
  99.3 6.9 %experts.4 = (bf16[2,128,2048]{2,1,0:T(8,128)(2,1)S(1)}, bf16[2,128,2048]{2,1,0:T(8,128)(2,1)S(1)}) custom-call(s32[1]{0:T(128)} %bitcast.14.refs_0_, f32[2,8,256]{2,1,0:T(8,128)S(1)} %slice.82.refs_1_, f32[2,8,256]{2,1,0:T(8,128)S(1)} %slice.83.refs_2_, bf16[2048,1024]{1,0:T(8,128)(2,1)S(1)} %get-tuple-element.51.refs_3_, ...), custom_call_target="tpu_custom_call" | custom-call | flops 8053063680 | bytes 16777216 | tf_op jit(solution)/shard_map/experts/pallas_call | solution.py:411
  106.4 0.5 collective-permute-start.19
  106.9 2.1 %collective-permute-done.29 = bf16[2,128,2048]{2,1,0:T(8,128)(2,1)S(1)} collective-permute-done((bf16[2,128,2048]{2,1,0:T(8,128)(2,1)S(1)}, bf16[2,128,2048]{2,1,0:T(8,128)(2,1)S(1)}, u32[]{:S(2)}, u32[]{:S(2)}) %collective-permute-start.29) | collective-permute-done | bytes 1048608 | tf_op jit(solution)/shard_map/ppermute | solution.py:23
  109.0 0.4 convert_add_fusion
  109.7 1.5 %collective-permute-start.31 = (bf16[128,2048]{1,0:T(8,128)(2,1)S(1)}, bf16[128,2048]{1,0:T(8,128)(2,1)S(1)}, u32[]{:S(2)}, u32[]{:S(2)}) collective-permute-start(bf16[128,2048]{1,0:T(8,128)(2,1)S(1)} %pad_maximum_fusion.3), channel_id=1, source_target_pairs={{0,4},{1,5},{2,6},{3,7},{4,0},{5,1},{6,2},{7,3},{8,12},{9,13},{10,... | collective-permute-start | bytes 1572872 | tf_op jit(solution)/shard_map/ppermute | solution.py:23
  111.2 0.6 collective-permute-start.30
  111.8 11.9 %collective-permute-done.31 = bf16[128,2048]{1,0:T(8,128)(2,1)S(1)} collective-permute-done((bf16[128,2048]{1,0:T(8,128)(2,1)S(1)}, bf16[128,2048]{1,0:T(8,128)(2,1)S(1)}, u32[]{:S(2)}, u32[]{:S(2)}) %collective-permute-start.31) | collective-permute-done | bytes 524320 | tf_op jit(solution)/shard_map/ppermute | solution.py:23
  123.7 1.3 %collective-permute-done.30 = bf16[128,2048]{1,0:T(8,128)(2,1)S(1)} collective-permute-done((bf16[128,2048]{1,0:T(8,128)(2,1)S(1)}, bf16[128,2048]{1,0:T(8,128)(2,1)S(1)}, u32[]{:S(2)}, u32[]{:S(2)}) %collective-permute-start.30) | collective-permute-done | bytes 524320 | tf_op jit(solution)/shard_map/ppermute | solution.py:23
  124.9 1.2 fusion.2
  (79 shorter events, 2.4 us)
Async XLA Ops:
  0.6 11.5 %copy-start.4 = (s32[2]{0:T(128)S(1)}, s32[2]{0:T(128)}, u32[]{:S(2)}) copy-start(s32[2]{0:T(128)} %my_prompts.1) | copy-start | bytes 28
  0.6 11.6 %copy-start.10 = (s32[2,64]{1,0:T(2,128)S(1)}, s32[2,64]{1,0:T(2,128)}, u32[]{:S(2)}) copy-start(s32[2,64]{1,0:T(2,128)} %param.20) | copy-start | bytes 1540
  0.7 12.3 %copy-start.11 = (s32[2,16]{1,0:T(2,128)S(1)}, s32[2,16]{1,0:T(2,128)}, u32[]{:S(2)}) copy-start(s32[2,16]{1,0:T(2,128)} %param.21) | copy-start | bytes 388
  3.7 36.5 %copy-start.1 = (bf16[208,1024]{1,0:T(8,128)(2,1)}, bf16[208,1024]{1,0:T(8,128)(2,1)S(1)}, u32[]{:S(2)}) copy-start(bf16[208,1024]{1,0:T(8,128)(2,1)S(1)} %get-tuple-element.35.prompts_here) | copy-start | bytes 1277956
  3.7 8.6 %collective-permute-start.3 = (bf16[208,1024]{1,0:T(8,128)(2,1)S(1)}, bf16[208,1024]{1,0:T(8,128)(2,1)S(1)}, u32[]{:S(2)}, u32[]{:S(2)}) collective-permute-start(bf16[208,1024]{1,0:T(8,128)(2,1)S(1)} %get-tuple-element.38), channel_id=1, source_target_pairs={{0,1},{1,0},{2,3},{3,2},{4,5},{5,4},{6,7},{7,6},{8,9},{9,8},{10,11... | collective-permute-start | bytes 1277960 | tf_op jit(solution)/shard_map/ppermute | solution.py:23
  4.2 13.0 %collective-permute-start = (bf16[208,1024]{1,0:T(8,128)(2,1)S(1)}, bf16[208,1024]{1,0:T(8,128)(2,1)S(1)}, u32[]{:S(2)}, u32[]{:S(2)}) collective-permute-start(bf16[208,1024]{1,0:T(8,128)(2,1)S(1)} %get-tuple-element.35.prompts_here), channel_id=1, source_target_pairs={{0,2},{1,3},{2,0},{3,1},{4,6},{5,7},{6,4},{7,5},{8,10},{9,11},{10,... | collective-permute-start | bytes 1277960 | tf_op jit(solution)/shard_map/ppermute | solution.py:23
  6.8 12.8 %collective-permute-start.5 = (bf16[208,1024]{1,0:T(8,128)(2,1)S(1)}, bf16[208,1024]{1,0:T(8,128)(2,1)}, u32[]{:S(2)}, u32[]{:S(2)}) collective-permute-start(bf16[208,1024]{1,0:T(8,128)(2,1)S(1)} %get-tuple-element.35.prompts_here), channel_id=1, source_target_pairs={{0,4},{1,5},{2,6},{3,7},{4,0},{5,1},{6,2},{7,3},{8,12},{9,13},{10,... | collective-permute-start | bytes 1277960 | tf_op jit(solution)/shard_map/ppermute | solution.py:23
  8.3 20.6 %collective-permute-start.9 = (bf16[128,2048]{1,0:T(8,128)(2,1)S(1)}, bf16[128,2048]{1,0:T(8,128)(2,1)S(1)}, u32[]{:S(2)}, u32[]{:S(2)}) collective-permute-start(bf16[128,2048]{1,0:T(8,128)(2,1)S(1)} %get-tuple-element.40), channel_id=1, source_target_pairs={{0,8},{8,16},{16,24},{24,0},{1,9},{9,17},{17,25},{25,1},{2,10},{10... | collective-permute-start | bytes 1572872 | tf_op jit(solution)/shard_map/ppermute | solution.py:242
  9.9 24.8 %collective-permute-start.10 = (bf16[128,2048]{1,0:T(8,128)(2,1)S(1)}, bf16[128,2048]{1,0:T(8,128)(2,1)}, u32[]{:S(2)}, u32[]{:S(2)}) collective-permute-start(bf16[128,2048]{1,0:T(8,128)(2,1)S(1)} %get-tuple-element.40), channel_id=1, source_target_pairs={{0,24},{8,0},{16,8},{24,16},{1,25},{9,1},{17,9},{25,17},{2,26},{10... | collective-permute-start | bytes 1572872 | tf_op jit(solution)/shard_map/ppermute | solution.py:242
  12.3 24.7 %copy-start.7 = (bf16[208,1024]{1,0:T(8,128)(2,1)}, bf16[208,1024]{1,0:T(8,128)(2,1)S(1)}, u32[]{:S(2)}) copy-start(bf16[208,1024]{1,0:T(8,128)(2,1)S(1)} %collective-permute-done.3.refs_4_) | copy-start | bytes 1277956
  12.3 16.2 %collective-permute-start.6 = (bf16[208,1024]{1,0:T(8,128)(2,1)S(1)}, bf16[208,1024]{1,0:T(8,128)(2,1)S(1)}, u32[]{:S(2)}, u32[]{:S(2)}) collective-permute-start(bf16[208,1024]{1,0:T(8,128)(2,1)S(1)} %collective-permute-done.3.refs_4_), channel_id=1, source_target_pairs={{0,4},{1,5},{2,6},{3,7},{4,0},{5,1},{6,2},{7,3},{8,12},{9,13},{10,... | collective-permute-start | bytes 1277960 | tf_op jit(solution)/shard_map/ppermute | solution.py:23
  17.2 19.8 %copy-start.8 = (bf16[208,1024]{1,0:T(8,128)(2,1)}, bf16[208,1024]{1,0:T(8,128)(2,1)S(1)}, u32[]{:S(2)}) copy-start(bf16[208,1024]{1,0:T(8,128)(2,1)S(1)} %collective-permute-done.refs_5_) | copy-start | bytes 1277956
  17.2 2.4 %collective-permute-start.1 = (s32[4,64]{1,0:T(4,128)S(1)}, s32[4,64]{1,0:T(4,128)S(1)}, u32[]{:S(2)}, u32[]{:S(2)}) collective-permute-start(s32[4,64]{1,0:T(4,128)S(1)} %pad_add_fusion.2), channel_id=1, source_target_pairs={{0,1},{1,0},{2,3},{3,2},{4,5},{5,4},{6,7},{7,6},{8,9},{9,8},{10,11... | collective-permute-start | bytes 3080 | tf_op jit(solution)/shard_map/ppermute | solution.py:23
  19.5 15.8 %collective-permute-start.4 = (bf16[208,1024]{1,0:T(8,128)(2,1)S(1)}, bf16[208,1024]{1,0:T(8,128)(2,1)}, u32[]{:S(2)}, u32[]{:S(2)}) collective-permute-start(bf16[208,1024]{1,0:T(8,128)(2,1)S(1)} %collective-permute-done.3.refs_4_), channel_id=1, source_target_pairs={{0,2},{1,3},{2,0},{3,1},{4,6},{5,7},{6,4},{7,5},{8,10},{9,11},{10,... | collective-permute-start | bytes 1277960 | tf_op jit(solution)/shard_map/ppermute | solution.py:23
  19.6 17.4 %collective-permute-start.7 = (bf16[208,1024]{1,0:T(8,128)(2,1)S(1)}, bf16[208,1024]{1,0:T(8,128)(2,1)}, u32[]{:S(2)}, u32[]{:S(2)}) collective-permute-start(bf16[208,1024]{1,0:T(8,128)(2,1)S(1)} %collective-permute-done.refs_5_), channel_id=1, source_target_pairs={{0,4},{1,5},{2,6},{3,7},{4,0},{5,1},{6,2},{7,3},{8,12},{9,13},{10,... | collective-permute-start | bytes 1277960 | tf_op jit(solution)/shard_map/ppermute | solution.py:23
  28.6 11.6 %copy-start.9 = (bf16[208,1024]{1,0:T(8,128)(2,1)}, bf16[208,1024]{1,0:T(8,128)(2,1)S(1)}, u32[]{:S(2)}) copy-start(bf16[208,1024]{1,0:T(8,128)(2,1)S(1)} %collective-permute-done.6.refs_8_) | copy-start | bytes 1277956
  28.6 10.5 %collective-permute-start.8 = (bf16[208,1024]{1,0:T(8,128)(2,1)S(1)}, bf16[208,1024]{1,0:T(8,128)(2,1)}, u32[]{:S(2)}, u32[]{:S(2)}) collective-permute-start(bf16[208,1024]{1,0:T(8,128)(2,1)S(1)} %collective-permute-done.6.refs_8_), channel_id=1, source_target_pairs={{0,2},{1,3},{2,0},{3,1},{4,6},{5,7},{6,4},{7,5},{8,10},{9,11},{10,... | collective-permute-start | bytes 1277960 | tf_op jit(solution)/shard_map/ppermute | solution.py:23
  28.9 15.5 %copy-start.5 = (s32[4]{0:T(128)S(1)}, s32[4]{0:T(128)}, u32[]{:S(2)}) copy-start(s32[4]{0:T(128)} %lengths.1) | copy-start | bytes 52
  28.9 14.6 %collective-permute-start.2 = (bf16[384,1024]{1,0:T(8,128)(2,1)}, bf16[384,1024]{1,0:T(8,128)(2,1)S(1)}, u32[]{:S(2)}, u32[]{:S(2)}) collective-permute-start(bf16[384,1024]{1,0:T(8,128)(2,1)} %get-tuple-element.37), channel_id=1, source_target_pairs={{0,1},{1,0},{2,3},{3,2},{4,5},{5,4},{6,7},{7,6},{8,9},{9,8},{10,11... | collective-permute-start | bytes 2359304 | tf_op jit(solution)/shard_map/ppermute | solution.py:23
  34.7 18.9 %collective-permute-start.13 = (bf16[128,2048]{1,0:T(8,128)(2,1)S(1)}, bf16[128,2048]{1,0:T(8,128)(2,1)S(1)}, u32[]{:S(2)}, u32[]{:S(2)}) collective-permute-start(bf16[128,2048]{1,0:T(8,128)(2,1)S(1)} %collective-permute-done.9), channel_id=1, source_target_pairs={{8,16},{16,24},{9,17},{17,25},{10,18},{18,26},{11,19},{19,27},{12,... | collective-permute-start | bytes 1572872 | tf_op jit(solution)/shard_map/ppermute | solution.py:245
  35.4 18.2 %collective-permute-start.14 = (bf16[128,2048]{1,0:T(8,128)(2,1)}, bf16[128,2048]{1,0:T(8,128)(2,1)S(1)}, u32[]{:S(2)}, u32[]{:S(2)}) collective-permute-start(bf16[128,2048]{1,0:T(8,128)(2,1)} %collective-permute-done.10), channel_id=1, source_target_pairs={{16,8},{8,0},{17,9},{9,1},{18,10},{10,2},{19,11},{11,3},{20,12},{1... | collective-permute-start | bytes 1572872 | tf_op jit(solution)/shard_map/ppermute | solution.py:246
  40.2 4.2 %copy-start.2 = (bf16[208,1024]{1,0:T(8,128)(2,1)S(1)}, bf16[208,1024]{1,0:T(8,128)(2,1)}, u32[]{:S(2)}) copy-start(bf16[208,1024]{1,0:T(8,128)(2,1)} %copy-done.1) | copy-start | bytes 1277956
  40.3 20.9 %collective-permute-start.11 = (bf16[128,2048]{1,0:T(8,128)(2,1)S(1)}, bf16[128,2048]{1,0:T(8,128)(2,1)S(1)}, u32[]{:S(2)}, u32[]{:S(2)}) collective-permute-start(bf16[128,2048]{1,0:T(8,128)(2,1)S(1)} %pad_maximum_fusion.refs_3_), channel_id=1, source_target_pairs={{0,2},{1,3},{2,0},{3,1},{4,6},{5,7},{6,4},{7,5},{8,10},{9,11},{10,... | collective-permute-start | bytes 1572872 | tf_op jit(solution)/shard_map/ppermute | solution.py:23
  41.9 19.3 %collective-permute-start.12 = (bf16[128,2048]{1,0:T(8,128)(2,1)S(1)}, bf16[128,2048]{1,0:T(8,128)(2,1)S(1)}, u32[]{:S(2)}, u32[]{:S(2)}) collective-permute-start(bf16[128,2048]{1,0:T(8,128)(2,1)S(1)} %pad_maximum_fusion.1.refs_4_), channel_id=1, source_target_pairs={{0,4},{1,5},{2,6},{3,7},{4,0},{5,1},{6,2},{7,3},{8,12},{9,13},{10,... | collective-permute-start | bytes 1572872 | tf_op jit(solution)/shard_map/ppermute | solution.py:23
  43.5 0.9 copy-start.6
  53.6 7.2 %collective-permute-start.15 = (bf16[64,2048]{1,0:T(8,128)(2,1)S(1)}, bf16[64,2048]{1,0:T(8,128)(2,1)S(1)}, u32[]{:S(2)}, u32[]{:S(2)}) collective-permute-start(bf16[64,2048]{1,0:T(8,128)(2,1)S(1)} %get-tuple-element.75.refs_7_), channel_id=1, source_target_pairs={{0,2},{1,3},{2,0},{3,1},{4,6},{5,7},{6,4},{7,5},{8,10},{9,11},{10,... | collective-permute-start | bytes 786440 | tf_op jit(solution)/shard_map/ppermute | solution.py:23
  54.2 7.0 %collective-permute-start.16 = (bf16[64,2048]{1,0:T(8,128)(2,1)S(1)}, bf16[64,2048]{1,0:T(8,128)(2,1)}, u32[]{:S(2)}, u32[]{:S(2)}) collective-permute-start(bf16[64,2048]{1,0:T(8,128)(2,1)S(1)} %get-tuple-element.74.refs_8_), channel_id=1, source_target_pairs={{0,4},{1,5},{2,6},{3,7},{4,0},{5,1},{6,2},{7,3},{8,12},{9,13},{10,... | collective-permute-start | bytes 786440 | tf_op jit(solution)/shard_map/ppermute | solution.py:23
  62.9 2.0 %copy-start = (bf16[128,2048]{1,0:T(8,128)(2,1)S(1)}, bf16[128,2048]{1,0:T(8,128)(2,1)}, u32[]{:S(2)}) copy-start(bf16[128,2048]{1,0:T(8,128)(2,1)} %hidden.1) | copy-start | bytes 1572868
  62.9 2.0 %copy-start.3 = (f32[2048]{0:T(1024)S(1)}, f32[2048]{0:T(1024)}, u32[]{:S(2)}) copy-start(f32[2048]{0:T(1024)} %param.27) | copy-start | bytes 24580
  62.9 2.0 %collective-permute-start.17 = (bf16[128,2048]{1,0:T(8,128)(2,1)S(1)}, bf16[128,2048]{1,0:T(8,128)(2,1)S(1)}, u32[]{:S(2)}, u32[]{:S(2)}) collective-permute-start(bf16[128,2048]{1,0:T(8,128)(2,1)S(1)} %project.3), channel_id=1, source_target_pairs={{0,1},{1,0},{2,3},{3,2},{4,5},{5,4},{6,7},{7,6},{8,9},{9,8},{10,11... | collective-permute-start | bytes 1572872 | tf_op jit(solution)/shard_map/ppermute | solution.py:23
  65.3 10.2 %collective-permute-start.18 = (bf16[128,2048]{1,0:T(8,128)(2,1)S(1)}, bf16[128,2048]{1,0:T(8,128)(2,1)S(1)}, u32[]{:S(2)}, u32[]{:S(2)}) collective-permute-start(bf16[128,2048]{1,0:T(8,128)(2,1)S(1)} %get-tuple-element.48.refs_11_), channel_id=1, source_target_pairs={{0,1},{1,0},{2,3},{3,2},{4,5},{5,4},{6,7},{7,6},{8,9},{9,8},{10,11... | collective-permute-start | bytes 1572872 | tf_op jit(solution)/shard_map/ppermute | solution.py:23
  65.7 15.7 %collective-permute-start.24 = (bf16[128,2048]{1,0:T(8,128)(2,1)S(1)}, bf16[128,2048]{1,0:T(8,128)(2,1)S(1)}, u32[]{:S(2)}, u32[]{:S(2)}) collective-permute-start(bf16[128,2048]{1,0:T(8,128)(2,1)S(1)} %get-tuple-element.48.refs_11_), channel_id=1, source_target_pairs={{0,6},{1,7},{2,4},{3,5},{4,2},{5,3},{6,0},{7,1},{8,14},{9,15},{10,... | collective-permute-start | bytes 1572872 | tf_op jit(solution)/shard_map/ppermute | solution.py:23
  81.4 2.2 %collective-permute-start.25 = (bf16[128,2048]{1,0:T(8,128)(2,1)S(1)}, bf16[128,2048]{1,0:T(8,128)(2,1)S(1)}, u32[]{:S(2)}, u32[]{:S(2)}) collective-permute-start(bf16[128,2048]{1,0:T(8,128)(2,1)S(1)} %collective-permute-done.24.refs_11_), channel_id=1, source_target_pairs={{0,1},{1,0},{2,3},{3,2},{4,5},{5,4},{6,7},{7,6},{8,9},{9,8},{10,11... | collective-permute-start | bytes 1572872 | tf_op jit(solution)/shard_map/ppermute | solution.py:23
  81.5 14.3 %collective-permute-start.20 = (bf16[128,2048]{1,0:T(8,128)(2,1)S(1)}, bf16[128,2048]{1,0:T(8,128)(2,1)S(1)}, u32[]{:S(2)}, u32[]{:S(2)}) collective-permute-start(bf16[128,2048]{1,0:T(8,128)(2,1)S(1)} %get-tuple-element.48.refs_11_), channel_id=1, source_target_pairs={{0,2},{1,3},{2,0},{3,1},{4,6},{5,7},{6,4},{7,5},{8,10},{9,11},{10,... | collective-permute-start | bytes 1572872 | tf_op jit(solution)/shard_map/ppermute | solution.py:23
  82.1 14.1 %collective-permute-start.22 = (bf16[128,2048]{1,0:T(8,128)(2,1)S(1)}, bf16[128,2048]{1,0:T(8,128)(2,1)S(1)}, u32[]{:S(2)}, u32[]{:S(2)}) collective-permute-start(bf16[128,2048]{1,0:T(8,128)(2,1)S(1)} %get-tuple-element.48.refs_11_), channel_id=1, source_target_pairs={{0,4},{1,5},{2,6},{3,7},{4,0},{5,1},{6,2},{7,3},{8,12},{9,13},{10,... | collective-permute-start | bytes 1572872 | tf_op jit(solution)/shard_map/ppermute | solution.py:23
  89.5 6.8 %collective-permute-start.26 = (bf16[1,128,2048]{2,1,0:T(8,128)(2,1)S(1)}, bf16[1,128,2048]{2,1,0:T(8,128)(2,1)S(1)}, u32[]{:S(2)}, u32[]{:S(2)}) collective-permute-start(bf16[1,128,2048]{2,1,0:T(8,128)(2,1)S(1)} %get-tuple-element.65), channel_id=1, source_target_pairs={{0,1},{1,0},{2,3},{3,2},{4,5},{5,4},{6,7},{7,6},{8,9},{9,8},{10,11... | collective-permute-start | bytes 1572872 | tf_op jit(solution)/shard_map/ppermute | solution.py:23
  95.8 3.5 %collective-permute-start.21 = (bf16[128,2048]{1,0:T(8,128)(2,1)S(1)}, bf16[128,2048]{1,0:T(8,128)(2,1)S(1)}, u32[]{:S(2)}, u32[]{:S(2)}) collective-permute-start(bf16[128,2048]{1,0:T(8,128)(2,1)S(1)} %collective-permute-done.20.refs_11_), channel_id=1, source_target_pairs={{0,1},{1,0},{2,3},{3,2},{4,5},{5,4},{6,7},{7,6},{8,9},{9,8},{10,11... | collective-permute-start | bytes 1572872 | tf_op jit(solution)/shard_map/ppermute | solution.py:23
  96.2 3.2 %collective-permute-start.23 = (bf16[128,2048]{1,0:T(8,128)(2,1)S(1)}, bf16[128,2048]{1,0:T(8,128)(2,1)S(1)}, u32[]{:S(2)}, u32[]{:S(2)}) collective-permute-start(bf16[128,2048]{1,0:T(8,128)(2,1)S(1)} %collective-permute-done.22.refs_13_), channel_id=1, source_target_pairs={{0,1},{1,0},{2,3},{3,2},{4,5},{5,4},{6,7},{7,6},{8,9},{9,8},{10,11... | collective-permute-start | bytes 1572872 | tf_op jit(solution)/shard_map/ppermute | solution.py:23
  96.5 9.7 %collective-permute-start.27 = (bf16[64,2048]{1,0:T(8,128)(2,1)S(1)}, bf16[64,2048]{1,0:T(8,128)(2,1)S(1)}, u32[]{:S(2)}, u32[]{:S(2)}) collective-permute-start(bf16[64,2048]{1,0:T(8,128)(2,1)S(1)} %get-tuple-element.77), channel_id=1, source_target_pairs={{0,2},{1,3},{2,0},{3,1},{4,6},{5,7},{6,4},{7,5},{8,10},{9,11},{10,... | collective-permute-start | bytes 786440 | tf_op jit(solution)/shard_map/ppermute | solution.py:23
  97.8 8.5 %collective-permute-start.28 = (bf16[64,2048]{1,0:T(8,128)(2,1)S(1)}, bf16[64,2048]{1,0:T(8,128)(2,1)S(1)}, u32[]{:S(2)}, u32[]{:S(2)}) collective-permute-start(bf16[64,2048]{1,0:T(8,128)(2,1)S(1)} %get-tuple-element.76), channel_id=1, source_target_pairs={{0,4},{1,5},{2,6},{3,7},{4,0},{5,1},{6,2},{7,3},{8,12},{9,13},{10,... | collective-permute-start | bytes 786440 | tf_op jit(solution)/shard_map/ppermute | solution.py:23
  106.3 2.7 %collective-permute-start.29 = (bf16[2,128,2048]{2,1,0:T(8,128)(2,1)S(1)}, bf16[2,128,2048]{2,1,0:T(8,128)(2,1)S(1)}, u32[]{:S(2)}, u32[]{:S(2)}) collective-permute-start(bf16[2,128,2048]{2,1,0:T(8,128)(2,1)S(1)} %get-tuple-element.66), channel_id=1, source_target_pairs={{0,1},{1,0},{2,3},{3,2},{4,5},{5,4},{6,7},{7,6},{8,9},{9,8},{10,11... | collective-permute-start | bytes 3145736 | tf_op jit(solution)/shard_map/ppermute | solution.py:23
  106.4 5.4 %collective-permute-start.19 = (bf16[1,128,2048]{2,1,0:T(8,128)(2,1)S(1)}, bf16[1,128,2048]{2,1,0:T(8,128)(2,1)S(1)}, u32[]{:S(2)}, u32[]{:S(2)}) collective-permute-start(bf16[1,128,2048]{2,1,0:T(8,128)(2,1)S(1)} %get-tuple-element.60), channel_id=1, source_target_pairs={{0,1},{1,0},{2,3},{3,2},{4,5},{5,4},{6,7},{7,6},{8,9},{9,8},{10,11... | collective-permute-start | bytes 1572872 | tf_op jit(solution)/shard_map/ppermute | solution.py:23
  109.7 14.0 %collective-permute-start.31 = (bf16[128,2048]{1,0:T(8,128)(2,1)S(1)}, bf16[128,2048]{1,0:T(8,128)(2,1)S(1)}, u32[]{:S(2)}, u32[]{:S(2)}) collective-permute-start(bf16[128,2048]{1,0:T(8,128)(2,1)S(1)} %pad_maximum_fusion.3), channel_id=1, source_target_pairs={{0,4},{1,5},{2,6},{3,7},{4,0},{5,1},{6,2},{7,3},{8,12},{9,13},{10,... | collective-permute-start | bytes 1572872 | tf_op jit(solution)/shard_map/ppermute | solution.py:23
  111.2 13.8 %collective-permute-start.30 = (bf16[128,2048]{1,0:T(8,128)(2,1)S(1)}, bf16[128,2048]{1,0:T(8,128)(2,1)S(1)}, u32[]{:S(2)}, u32[]{:S(2)}) collective-permute-start(bf16[128,2048]{1,0:T(8,128)(2,1)S(1)} %pad_maximum_fusion.2), channel_id=1, source_target_pairs={{0,2},{1,3},{2,0},{3,1},{4,6},{5,7},{6,4},{7,5},{8,10},{9,11},{10,... | collective-permute-start | bytes 1572872 | tf_op jit(solution)/shard_map/ppermute | solution.py:23

commit v5 on v4

--- a/solution.py
+++ b/solution.py
@@ -141,12 +141,12 @@
 
 
 def chip_attention_body(
-    me, my_prompts, sibling, lengths, columns, parents, accepted, prompts_here, *refs
+    me, my_prompts, sibling, lengths, columns, parents, accepted, prompts_here, got, *refs
 ):
-    copies = [pltpu.make_async_copy(refs[i], refs[16 + i], refs[27].at[i]) for i in range(11)]
+    copies = [pltpu.make_async_copy(refs[i], refs[15 + i], refs[25].at[i]) for i in range(10)]
     for copy in copies:
         copy.start()
-    (attended, cache, ids, gates, bias), (queries_here, tree_keys, tree_values, got, *holders) = refs[11:16], refs[16:27]
+    (attended, cache, ids, gates, bias), (queries_here, tree_keys, tree_values, *holders) = refs[10:15], refs[15:25]
     holders = [prompts_here, *holders]
     rows = tree_keys.shape[0]
     requests = my_prompts.shape[0]
@@ -182,7 +182,7 @@
         gates[index // 2, :, lanes] = first[8:] + second[8:]
 
 
-def chip_attention(scalars, columns, parents, accepted, queries, tree_keys, tree_values, prompts, blocks):
+def chip_attention(scalars, columns, parents, accepted, queries, tree_keys, tree_values, prompts, got, blocks):
     rows, features = tree_keys.shape
     width = columns.shape[1] + 2 * rows
     heads = features // HEAD_DIM // 2
@@ -195,14 +195,14 @@
             everywhere((4, 8, 2 * rows), F32),
             everywhere((4, 8, 2 * rows), F32),
         ),
-        in_specs=[IN_SMEM] * 4 + [IN_VMEM] * 4 + [IN_PLACE] * len(copied),
+        in_specs=[IN_SMEM] * 4 + [IN_VMEM] * 5 + [IN_PLACE] * len(copied),
         out_specs=(IN_VMEM,) * 4,
         scratch_shapes=[pltpu.VMEM((2 * rows, width), F32)]
         + [pltpu.VMEM(part.shape, BF16) for part in copied]
         + [pltpu.SemaphoreType.DMA((len(copied),))],
         compiler_params=pltpu.CompilerParams(vmem_limit_bytes=14 * 2**20),
         name="attention",
-    )(*scalars, columns, parents, accepted, prompts, *copied)
+    )(*scalars, columns, parents, accepted, prompts, got, *copied)
 
 
 def plain_attention_body(
@@ -335,12 +335,8 @@
     return staged[:count], staged[count:]
 
 
-def experts_body(per_pair, local_experts, first_expert, ids, gates, *refs):
+def route_body(local_experts, first_expert, ids, gates, chosen, slot_gates):
     pairs, top, tokens = ids.shape
-    gate_up, down, refs = refs[:local_experts], refs[local_experts : 2 * local_experts], refs[2 * local_experts :]
-    sources = refs[: pairs * per_pair]
-    same_core, other_core, picked, produced, hidden, chosen, slot_gates = refs[pairs * per_pair :]
-    features, units = gate_up[0].shape[0], down[0].shape[0]
     slots = 2 * CAP
     earlier = lax.broadcasted_iota(jnp.int32, (tokens, tokens), 0)
     later = lax.broadcasted_iota(jnp.int32, (tokens, tokens), 1)
@@ -357,10 +353,32 @@
         for expert in range(local_experts):
             place = jnp.where(hits[expert] > 0.5, places[expert : expert + 1], -1.0)
             taken = jnp.where(slot_ids == place, 1.0, 0.0)
-            chosen[pair, expert * slots : (expert + 1) * slots, :] = taken.astype(BF16)
-            slot_gates[expert, pair * slots : (pair + 1) * slots, :] = jnp.sum(
-                taken * shares[expert], axis=1, keepdims=True
-            )
+            rows = slice(expert * slots, (expert + 1) * slots)
+            chosen[pair, rows, :] = taken.astype(BF16)
+            slot_gates[pair, rows, :] = jnp.sum(taken * shares[expert], axis=1, keepdims=True)
+
+
+def route(first_expert, ids, gates, local_experts):
+    pairs, top, tokens = ids.shape
+    rows = local_experts * 2 * CAP
+    return pl.pallas_call(
+        lambda *refs: route_body(local_experts, *refs),
+        out_shape=(everywhere((pairs, rows, tokens), BF16), everywhere((pairs, rows, 1), F32)),
+        in_specs=[IN_SMEM, IN_VMEM, IN_VMEM],
+        out_specs=(IN_VMEM,) * 2,
+        compiler_params=pltpu.CompilerParams(vmem_limit_bytes=24 * 2**20),
+        name="route",
+    )(first_expert, ids, gates)
+
+
+def experts_body(per_pair, local_experts, chosen, slot_gates, *refs):
+    pairs, _, tokens = chosen.shape
+    gate_up, down, refs = refs[:local_experts], refs[local_experts : 2 * local_experts], refs[2 * local_experts :]
+    sources = refs[: pairs * per_pair]
+    same_core, other_core, picked, produced, hidden = refs[pairs * per_pair :]
+    features, units = gate_up[0].shape[0], down[0].shape[0]
+    slots = 2 * CAP
+    for pair in range(pairs):
         group = sources[pair * per_pair : (pair + 1) * per_pair]
         step = 512
         for column in range(0, features, step):
@@ -374,7 +392,13 @@
     for expert in range(local_experts):
         for low in range(0, pairs * slots, chunk):
             rows = picked[expert, low : low + chunk, :]
-            gate_rows = slot_gates[expert, low : low + chunk, :]
+            gate_rows = jnp.concatenate(
+                [
+                    slot_gates[low // slots + inner, expert * slots : (expert + 1) * slots, :]
+                    for inner in range(chunk // slots)
+                ],
+                axis=0,
+            )
             for column in range(0, units, 256):
                 gate = jnp.dot(rows, gate_up[expert][:, column : column + 256], preferred_element_type=F32)
                 up = jnp.dot(
@@ -400,8 +424,8 @@
             other_core[pair, :, column : column + 512] = mixture[tokens // 2 :]
 
 
-def experts(first_expert, ids, gates, gate_up, down, sources, limit, pin=False):
-    pairs, top, tokens = ids.shape
+def experts(chosen, slot_gates, gate_up, down, sources, limit, pin=False):
+    pairs, _, tokens = chosen.shape
     local_experts, (features, _) = len(gate_up), gate_up[0].shape
     units = down[0].shape[0]
     slots = 2 * CAP
@@ -411,21 +435,19 @@
     return pl.pallas_call(
         lambda *refs: experts_body(len(sources) // pairs, local_experts, *refs),
         out_shape=(everywhere((pairs, tokens // 2, features), BF16),) * 2,
-        in_specs=[IN_SMEM] + [IN_VMEM] * (2 + 2 * local_experts + len(sources)),
+        in_specs=[IN_VMEM] * (2 + 2 * local_experts + len(sources)),
         out_specs=(IN_VMEM,) * 2,
         scratch_shapes=[
             pltpu.VMEM((local_experts, pairs * slots, features), BF16),
             pltpu.VMEM((pairs, local_experts * slots, features), BF16),
             pltpu.VMEM((pairs * slots, units), BF16),
-            pltpu.VMEM((pairs, local_experts * slots, tokens), BF16),
-            pltpu.VMEM((local_experts, pairs * slots, 1), F32),
         ],
         compiler_params=pltpu.CompilerParams(vmem_limit_bytes=limit),
         cost_estimate=pl.CostEstimate(
             flops=12 * local_experts * pairs * slots * features * units, bytes_accessed=16 * 2**20, transcendentals=0
         ),
         name="experts",
-    )(first_expert, ids, gates, *matrices, *sources)
+    )(chosen, slot_gates, *matrices, *sources)
 
 
 def add_rows(left, right):
@@ -463,7 +485,7 @@
     chip_parents = jnp.where(chip_parents < 0, -1, chip_parents + first_node).reshape(-1, 1)
     attended, cache, ids, gates = chip_attention(
         (me.reshape(1), request_prompt, sibling, prompt_lengths), columns, chip_parents, accepted,
-        tree_queries, tree_keys, tree_values, prompts, (got, theirs, x_mine, x_theirs, y_mine, y_theirs, far_a, far_b),
+        tree_queries, tree_keys, tree_values, prompts, got, (theirs, x_mine, x_theirs, y_mine, y_theirs, far_a, far_b),
     )
     up, down_rows = after((up, down_rows), attended)
     edge = up.shape[0] // 2
@@ -471,18 +493,19 @@
         jnp.where(lax.axis_index("rep") >= 2, up[rows], down_rows[rows]) for rows in (slice(0, edge), slice(edge, None))
     ]
     weights += [last_first, last_second, flip(last_first, 2, 8), flip(last_second, 4, 8)]
+    chosen, slot_gates = route((me * gate_up.shape[0]).reshape(1), after(ids, last_first), gates, gate_up.shape[0])
+    attended = after(attended, chosen)
     other = flip(chip_project(order, attended, weights, pieces, tok_rows, BF16), 1, 8)
     mine = chip_project(order, attended, weights, pieces, 0, F32)
     residual, normed = norm(hidden_in, mine, other, gain)
 
     across, from_x, from_y = flip(normed, 6, 8), flip(normed, 2, 8), flip(normed, 4, 8)
     sibling_rows = flip(normed, 1, 8)
-    first_expert = (me * gate_up.shape[0]).reshape(1)
     gate_up, down = stage(*after((gate_up, down), normed))
 
     def run(low, high, sources, megabytes, *done):
         return experts(
-            first_expert, after(ids[low:high], done), gates[low:high], gate_up, down, sources, megabytes * 2**20, True
+            after(chosen[low:high], done), slot_gates[low:high], gate_up, down, sources, megabytes * 2**20, True
         )
 
     near_same, near_other = run(0, 1, [normed, sibling_rows], 12)
@@ -526,8 +549,9 @@
     top = expert_ids.shape[1]
     everyone = lax.all_gather(normed, "ep", axis=0, tiled=True)
     sources = [everyone[i * 2 * tok_rows : (i + 1) * 2 * tok_rows] for i in range(ep_size // 2)]
+    slots = route((me * gate_up.shape[0]).reshape(1), routing[:, :top], routing[:, top:], gate_up.shape[0])
     same_core, other_core = experts(
-        (me * gate_up.shape[0]).reshape(1), routing[:, :top], routing[:, top:], list(gate_up), list(down), sources,
+        *slots, list(gate_up), list(down), sources,
         VMEM_LIMIT
     )
     shares = jnp.stack([same_core, other_core], axis=1).reshape(ep_size, tok_rows, features)

time: 126 us -> 126 us (level)
  no operation moved by 1% of the time
where the time goes in v5:
time: 126 us
  waiting for transfers between devices  49.4 us (39%)
  Pallas kernels  42.5 us (34%)
  starting transfers between devices  27 us (21%)
  local copies, waits for them, and re-layouts  3.2 us (3%)
  other arithmetic  2.38 us (2%)
    ppermute x28, waiting for transfers between devices, flip(): return lax.ppermute(value, 'ep', [(i, i ^ bits) for i in range(size)])  43 us
    ppermute x28, starting transfers between devices, flip(): return lax.ppermute(value, 'ep', [(i, i ^ bits) for i in range(size)])  21.4 us
    pallas_call x3, Pallas kernels, experts(): pl.pallas_call(lambda *refs: experts_body(len(sources) // pairs, local_ex...  18 us
    pallas_call x1, Pallas kernels, chip_attention(): pl.pallas_call(chip_attention_body, out_shape=(everywhere((heads, 2 * row...  8.89 us
    pallas_call x1, Pallas kernels, stage(): pl.pallas_call(stage_body, out_shape=[pltpu.VMEM(gate_up.shape[1:], BF16)...  8.32 us
    ppermute x2, waiting for transfers between devices, shifted(): return lax.ppermute(value, 'rep', [(i, (i + by) % 4) for i in range(4)])  6.41 us
    ppermute x2, starting transfers between devices, shifted(): return lax.ppermute(value, 'rep', [(i, (i + by) % 4) for i in range(4)])  3.6 us
    pallas_call x2, Pallas kernels, chip_project(): pl.pallas_call(lambda *refs: chip_project_body(pieces, low_row, *refs), o...  3.43 us
  transfers between devices with their start and end apart: 32, of which 14 were waited for; matrix products, arithmetic and copies ran while one was open for 3% of the time, Pallas kernels for 30%

profile of v5, /device:TPU:0, one launch (start us, length us, event | category | flops | bytes accessed | tf_op | source)
XLA Modules:
  0.0 125.6 jit_solution(10147762835483345527)
XLA Ops:
  0.7 3.0 %pack.1 = (bf16[384,1024]{1,0:T(8,128)(2,1)}, bf16[208,1024]{1,0:T(8,128)(2,1)S(1)}, bf16[208,1024]{1,0:T(8,128)(2,1)S(1)}, bf16[128,2048]{1,0:T(8,128)(2,1)S(1)}) custom-call(s32[1]{0:T(128)} %bitcast.8.place.me, bf16[128,2048]{1,0:T(8,128)(2,1)} %refs_0_.3, bf16[128,2048]{1,0:T(8,128)(2,1)} %refs_1_.3, bf16[128,2048]{1,0:T(8,128)(2,1)} %refs_2_.3, ...), custom_call_target="tpu_custom_call" | custom-call | tf_op jit(solution)/shard_map/pack/pallas_call | solution.py:92
  3.7 0.5 collective-permute-start.3
  4.2 2.6 %collective-permute-start = (bf16[208,1024]{1,0:T(8,128)(2,1)S(1)}, bf16[208,1024]{1,0:T(8,128)(2,1)S(1)}, u32[]{:S(2)}, u32[]{:S(2)}) collective-permute-start(bf16[208,1024]{1,0:T(8,128)(2,1)S(1)} %get-tuple-element.39.prompts_here), channel_id=1, source_target_pairs={{0,2},{1,3},{2,0},{3,1},{4,6},{5,7},{6,4},{7,5},{8,10},{9,11},{10,... | collective-permute-start | bytes 1277960 | tf_op jit(solution)/shard_map/ppermute | solution.py:23
  6.8 1.5 %collective-permute-start.5 = (bf16[208,1024]{1,0:T(8,128)(2,1)S(1)}, bf16[208,1024]{1,0:T(8,128)(2,1)S(1)}, u32[]{:S(2)}, u32[]{:S(2)}) collective-permute-start(bf16[208,1024]{1,0:T(8,128)(2,1)S(1)} %get-tuple-element.39.prompts_here), channel_id=1, source_target_pairs={{0,4},{1,5},{2,6},{3,7},{4,0},{5,1},{6,2},{7,3},{8,12},{9,13},{10,... | collective-permute-start | bytes 1277960 | tf_op jit(solution)/shard_map/ppermute | solution.py:23
  8.3 3.6 %collective-permute-start.11 = (bf16[128,2048]{1,0:T(8,128)(2,1)S(1)}, bf16[128,2048]{1,0:T(8,128)(2,1)}, u32[]{:S(2)}, u32[]{:S(2)}) collective-permute-start(bf16[128,2048]{1,0:T(8,128)(2,1)S(1)} %get-tuple-element.45), channel_id=1, source_target_pairs={{0,24},{8,0},{16,8},{24,16},{1,25},{9,1},{17,9},{25,17},{2,26},{10... | collective-permute-start | bytes 1572872 | tf_op jit(solution)/shard_map/ppermute | solution.py:242
  12.1 0.6 collective-permute-start.6
  12.8 4.4 %collective-permute-done.refs_4_ = bf16[208,1024]{1,0:T(8,128)(2,1)S(1)} collective-permute-done((bf16[208,1024]{1,0:T(8,128)(2,1)S(1)}, bf16[208,1024]{1,0:T(8,128)(2,1)S(1)}, u32[]{:S(2)}, u32[]{:S(2)}) %collective-permute-start) | collective-permute-done | bytes 426016 | tf_op jit(solution)/shard_map/ppermute | solution.py:23
  17.3 2.2 %collective-permute-done.5.refs_6_ = bf16[208,1024]{1,0:T(8,128)(2,1)S(1)} collective-permute-done((bf16[208,1024]{1,0:T(8,128)(2,1)S(1)}, bf16[208,1024]{1,0:T(8,128)(2,1)S(1)}, u32[]{:S(2)}, u32[]{:S(2)}) %collective-permute-start.5) | collective-permute-done | bytes 426016 | tf_op jit(solution)/shard_map/ppermute | solution.py:23
  19.4 1.5 %collective-permute-start.7 = (bf16[208,1024]{1,0:T(8,128)(2,1)S(1)}, bf16[208,1024]{1,0:T(8,128)(2,1)S(1)}, u32[]{:S(2)}, u32[]{:S(2)}) collective-permute-start(bf16[208,1024]{1,0:T(8,128)(2,1)S(1)} %collective-permute-done.refs_4_), channel_id=1, source_target_pairs={{0,4},{1,5},{2,6},{3,7},{4,0},{5,1},{6,2},{7,3},{8,12},{9,13},{10,... | collective-permute-start | bytes 1277960 | tf_op jit(solution)/shard_map/ppermute | solution.py:23
  21.0 0.5 collective-permute-start.4
  21.5 7.1 %collective-permute-done.6.refs_7_ = bf16[208,1024]{1,0:T(8,128)(2,1)S(1)} collective-permute-done((bf16[208,1024]{1,0:T(8,128)(2,1)S(1)}, bf16[208,1024]{1,0:T(8,128)(2,1)S(1)}, u32[]{:S(2)}, u32[]{:S(2)}) %collective-permute-start.6) | collective-permute-done | bytes 426016 | tf_op jit(solution)/shard_map/ppermute | solution.py:23
  29.0 6.4 %collective-permute-done.9 = bf16[128,2048]{1,0:T(8,128)(2,1)} collective-permute-done((bf16[128,2048]{1,0:T(8,128)(2,1)S(1)}, bf16[128,2048]{1,0:T(8,128)(2,1)}, u32[]{:S(2)}, u32[]{:S(2)}) %collective-permute-start.9) | collective-permute-done | bytes 524320 | tf_op jit(solution)/shard_map/ppermute | solution.py:242
  35.4 0.7 collective-permute-start.10
  36.1 0.9 collective-permute-done.7.refs_8_
  36.9 1.3 %collective-permute-start.12 = (bf16[128,2048]{1,0:T(8,128)(2,1)}, bf16[128,2048]{1,0:T(8,128)(2,1)S(1)}, u32[]{:S(2)}, u32[]{:S(2)}) collective-permute-start(bf16[128,2048]{1,0:T(8,128)(2,1)} %collective-permute-done.11), channel_id=1, source_target_pairs={{16,8},{8,0},{17,9},{9,1},{18,10},{10,2},{19,11},{11,3},{20,12},{1... | collective-permute-start | bytes 1572872 | tf_op jit(solution)/shard_map/ppermute | solution.py:246
  38.2 2.1 %collective-permute-done.8.refs_9_ = bf16[208,1024]{1,0:T(8,128)(2,1)} collective-permute-done((bf16[208,1024]{1,0:T(8,128)(2,1)S(1)}, bf16[208,1024]{1,0:T(8,128)(2,1)}, u32[]{:S(2)}, u32[]{:S(2)}) %collective-permute-start.8) | collective-permute-done | bytes 426016 | tf_op jit(solution)/shard_map/ppermute | solution.py:23
  40.4 1.3 %fusion.10 = (bf16[64,2048]{1,0:T(8,128)(2,1)S(1)}, bf16[64,2048]{1,0:T(8,128)(2,1)S(1)}, bf16[64,2048]{1,0:T(8,128)(2,1)S(1)}, bf16[64,2048]{1,0:T(8,128)(2,1)S(1)}) fusion(bf16[128,2048]{1,0:T(8,128)(2,1)} %collective-permute-done.9, bf16[128,2048]{1,0:T(8,128)(2,1)} %collective-permute-done.11), kind=kLoop, calls=%fused_computation.41 | loop fusion | bytes 2097152 | tf_op jit(solution)/shard_map/slice | solution.py:254
  41.7 1.0 collective-permute-start.14
  42.7 1.6 %collective-permute-start.13 = (bf16[128,2048]{1,0:T(8,128)(2,1)S(1)}, bf16[128,2048]{1,0:T(8,128)(2,1)S(1)}, u32[]{:S(2)}, u32[]{:S(2)}) collective-permute-start(bf16[128,2048]{1,0:T(8,128)(2,1)S(1)} %pad_maximum_fusion.refs_3_), channel_id=1, source_target_pairs={{0,2},{1,3},{2,0},{3,1},{4,6},{5,7},{6,4},{7,5},{8,10},{9,11},{10,... | collective-permute-start | bytes 1572872 | tf_op jit(solution)/shard_map/ppermute | solution.py:23
  44.3 8.9 %attention.1 = (bf16[8,256,128]{2,1,0:T(8,128)(2,1)S(1)}, bf16[32,4096]{1,0:T(8,128)(2,1)}, f32[4,8,256]{2,1,0:T(8,128)S(1)}, f32[4,8,256]{2,1,0:T(8,128)S(1)}) custom-call(s32[1]{0:T(128)} %bitcast.8.place.me, s32[2]{0:T(128)S(1)} %copy-done.4, s32[4,64]{1,0:T(4,128)S(1)} %collective-permute-done.1.sibling, s32[4]{0:T(128)S(1)} %copy-done.5, ...), custom_call_target="tpu_custom_call" | custom-call | tf_op jit(solution)/shard_map/attention/pallas_call | solution.py:190
  53.3 0.6 collective-permute-start.15
  53.9 1.1 collective-permute-start.16
  55.1 1.3 %constant_dynamic-slice_fusion.refs_2_ = bf16[256,2048]{1,0:T(8,128)(2,1)S(1)} fusion(bf16[512,2048]{1,0:T(8,128)(2,1)} %refs_7_.1, s32[]{:T(128)S(6)} %select_n.120), kind=kLoop, calls=%fused_computation.37 | loop fusion | bytes 2097156 | tf_op jit(solution)/shard_map/dynamic_slice | solution.py:239
  56.4 0.4 route.1
  56.8 4.2 %collective-permute-done.15.refs_9_ = bf16[64,2048]{1,0:T(8,128)(2,1)S(1)} collective-permute-done((bf16[64,2048]{1,0:T(8,128)(2,1)S(1)}, bf16[64,2048]{1,0:T(8,128)(2,1)S(1)}, u32[]{:S(2)}, u32[]{:S(2)}) %collective-permute-start.15) | collective-permute-done | bytes 262176 | tf_op jit(solution)/shard_map/ppermute | solution.py:23
  61.1 1.7 %project.3 = bf16[128,2048]{1,0:T(8,128)(2,1)S(1)} custom-call(s32[8]{0:T(128)S(1)} %stack.41.refs_0_, bf16[8,256,128]{2,1,0:T(8,128)(2,1)S(1)} %get-tuple-element.51.refs_1_, bf16[256,2048]{1,0:T(8,128)(2,1)S(1)} %constant_dynamic-slice_fusion.refs_2_, bf16[128,2048]{1,0:T(8,128)(2,1)S(1)} %pad_maximum_fusion.refs_3_, ...), custom_call_target="tpu_custom_call" | custom-call | tf_op jit(solution)/shard_map/project/pallas_call | solution.py:281
  62.9 1.7 %project.2.mine = f32[128,2048]{1,0:T(8,128)S(1)} custom-call(s32[8]{0:T(128)S(1)} %stack.41.refs_0_, bf16[8,256,128]{2,1,0:T(8,128)(2,1)S(1)} %get-tuple-element.51.refs_1_, bf16[256,2048]{1,0:T(8,128)(2,1)S(1)} %constant_dynamic-slice_fusion.refs_2_, bf16[128,2048]{1,0:T(8,128)(2,1)S(1)} %pad_maximum_fusion.refs_3_, ...), custom_call_target="tpu_custom_call" | custom-call | tf_op jit(solution)/shard_map/project/pallas_call | solution.py:281
  64.8 0.4 norm.1
  65.2 0.4 collective-permute-start.18
  65.6 1.5 %collective-permute-start.24 = (bf16[128,2048]{1,0:T(8,128)(2,1)S(1)}, bf16[128,2048]{1,0:T(8,128)(2,1)S(1)}, u32[]{:S(2)}, u32[]{:S(2)}) collective-permute-start(bf16[128,2048]{1,0:T(8,128)(2,1)S(1)} %get-tuple-element.56.refs_10_), channel_id=1, source_target_pairs={{0,6},{1,7},{2,4},{3,5},{4,2},{5,3},{6,0},{7,1},{8,14},{9,15},{10,... | collective-permute-start | bytes 1572872 | tf_op jit(solution)/shard_map/ppermute | solution.py:23
  67.2 8.3 %stage.1 = (bf16[2048,1024]{1,0:T(8,128)(2,1)S(1)}, bf16[2048,1024]{1,0:T(8,128)(2,1)S(1)}, bf16[2048,1024]{1,0:T(8,128)(2,1)S(1)}, bf16[2048,1024]{1,0:T(8,128)...) custom-call(bf16[4,2048,1024]{2,1,0:T(8,128)(2,1)} %gate_up, ...), custom_call_target="tpu_custom_call" | custom-call | bytes 25165824 | tf_op jit(solution)/shard_map/stage/pallas_call | solution.py:325
  75.6 5.9 %experts.3 = (bf16[1,128,2048]{2,1,0:T(8,128)(2,1)S(1)}, bf16[1,128,2048]{2,1,0:T(8,128)(2,1)S(1)}) custom-call(bf16[1,320,256]{2,1,0:T(8,128)(2,1)S(1)} %get-tuple-element.86.refs_0_, f32[1,320,1]{2,1,0:T(8,128)S(1)} %get-tuple-element.84.refs_1_, bf16[2048,1024]{1,0:T(8,128)(2,1)S(1)} %get-tuple-element.59.refs_2_, ...), custom_call_target="tpu_custom_call" | custom-call | flops 4026531840 | bytes 16777216 | tf_op jit(solution)/shard_map/experts/pallas_call | solution.py:435
  81.5 1.0 collective-permute-start.20
  82.5 1.1 collective-permute-start.22
  83.6 5.7 %experts.5 = (bf16[1,128,2048]{2,1,0:T(8,128)(2,1)S(1)}, bf16[1,128,2048]{2,1,0:T(8,128)(2,1)S(1)}) custom-call(bf16[1,320,256]{2,1,0:T(8,128)(2,1)S(1)} %get-tuple-element.87.refs_0_, f32[1,320,1]{2,1,0:T(8,128)S(1)} %get-tuple-element.85.refs_1_, bf16[2048,1024]{1,0:T(8,128)(2,1)S(1)} %get-tuple-element.59.refs_2_, ...), custom_call_target="tpu_custom_call" | custom-call | flops 4026531840 | bytes 16777216 | tf_op jit(solution)/shard_map/experts/pallas_call | solution.py:435
  89.4 6.4 %collective-permute-done.20.refs_10_ = bf16[128,2048]{1,0:T(8,128)(2,1)S(1)} collective-permute-done((bf16[128,2048]{1,0:T(8,128)(2,1)S(1)}, bf16[128,2048]{1,0:T(8,128)(2,1)S(1)}, u32[]{:S(2)}, u32[]{:S(2)}) %collective-permute-start.20) | collective-permute-done | bytes 524320 | tf_op jit(solution)/shard_map/ppermute | solution.py:23
  95.8 0.6 collective-permute-done.22.refs_12_
  96.7 1.2 collective-permute-start.27
  97.8 1.7 %collective-permute-start.28 = (bf16[64,2048]{1,0:T(8,128)(2,1)S(1)}, bf16[64,2048]{1,0:T(8,128)(2,1)S(1)}, u32[]{:S(2)}, u32[]{:S(2)}) collective-permute-start(bf16[64,2048]{1,0:T(8,128)(2,1)S(1)} %get-tuple-element.88), channel_id=1, source_target_pairs={{0,4},{1,5},{2,6},{3,7},{4,0},{5,1},{6,2},{7,3},{8,12},{9,13},{10,... | collective-permute-start | bytes 786440 | tf_op jit(solution)/shard_map/ppermute | solution.py:23
  99.6 6.4 %experts.4 = (bf16[2,128,2048]{2,1,0:T(8,128)(2,1)S(1)}, bf16[2,128,2048]{2,1,0:T(8,128)(2,1)S(1)}) custom-call(bf16[2,320,256]{2,1,0:T(8,128)(2,1)S(1)} %slice.82.refs_0_, f32[2,320,1]{2,1,0:T(8,128)S(1)} %slice.83.refs_1_, bf16[2048,1024]{1,0:T(8,128)(2,1)S(1)} %get-tuple-element.59.refs_2_, bf16[2048,1024]{1,0:T(8,128)(2,1)S(1)} %get-tuple-element.60.refs_3_, ...), custom_call_target="tpu_custom_call" | custom-call | flops 8053063680 | bytes 16777216 | tf_op jit(solution)/shard_map/experts/pallas_call | solution.py:435
  106.3 0.5 collective-permute-start.19
  106.8 2.1 %collective-permute-done.29 = bf16[2,128,2048]{2,1,0:T(8,128)(2,1)S(1)} collective-permute-done((bf16[2,128,2048]{2,1,0:T(8,128)(2,1)S(1)}, bf16[2,128,2048]{2,1,0:T(8,128)(2,1)S(1)}, u32[]{:S(2)}, u32[]{:S(2)}) %collective-permute-start.29) | collective-permute-done | bytes 1048608 | tf_op jit(solution)/shard_map/ppermute | solution.py:23
  108.9 0.4 convert_add_fusion
  109.6 1.0 collective-permute-start.30
  110.6 1.2 collective-permute-start.31
  111.9 11.8 %collective-permute-done.30 = bf16[128,2048]{1,0:T(8,128)(2,1)S(1)} collective-permute-done((bf16[128,2048]{1,0:T(8,128)(2,1)S(1)}, bf16[128,2048]{1,0:T(8,128)(2,1)S(1)}, u32[]{:S(2)}, u32[]{:S(2)}) %collective-permute-start.30) | collective-permute-done | bytes 524320 | tf_op jit(solution)/shard_map/ppermute | solution.py:23
  123.6 0.7 collective-permute-done.31
  124.4 1.2 fusion.2
  (82 shorter events, 2.1 us)
Async XLA Ops:
  0.6 11.3 %copy-start.4 = (s32[2]{0:T(128)S(1)}, s32[2]{0:T(128)}, u32[]{:S(2)}) copy-start(s32[2]{0:T(128)} %my_prompts.1) | copy-start | bytes 28
  0.6 11.3 %copy-start.11 = (s32[2,64]{1,0:T(2,128)S(1)}, s32[2,64]{1,0:T(2,128)}, u32[]{:S(2)}) copy-start(s32[2,64]{1,0:T(2,128)} %param.20) | copy-start | bytes 1540
  0.7 12.0 %copy-start.12 = (s32[2,16]{1,0:T(2,128)S(1)}, s32[2,16]{1,0:T(2,128)}, u32[]{:S(2)}) copy-start(s32[2,16]{1,0:T(2,128)} %param.21) | copy-start | bytes 388
  3.7 37.9 %copy-start.1 = (bf16[208,1024]{1,0:T(8,128)(2,1)}, bf16[208,1024]{1,0:T(8,128)(2,1)S(1)}, u32[]{:S(2)}) copy-start(bf16[208,1024]{1,0:T(8,128)(2,1)S(1)} %get-tuple-element.39.prompts_here) | copy-start | bytes 1277956
  3.7 8.4 %collective-permute-start.3 = (bf16[208,1024]{1,0:T(8,128)(2,1)S(1)}, bf16[208,1024]{1,0:T(8,128)(2,1)S(1)}, u32[]{:S(2)}, u32[]{:S(2)}) collective-permute-start(bf16[208,1024]{1,0:T(8,128)(2,1)S(1)} %get-tuple-element.42), channel_id=1, source_target_pairs={{0,1},{1,0},{2,3},{3,2},{4,5},{5,4},{6,7},{7,6},{8,9},{9,8},{10,11... | collective-permute-start | bytes 1277960 | tf_op jit(solution)/shard_map/ppermute | solution.py:23
  4.2 13.0 %collective-permute-start = (bf16[208,1024]{1,0:T(8,128)(2,1)S(1)}, bf16[208,1024]{1,0:T(8,128)(2,1)S(1)}, u32[]{:S(2)}, u32[]{:S(2)}) collective-permute-start(bf16[208,1024]{1,0:T(8,128)(2,1)S(1)} %get-tuple-element.39.prompts_here), channel_id=1, source_target_pairs={{0,2},{1,3},{2,0},{3,1},{4,6},{5,7},{6,4},{7,5},{8,10},{9,11},{10,... | collective-permute-start | bytes 1277960 | tf_op jit(solution)/shard_map/ppermute | solution.py:23
  6.8 12.7 %collective-permute-start.5 = (bf16[208,1024]{1,0:T(8,128)(2,1)S(1)}, bf16[208,1024]{1,0:T(8,128)(2,1)S(1)}, u32[]{:S(2)}, u32[]{:S(2)}) collective-permute-start(bf16[208,1024]{1,0:T(8,128)(2,1)S(1)} %get-tuple-element.39.prompts_here), channel_id=1, source_target_pairs={{0,4},{1,5},{2,6},{3,7},{4,0},{5,1},{6,2},{7,3},{8,12},{9,13},{10,... | collective-permute-start | bytes 1277960 | tf_op jit(solution)/shard_map/ppermute | solution.py:23
  8.3 20.6 %collective-permute-start.11 = (bf16[128,2048]{1,0:T(8,128)(2,1)S(1)}, bf16[128,2048]{1,0:T(8,128)(2,1)}, u32[]{:S(2)}, u32[]{:S(2)}) collective-permute-start(bf16[128,2048]{1,0:T(8,128)(2,1)S(1)} %get-tuple-element.45), channel_id=1, source_target_pairs={{0,24},{8,0},{16,8},{24,16},{1,25},{9,1},{17,9},{25,17},{2,26},{10... | collective-permute-start | bytes 1572872 | tf_op jit(solution)/shard_map/ppermute | solution.py:242
  11.9 23.5 %collective-permute-start.9 = (bf16[128,2048]{1,0:T(8,128)(2,1)S(1)}, bf16[128,2048]{1,0:T(8,128)(2,1)}, u32[]{:S(2)}, u32[]{:S(2)}) collective-permute-start(bf16[128,2048]{1,0:T(8,128)(2,1)S(1)} %get-tuple-element.45), channel_id=1, source_target_pairs={{0,8},{8,16},{16,24},{24,0},{1,9},{9,17},{17,25},{25,1},{2,10},{10... | collective-permute-start | bytes 1572872 | tf_op jit(solution)/shard_map/ppermute | solution.py:242
  12.1 26.1 %copy-start.6 = (bf16[208,1024]{1,0:T(8,128)(2,1)}, bf16[208,1024]{1,0:T(8,128)(2,1)S(1)}, u32[]{:S(2)}) copy-start(bf16[208,1024]{1,0:T(8,128)(2,1)S(1)} %collective-permute-done.3.refs_3_) | copy-start | bytes 1277956
  12.1 16.4 %collective-permute-start.6 = (bf16[208,1024]{1,0:T(8,128)(2,1)S(1)}, bf16[208,1024]{1,0:T(8,128)(2,1)S(1)}, u32[]{:S(2)}, u32[]{:S(2)}) collective-permute-start(bf16[208,1024]{1,0:T(8,128)(2,1)S(1)} %collective-permute-done.3.refs_3_), channel_id=1, source_target_pairs={{0,4},{1,5},{2,6},{3,7},{4,0},{5,1},{6,2},{7,3},{8,12},{9,13},{10,... | collective-permute-start | bytes 1277960 | tf_op jit(solution)/shard_map/ppermute | solution.py:23
  17.2 21.0 %copy-start.7 = (bf16[208,1024]{1,0:T(8,128)(2,1)}, bf16[208,1024]{1,0:T(8,128)(2,1)S(1)}, u32[]{:S(2)}) copy-start(bf16[208,1024]{1,0:T(8,128)(2,1)S(1)} %collective-permute-done.refs_4_) | copy-start | bytes 1277956
  17.2 3.8 %collective-permute-start.1 = (s32[4,64]{1,0:T(4,128)S(1)}, s32[4,64]{1,0:T(4,128)S(1)}, u32[]{:S(2)}, u32[]{:S(2)}) collective-permute-start(s32[4,64]{1,0:T(4,128)S(1)} %pad_add_fusion.2), channel_id=1, source_target_pairs={{0,1},{1,0},{2,3},{3,2},{4,5},{5,4},{6,7},{7,6},{8,9},{9,8},{10,11... | collective-permute-start | bytes 3080 | tf_op jit(solution)/shard_map/ppermute | solution.py:23
  19.4 9.2 %copy-start.8 = (bf16[208,1024]{1,0:T(8,128)(2,1)}, bf16[208,1024]{1,0:T(8,128)(2,1)S(1)}, u32[]{:S(2)}) copy-start(bf16[208,1024]{1,0:T(8,128)(2,1)S(1)} %collective-permute-done.5.refs_6_) | copy-start | bytes 1277956
  19.4 17.5 %collective-permute-start.7 = (bf16[208,1024]{1,0:T(8,128)(2,1)S(1)}, bf16[208,1024]{1,0:T(8,128)(2,1)S(1)}, u32[]{:S(2)}, u32[]{:S(2)}) collective-permute-start(bf16[208,1024]{1,0:T(8,128)(2,1)S(1)} %collective-permute-done.refs_4_), channel_id=1, source_target_pairs={{0,4},{1,5},{2,6},{3,7},{4,0},{5,1},{6,2},{7,3},{8,12},{9,13},{10,... | collective-permute-start | bytes 1277960 | tf_op jit(solution)/shard_map/ppermute | solution.py:23
  21.0 17.3 %collective-permute-start.4 = (bf16[208,1024]{1,0:T(8,128)(2,1)S(1)}, bf16[208,1024]{1,0:T(8,128)(2,1)}, u32[]{:S(2)}, u32[]{:S(2)}) collective-permute-start(bf16[208,1024]{1,0:T(8,128)(2,1)S(1)} %collective-permute-done.3.refs_3_), channel_id=1, source_target_pairs={{0,2},{1,3},{2,0},{3,1},{4,6},{5,7},{6,4},{7,5},{8,10},{9,11},{10,... | collective-permute-start | bytes 1277960 | tf_op jit(solution)/shard_map/ppermute | solution.py:23
  28.6 13.1 %copy-start.9 = (bf16[208,1024]{1,0:T(8,128)(2,1)}, bf16[208,1024]{1,0:T(8,128)(2,1)S(1)}, u32[]{:S(2)}) copy-start(bf16[208,1024]{1,0:T(8,128)(2,1)S(1)} %collective-permute-done.6.refs_7_) | copy-start | bytes 1277956
  28.6 11.8 %collective-permute-start.8 = (bf16[208,1024]{1,0:T(8,128)(2,1)S(1)}, bf16[208,1024]{1,0:T(8,128)(2,1)}, u32[]{:S(2)}, u32[]{:S(2)}) collective-permute-start(bf16[208,1024]{1,0:T(8,128)(2,1)S(1)} %collective-permute-done.6.refs_7_), channel_id=1, source_target_pairs={{0,2},{1,3},{2,0},{3,1},{4,6},{5,7},{6,4},{7,5},{8,10},{9,11},{10,... | collective-permute-start | bytes 1277960 | tf_op jit(solution)/shard_map/ppermute | solution.py:23
  28.9 15.4 %copy-start.5 = (s32[4]{0:T(128)S(1)}, s32[4]{0:T(128)}, u32[]{:S(2)}) copy-start(s32[4]{0:T(128)} %lengths.1) | copy-start | bytes 52
  28.9 15.4 %collective-permute-start.2 = (bf16[384,1024]{1,0:T(8,128)(2,1)}, bf16[384,1024]{1,0:T(8,128)(2,1)S(1)}, u32[]{:S(2)}, u32[]{:S(2)}) collective-permute-start(bf16[384,1024]{1,0:T(8,128)(2,1)} %get-tuple-element.41), channel_id=1, source_target_pairs={{0,1},{1,0},{2,3},{3,2},{4,5},{5,4},{6,7},{7,6},{8,9},{9,8},{10,11... | collective-permute-start | bytes 2359304 | tf_op jit(solution)/shard_map/ppermute | solution.py:23
  35.4 17.8 %collective-permute-start.10 = (bf16[128,2048]{1,0:T(8,128)(2,1)}, bf16[128,2048]{1,0:T(8,128)(2,1)S(1)}, u32[]{:S(2)}, u32[]{:S(2)}) collective-permute-start(bf16[128,2048]{1,0:T(8,128)(2,1)} %collective-permute-done.9), channel_id=1, source_target_pairs={{8,16},{16,24},{9,17},{17,25},{10,18},{18,26},{11,19},{19,27},{12,... | collective-permute-start | bytes 1572872 | tf_op jit(solution)/shard_map/ppermute | solution.py:245
  36.9 4.7 %copy-start.10 = (bf16[208,1024]{1,0:T(8,128)(2,1)}, bf16[208,1024]{1,0:T(8,128)(2,1)S(1)}, u32[]{:S(2)}) copy-start(bf16[208,1024]{1,0:T(8,128)(2,1)S(1)} %collective-permute-done.7.refs_8_) | copy-start | bytes 1277956
  36.9 16.3 %collective-permute-start.12 = (bf16[128,2048]{1,0:T(8,128)(2,1)}, bf16[128,2048]{1,0:T(8,128)(2,1)S(1)}, u32[]{:S(2)}, u32[]{:S(2)}) collective-permute-start(bf16[128,2048]{1,0:T(8,128)(2,1)} %collective-permute-done.11), channel_id=1, source_target_pairs={{16,8},{8,0},{17,9},{9,1},{18,10},{10,2},{19,11},{11,3},{20,12},{1... | collective-permute-start | bytes 1572872 | tf_op jit(solution)/shard_map/ppermute | solution.py:246
  41.7 2.7 %copy-start.2 = (bf16[208,1024]{1,0:T(8,128)(2,1)S(1)}, bf16[208,1024]{1,0:T(8,128)(2,1)}, u32[]{:S(2)}) copy-start(bf16[208,1024]{1,0:T(8,128)(2,1)} %copy-done.1) | copy-start | bytes 1277956
  41.7 19.4 %collective-permute-start.14 = (bf16[128,2048]{1,0:T(8,128)(2,1)S(1)}, bf16[128,2048]{1,0:T(8,128)(2,1)S(1)}, u32[]{:S(2)}, u32[]{:S(2)}) collective-permute-start(bf16[128,2048]{1,0:T(8,128)(2,1)S(1)} %pad_maximum_fusion.1.refs_4_), channel_id=1, source_target_pairs={{0,4},{1,5},{2,6},{3,7},{4,0},{5,1},{6,2},{7,3},{8,12},{9,13},{10,... | collective-permute-start | bytes 1572872 | tf_op jit(solution)/shard_map/ppermute | solution.py:23
  42.7 18.3 %collective-permute-start.13 = (bf16[128,2048]{1,0:T(8,128)(2,1)S(1)}, bf16[128,2048]{1,0:T(8,128)(2,1)S(1)}, u32[]{:S(2)}, u32[]{:S(2)}) collective-permute-start(bf16[128,2048]{1,0:T(8,128)(2,1)S(1)} %pad_maximum_fusion.refs_3_), channel_id=1, source_target_pairs={{0,2},{1,3},{2,0},{3,1},{4,6},{5,7},{6,4},{7,5},{8,10},{9,11},{10,... | collective-permute-start | bytes 1572872 | tf_op jit(solution)/shard_map/ppermute | solution.py:23
  53.3 7.8 %collective-permute-start.15 = (bf16[64,2048]{1,0:T(8,128)(2,1)S(1)}, bf16[64,2048]{1,0:T(8,128)(2,1)S(1)}, u32[]{:S(2)}, u32[]{:S(2)}) collective-permute-start(bf16[64,2048]{1,0:T(8,128)(2,1)S(1)} %get-tuple-element.83.refs_7_), channel_id=1, source_target_pairs={{0,2},{1,3},{2,0},{3,1},{4,6},{5,7},{6,4},{7,5},{8,10},{9,11},{10,... | collective-permute-start | bytes 786440 | tf_op jit(solution)/shard_map/ppermute | solution.py:23
  53.9 7.2 %collective-permute-start.16 = (bf16[64,2048]{1,0:T(8,128)(2,1)S(1)}, bf16[64,2048]{1,0:T(8,128)(2,1)}, u32[]{:S(2)}, u32[]{:S(2)}) collective-permute-start(bf16[64,2048]{1,0:T(8,128)(2,1)S(1)} %get-tuple-element.82.refs_8_), channel_id=1, source_target_pairs={{0,4},{1,5},{2,6},{3,7},{4,0},{5,1},{6,2},{7,3},{8,12},{9,13},{10,... | collective-permute-start | bytes 786440 | tf_op jit(solution)/shard_map/ppermute | solution.py:23
  62.8 2.0 %copy-start = (bf16[128,2048]{1,0:T(8,128)(2,1)S(1)}, bf16[128,2048]{1,0:T(8,128)(2,1)}, u32[]{:S(2)}) copy-start(bf16[128,2048]{1,0:T(8,128)(2,1)} %hidden.1) | copy-start | bytes 1572868
  62.8 2.0 %copy-start.3 = (f32[2048]{0:T(1024)S(1)}, f32[2048]{0:T(1024)}, u32[]{:S(2)}) copy-start(f32[2048]{0:T(1024)} %param.27) | copy-start | bytes 24580
  62.8 2.0 %collective-permute-start.17 = (bf16[128,2048]{1,0:T(8,128)(2,1)S(1)}, bf16[128,2048]{1,0:T(8,128)(2,1)S(1)}, u32[]{:S(2)}, u32[]{:S(2)}) collective-permute-start(bf16[128,2048]{1,0:T(8,128)(2,1)S(1)} %project.3), channel_id=1, source_target_pairs={{0,1},{1,0},{2,3},{3,2},{4,5},{5,4},{6,7},{7,6},{8,9},{9,8},{10,11... | collective-permute-start | bytes 1572872 | tf_op jit(solution)/shard_map/ppermute | solution.py:23
  65.2 10.3 %collective-permute-start.18 = (bf16[128,2048]{1,0:T(8,128)(2,1)S(1)}, bf16[128,2048]{1,0:T(8,128)(2,1)S(1)}, u32[]{:S(2)}, u32[]{:S(2)}) collective-permute-start(bf16[128,2048]{1,0:T(8,128)(2,1)S(1)} %get-tuple-element.56.refs_10_), channel_id=1, source_target_pairs={{0,1},{1,0},{2,3},{3,2},{4,5},{5,4},{6,7},{7,6},{8,9},{9,8},{10,11... | collective-permute-start | bytes 1572872 | tf_op jit(solution)/shard_map/ppermute | solution.py:23
  65.6 15.8 %collective-permute-start.24 = (bf16[128,2048]{1,0:T(8,128)(2,1)S(1)}, bf16[128,2048]{1,0:T(8,128)(2,1)S(1)}, u32[]{:S(2)}, u32[]{:S(2)}) collective-permute-start(bf16[128,2048]{1,0:T(8,128)(2,1)S(1)} %get-tuple-element.56.refs_10_), channel_id=1, source_target_pairs={{0,6},{1,7},{2,4},{3,5},{4,2},{5,3},{6,0},{7,1},{8,14},{9,15},{10,... | collective-permute-start | bytes 1572872 | tf_op jit(solution)/shard_map/ppermute | solution.py:23
  81.4 2.2 %collective-permute-start.25 = (bf16[128,2048]{1,0:T(8,128)(2,1)S(1)}, bf16[128,2048]{1,0:T(8,128)(2,1)S(1)}, u32[]{:S(2)}, u32[]{:S(2)}) collective-permute-start(bf16[128,2048]{1,0:T(8,128)(2,1)S(1)} %collective-permute-done.24.refs_10_), channel_id=1, source_target_pairs={{0,1},{1,0},{2,3},{3,2},{4,5},{5,4},{6,7},{7,6},{8,9},{9,8},{10,11... | collective-permute-start | bytes 1572872 | tf_op jit(solution)/shard_map/ppermute | solution.py:23
  81.5 14.3 %collective-permute-start.20 = (bf16[128,2048]{1,0:T(8,128)(2,1)S(1)}, bf16[128,2048]{1,0:T(8,128)(2,1)S(1)}, u32[]{:S(2)}, u32[]{:S(2)}) collective-permute-start(bf16[128,2048]{1,0:T(8,128)(2,1)S(1)} %get-tuple-element.56.refs_10_), channel_id=1, source_target_pairs={{0,2},{1,3},{2,0},{3,1},{4,6},{5,7},{6,4},{7,5},{8,10},{9,11},{10,... | collective-permute-start | bytes 1572872 | tf_op jit(solution)/shard_map/ppermute | solution.py:23
  82.5 14.0 %collective-permute-start.22 = (bf16[128,2048]{1,0:T(8,128)(2,1)S(1)}, bf16[128,2048]{1,0:T(8,128)(2,1)S(1)}, u32[]{:S(2)}, u32[]{:S(2)}) collective-permute-start(bf16[128,2048]{1,0:T(8,128)(2,1)S(1)} %get-tuple-element.56.refs_10_), channel_id=1, source_target_pairs={{0,4},{1,5},{2,6},{3,7},{4,0},{5,1},{6,2},{7,3},{8,12},{9,13},{10,... | collective-permute-start | bytes 1572872 | tf_op jit(solution)/shard_map/ppermute | solution.py:23
  89.3 7.2 %collective-permute-start.26 = (bf16[1,128,2048]{2,1,0:T(8,128)(2,1)S(1)}, bf16[1,128,2048]{2,1,0:T(8,128)(2,1)S(1)}, u32[]{:S(2)}, u32[]{:S(2)}) collective-permute-start(bf16[1,128,2048]{2,1,0:T(8,128)(2,1)S(1)} %get-tuple-element.73), channel_id=1, source_target_pairs={{0,1},{1,0},{2,3},{3,2},{4,5},{5,4},{6,7},{7,6},{8,9},{9,8},{10,11... | collective-permute-start | bytes 1572872 | tf_op jit(solution)/shard_map/ppermute | solution.py:23
  95.8 3.7 %collective-permute-start.21 = (bf16[128,2048]{1,0:T(8,128)(2,1)S(1)}, bf16[128,2048]{1,0:T(8,128)(2,1)S(1)}, u32[]{:S(2)}, u32[]{:S(2)}) collective-permute-start(bf16[128,2048]{1,0:T(8,128)(2,1)S(1)} %collective-permute-done.20.refs_10_), channel_id=1, source_target_pairs={{0,1},{1,0},{2,3},{3,2},{4,5},{5,4},{6,7},{7,6},{8,9},{9,8},{10,11... | collective-permute-start | bytes 1572872 | tf_op jit(solution)/shard_map/ppermute | solution.py:23
  96.5 3.1 %collective-permute-start.23 = (bf16[128,2048]{1,0:T(8,128)(2,1)S(1)}, bf16[128,2048]{1,0:T(8,128)(2,1)S(1)}, u32[]{:S(2)}, u32[]{:S(2)}) collective-permute-start(bf16[128,2048]{1,0:T(8,128)(2,1)S(1)} %collective-permute-done.22.refs_12_), channel_id=1, source_target_pairs={{0,1},{1,0},{2,3},{3,2},{4,5},{5,4},{6,7},{7,6},{8,9},{9,8},{10,11... | collective-permute-start | bytes 1572872 | tf_op jit(solution)/shard_map/ppermute | solution.py:23
  96.7 9.4 %collective-permute-start.27 = (bf16[64,2048]{1,0:T(8,128)(2,1)S(1)}, bf16[64,2048]{1,0:T(8,128)(2,1)S(1)}, u32[]{:S(2)}, u32[]{:S(2)}) collective-permute-start(bf16[64,2048]{1,0:T(8,128)(2,1)S(1)} %get-tuple-element.89), channel_id=1, source_target_pairs={{0,2},{1,3},{2,0},{3,1},{4,6},{5,7},{6,4},{7,5},{8,10},{9,11},{10,... | collective-permute-start | bytes 786440 | tf_op jit(solution)/shard_map/ppermute | solution.py:23
  97.8 8.4 %collective-permute-start.28 = (bf16[64,2048]{1,0:T(8,128)(2,1)S(1)}, bf16[64,2048]{1,0:T(8,128)(2,1)S(1)}, u32[]{:S(2)}, u32[]{:S(2)}) collective-permute-start(bf16[64,2048]{1,0:T(8,128)(2,1)S(1)} %get-tuple-element.88), channel_id=1, source_target_pairs={{0,4},{1,5},{2,6},{3,7},{4,0},{5,1},{6,2},{7,3},{8,12},{9,13},{10,... | collective-permute-start | bytes 786440 | tf_op jit(solution)/shard_map/ppermute | solution.py:23
  106.3 2.7 %collective-permute-start.29 = (bf16[2,128,2048]{2,1,0:T(8,128)(2,1)S(1)}, bf16[2,128,2048]{2,1,0:T(8,128)(2,1)S(1)}, u32[]{:S(2)}, u32[]{:S(2)}) collective-permute-start(bf16[2,128,2048]{2,1,0:T(8,128)(2,1)S(1)} %get-tuple-element.74), channel_id=1, source_target_pairs={{0,1},{1,0},{2,3},{3,2},{4,5},{5,4},{6,7},{7,6},{8,9},{9,8},{10,11... | collective-permute-start | bytes 3145736 | tf_op jit(solution)/shard_map/ppermute | solution.py:23
  106.3 5.6 %collective-permute-start.19 = (bf16[1,128,2048]{2,1,0:T(8,128)(2,1)S(1)}, bf16[1,128,2048]{2,1,0:T(8,128)(2,1)S(1)}, u32[]{:S(2)}, u32[]{:S(2)}) collective-permute-start(bf16[1,128,2048]{2,1,0:T(8,128)(2,1)S(1)} %get-tuple-element.68), channel_id=1, source_target_pairs={{0,1},{1,0},{2,3},{3,2},{4,5},{5,4},{6,7},{7,6},{8,9},{9,8},{10,11... | collective-permute-start | bytes 1572872 | tf_op jit(solution)/shard_map/ppermute | solution.py:23
  109.6 14.0 %collective-permute-start.30 = (bf16[128,2048]{1,0:T(8,128)(2,1)S(1)}, bf16[128,2048]{1,0:T(8,128)(2,1)S(1)}, u32[]{:S(2)}, u32[]{:S(2)}) collective-permute-start(bf16[128,2048]{1,0:T(8,128)(2,1)S(1)} %pad_maximum_fusion.2), channel_id=1, source_target_pairs={{0,2},{1,3},{2,0},{3,1},{4,6},{5,7},{6,4},{7,5},{8,10},{9,11},{10,... | collective-permute-start | bytes 1572872 | tf_op jit(solution)/shard_map/ppermute | solution.py:23
  110.6 13.8 %collective-permute-start.31 = (bf16[128,2048]{1,0:T(8,128)(2,1)S(1)}, bf16[128,2048]{1,0:T(8,128)(2,1)S(1)}, u32[]{:S(2)}, u32[]{:S(2)}) collective-permute-start(bf16[128,2048]{1,0:T(8,128)(2,1)S(1)} %pad_maximum_fusion.3), channel_id=1, source_target_pairs={{0,4},{1,5},{2,6},{3,7},{4,0},{5,1},{6,2},{7,3},{8,12},{9,13},{10,... | collective-permute-start | bytes 1572872 | tf_op jit(solution)/shard_map/ppermute | solution.py:23

commit v6 on v5

--- a/solution.py
+++ b/solution.py
@@ -233,6 +233,25 @@
     )(prompts, lengths, columns, parents, accepted, queries, tree_keys, tree_values, keys, values)
 
 
+def weave_body(upper, lower, first, second):
+    half = upper.shape[0] // 2
+    first[:half, :] = upper[:half, :]
+    first[half:, :] = lower[:half, :]
+    second[:half, :] = upper[half:, :]
+    second[half:, :] = lower[half:, :]
+
+
+def weave(upper, lower):
+    return pl.pallas_call(
+        weave_body,
+        out_shape=(everywhere(upper.shape, upper.dtype),) * 2,
+        in_specs=[IN_VMEM] * 2,
+        out_specs=(IN_VMEM,) * 2,
+        compiler_params=pltpu.CompilerParams(vmem_limit_bytes=6 * 2**20),
+        name="weave",
+    )(upper, lower)
+
+
 def fetch_projection(out_proj, block, before_shared):
     me, place = lax.axis_index("rep"), lax.axis_index("ep")
     core, parity = place % 2, (place // 2 + place // 4) % 2
@@ -250,8 +269,7 @@
         order += [2 * shard + parity, 2 * shard + 1 - parity]
     half = HEAD_DIM // 2
     came1, came3 = after((came1, came3), before_shared)
-    first = jnp.concatenate([came1[:half], came3[:half]], axis=0)
-    second = jnp.concatenate([came1[half:], came3[half:]], axis=0)
+    first, second = weave(came1, came3)
     from_x, from_y = flip(first, 2, 8), flip(second, 4, 8)
     weights = [own, first, second, from_x, from_y]
     pieces = [(0, 0, 2 * HEAD_DIM)]

time: 126 us -> 150 us (1.19)
  waiting for transfers between devices: 49.4 us -> 68.7 us
  starting transfers between devices: 27 us -> 29.8 us
    ppermute x28, waiting for transfers between devices: 43 us -> 65.9 us  [flip(): return lax.ppermute(value, 'ep', [(i, i ^ bits) for i in range(size)])]
    ppermute x2, waiting for transfers between devices: 6.41 us -> 2.83 us  [shifted(): return lax.ppermute(value, 'rep', [(i, (i + by) % 4) for i in range(4)])]
    unnamed x26 -> x24, local copies, waits for them, and re-layouts: 0.06 us -> 2.57 us
    ppermute x28, starting transfers between devices: 21.4 us -> 23.2 us  [flip(): return lax.ppermute(value, 'ep', [(i, i ^ bits) for i in range(size)])]
  transfers between devices with their start and end apart: 32 -> 32, of which waited for: 14 -> 15; matrix products, arithmetic and copies ran while one was open for 3% -> 3% of each run, Pallas kernels for 30% -> 25%
where the time goes in v6:
time: 150 us; the launch traced here: 149 us
  waiting for transfers between devices  68.7 us (46%)
  Pallas kernels  41.6 us (28%)
  starting transfers between devices  29.8 us (20%)
  local copies, waits for them, and re-layouts  4.44 us (3%)
  other arithmetic  3.48 us (2%)
    ppermute x28, waiting for transfers between devices, flip(): return lax.ppermute(value, 'ep', [(i, i ^ bits) for i in range(size)])  65.9 us
    ppermute x28, starting transfers between devices, flip(): return lax.ppermute(value, 'ep', [(i, i ^ bits) for i in range(size)])  23.2 us
    pallas_call x3, Pallas kernels, experts(): pl.pallas_call(lambda *refs: experts_body(len(sources) // pairs, local_ex...  18 us
    pallas_call x1, Pallas kernels, chip_attention(): pl.pallas_call(chip_attention_body, out_shape=(everywhere((heads, 2 * row...  8.88 us
    pallas_call x1, Pallas kernels, stage(): pl.pallas_call(stage_body, out_shape=[pltpu.VMEM(gate_up.shape[1:], BF16)...  8.32 us
    ppermute x2, starting transfers between devices, shifted(): return lax.ppermute(value, 'rep', [(i, (i + by) % 4) for i in range(4)])  3.82 us
    pallas_call x2, Pallas kernels, chip_project(): pl.pallas_call(lambda *refs: chip_project_body(pieces, low_row, *refs), o...  3.43 us
  transfers between devices with their start and end apart: 32, of which 15 were waited for; matrix products, arithmetic and copies ran while one was open for 3% of the time, Pallas kernels for 25%

profile of v6, /device:TPU:0, one launch (start us, length us, event | category | flops | bytes accessed | tf_op | source)
XLA Modules:
  0.0 149.1 jit_solution(9477167660386856492)
XLA Ops:
  0.7 2.1 %pack.1 = (bf16[384,1024]{1,0:T(8,128)(2,1)S(1)}, bf16[208,1024]{1,0:T(8,128)(2,1)S(1)}, bf16[208,1024]{1,0:T(8,128)(2,1)S(1)}, bf16[128,2048]{1,0:T(8,128)(2,1)S(1)}) custom-call(s32[1]{0:T(128)} %bitcast.8.place.me, bf16[128,2048]{1,0:T(8,128)(2,1)} %refs_0_.3, bf16[128,2048]{1,0:T(8,128)(2,1)} %refs_1_.3, bf16[128,2048]{1,0:T(8,128)(2,1)} %refs_2_.3, ...), custom_call_target="tpu_custom_call" | custom-call | tf_op jit(solution)/shard_map/pack/pallas_call | solution.py:92
  2.8 3.0 %collective-permute-start = (bf16[208,1024]{1,0:T(8,128)(2,1)S(1)}, bf16[208,1024]{1,0:T(8,128)(2,1)S(1)}, u32[]{:S(2)}, u32[]{:S(2)}) collective-permute-start(bf16[208,1024]{1,0:T(8,128)(2,1)S(1)} %get-tuple-element.41.prompts_here), channel_id=1, source_target_pairs={{0,2},{1,3},{2,0},{3,1},{4,6},{5,7},{6,4},{7,5},{8,10},{9,11},{10,... | collective-permute-start | bytes 1277960 | tf_op jit(solution)/shard_map/ppermute | solution.py:23
  5.8 0.5 collective-permute-start.2
  6.3 1.6 %collective-permute-start.9 = (bf16[128,2048]{1,0:T(8,128)(2,1)S(1)}, bf16[128,2048]{1,0:T(8,128)(2,1)S(1)}, u32[]{:S(2)}, u32[]{:S(2)}) collective-permute-start(bf16[128,2048]{1,0:T(8,128)(2,1)S(1)} %get-tuple-element.47), channel_id=1, source_target_pairs={{0,8},{8,16},{16,24},{24,0},{1,9},{9,17},{17,25},{25,1},{2,10},{10... | collective-permute-start | bytes 1572872 | tf_op jit(solution)/shard_map/ppermute | solution.py:261
  7.9 2.2 %collective-permute-start.11 = (bf16[128,2048]{1,0:T(8,128)(2,1)S(1)}, bf16[128,2048]{1,0:T(8,128)(2,1)S(1)}, u32[]{:S(2)}, u32[]{:S(2)}) collective-permute-start(bf16[128,2048]{1,0:T(8,128)(2,1)S(1)} %get-tuple-element.47), channel_id=1, source_target_pairs={{0,24},{8,0},{16,8},{24,16},{1,25},{9,1},{17,9},{25,17},{2,26},{10... | collective-permute-start | bytes 1572872 | tf_op jit(solution)/shard_map/ppermute | solution.py:261
  10.3 5.3 %collective-permute-done.refs_4_ = bf16[208,1024]{1,0:T(8,128)(2,1)S(1)} collective-permute-done((bf16[208,1024]{1,0:T(8,128)(2,1)S(1)}, bf16[208,1024]{1,0:T(8,128)(2,1)S(1)}, u32[]{:S(2)}, u32[]{:S(2)}) %collective-permute-start) | collective-permute-done | bytes 426016 | tf_op jit(solution)/shard_map/ppermute | solution.py:23
  15.6 1.8 %collective-permute-start.5 = (bf16[208,1024]{1,0:T(8,128)(2,1)S(1)}, bf16[208,1024]{1,0:T(8,128)(2,1)S(1)}, u32[]{:S(2)}, u32[]{:S(2)}) collective-permute-start(bf16[208,1024]{1,0:T(8,128)(2,1)S(1)} %get-tuple-element.41.prompts_here), channel_id=1, source_target_pairs={{0,4},{1,5},{2,6},{3,7},{4,0},{5,1},{6,2},{7,3},{8,12},{9,13},{10,... | collective-permute-start | bytes 1277960 | tf_op jit(solution)/shard_map/ppermute | solution.py:23
  17.4 0.8 copy-done.1
  18.6 9.8 %collective-permute-done.5.refs_6_ = bf16[208,1024]{1,0:T(8,128)(2,1)S(1)} collective-permute-done((bf16[208,1024]{1,0:T(8,128)(2,1)S(1)}, bf16[208,1024]{1,0:T(8,128)(2,1)S(1)}, u32[]{:S(2)}, u32[]{:S(2)}) %collective-permute-start.5) | collective-permute-done | bytes 426016 | tf_op jit(solution)/shard_map/ppermute | solution.py:23
  28.4 1.5 collective-permute-start.10
  29.8 2.8 %collective-permute-done.11.lower = bf16[128,2048]{1,0:T(8,128)(2,1)S(1)} collective-permute-done((bf16[128,2048]{1,0:T(8,128)(2,1)S(1)}, bf16[128,2048]{1,0:T(8,128)(2,1)S(1)}, u32[]{:S(2)}, u32[]{:S(2)}) %collective-permute-start.11) | collective-permute-done | bytes 524320 | tf_op jit(solution)/shard_map/ppermute | solution.py:261
  32.7 1.3 collective-permute-start.12
  34.1 1.6 %collective-permute-start.7 = (bf16[208,1024]{1,0:T(8,128)(2,1)S(1)}, bf16[208,1024]{1,0:T(8,128)(2,1)}, u32[]{:S(2)}, u32[]{:S(2)}) collective-permute-start(bf16[208,1024]{1,0:T(8,128)(2,1)S(1)} %collective-permute-done.refs_4_), channel_id=1, source_target_pairs={{0,4},{1,5},{2,6},{3,7},{4,0},{5,1},{6,2},{7,3},{8,12},{9,13},{10,... | collective-permute-start | bytes 1277960 | tf_op jit(solution)/shard_map/ppermute | solution.py:23
  35.7 0.5 collective-permute-start.4
  36.2 1.5 %collective-permute-start.8 = (bf16[208,1024]{1,0:T(8,128)(2,1)}, bf16[208,1024]{1,0:T(8,128)(2,1)S(1)}, u32[]{:S(2)}, u32[]{:S(2)}) collective-permute-start(bf16[208,1024]{1,0:T(8,128)(2,1)} %collective-permute-done.6.refs_7_), channel_id=1, source_target_pairs={{0,2},{1,3},{2,0},{3,1},{4,6},{5,7},{6,4},{7,5},{8,10},{9,11},{10,... | collective-permute-start | bytes 1277960 | tf_op jit(solution)/shard_map/ppermute | solution.py:23
  37.9 7.5 %collective-permute-done.7.refs_8_ = bf16[208,1024]{1,0:T(8,128)(2,1)} collective-permute-done((bf16[208,1024]{1,0:T(8,128)(2,1)S(1)}, bf16[208,1024]{1,0:T(8,128)(2,1)}, u32[]{:S(2)}, u32[]{:S(2)}) %collective-permute-start.7) | collective-permute-done | bytes 426016 | tf_op jit(solution)/shard_map/ppermute | solution.py:23
  45.5 3.1 %collective-permute-done.4.refs_5_ = bf16[208,1024]{1,0:T(8,128)(2,1)S(1)} collective-permute-done((bf16[208,1024]{1,0:T(8,128)(2,1)}, bf16[208,1024]{1,0:T(8,128)(2,1)S(1)}, u32[]{:S(2)}, u32[]{:S(2)}) %collective-permute-start.4) | collective-permute-done | bytes 426016 | tf_op jit(solution)/shard_map/ppermute | solution.py:23
  48.6 7.3 %collective-permute-done.8.refs_9_ = bf16[208,1024]{1,0:T(8,128)(2,1)S(1)} collective-permute-done((bf16[208,1024]{1,0:T(8,128)(2,1)}, bf16[208,1024]{1,0:T(8,128)(2,1)S(1)}, u32[]{:S(2)}, u32[]{:S(2)}) %collective-permute-start.8) | collective-permute-done | bytes 426016 | tf_op jit(solution)/shard_map/ppermute | solution.py:23
  56.0 0.8 copy-done.9
  56.7 1.0 copy-done.2
  57.8 8.9 %attention.1 = (bf16[8,256,128]{2,1,0:T(8,128)(2,1)S(1)}, bf16[32,4096]{1,0:T(8,128)(2,1)}, f32[4,8,256]{2,1,0:T(8,128)S(1)}, f32[4,8,256]{2,1,0:T(8,128)S(1)}) custom-call(s32[1]{0:T(128)} %bitcast.8.place.me, s32[2]{0:T(128)S(1)} %copy-done.4, s32[4,64]{1,0:T(4,128)S(1)} %collective-permute-done.1.sibling, s32[4]{0:T(128)S(1)} %copy-done.5, ...), custom_call_target="tpu_custom_call" | custom-call | tf_op jit(solution)/shard_map/attention/pallas_call | solution.py:190
  66.7 0.6 collective-permute-start.13
  67.3 0.5 collective-permute-start.14
  67.8 1.2 slice_select_fusion
  69.1 1.6 %collective-permute-start.15 = (bf16[64,2048]{1,0:T(8,128)(2,1)S(1)}, bf16[64,2048]{1,0:T(8,128)(2,1)S(1)}, u32[]{:S(2)}, u32[]{:S(2)}) collective-permute-start(bf16[64,2048]{1,0:T(8,128)(2,1)S(1)} %get-tuple-element.87.refs_7_), channel_id=1, source_target_pairs={{0,2},{1,3},{2,0},{3,1},{4,6},{5,7},{6,4},{7,5},{8,10},{9,11},{10,... | collective-permute-start | bytes 786440 | tf_op jit(solution)/shard_map/ppermute | solution.py:23
  70.6 1.5 %collective-permute-start.16 = (bf16[64,2048]{1,0:T(8,128)(2,1)S(1)}, bf16[64,2048]{1,0:T(8,128)(2,1)}, u32[]{:S(2)}, u32[]{:S(2)}) collective-permute-start(bf16[64,2048]{1,0:T(8,128)(2,1)S(1)} %get-tuple-element.86.refs_8_), channel_id=1, source_target_pairs={{0,4},{1,5},{2,6},{3,7},{4,0},{5,1},{6,2},{7,3},{8,12},{9,13},{10,... | collective-permute-start | bytes 786440 | tf_op jit(solution)/shard_map/ppermute | solution.py:23
  72.2 1.3 constant_dynamic-slice_fusion.refs_2_
  74.0 10.6 %collective-permute-done.15.refs_9_ = bf16[64,2048]{1,0:T(8,128)(2,1)S(1)} collective-permute-done((bf16[64,2048]{1,0:T(8,128)(2,1)S(1)}, bf16[64,2048]{1,0:T(8,128)(2,1)S(1)}, u32[]{:S(2)}, u32[]{:S(2)}) %collective-permute-start.15) | collective-permute-done | bytes 262176 | tf_op jit(solution)/shard_map/ppermute | solution.py:23
  84.9 1.7 %project.3 = bf16[128,2048]{1,0:T(8,128)(2,1)S(1)} custom-call(s32[8]{0:T(128)S(1)} %stack.41.refs_0_, bf16[8,256,128]{2,1,0:T(8,128)(2,1)S(1)} %get-tuple-element.53.refs_1_, bf16[256,2048]{1,0:T(8,128)(2,1)S(1)} %constant_dynamic-slice_fusion.refs_2_, bf16[128,2048]{1,0:T(8,128)(2,1)S(1)} %get-tuple-element.56.refs_3_, ...), custom_call_target="tpu_custom_call" | custom-call | tf_op jit(solution)/shard_map/project/pallas_call | solution.py:299
  86.7 1.7 %project.2.mine = f32[128,2048]{1,0:T(8,128)S(1)} custom-call(s32[8]{0:T(128)S(1)} %stack.41.refs_0_, bf16[8,256,128]{2,1,0:T(8,128)(2,1)S(1)} %get-tuple-element.53.refs_1_, bf16[256,2048]{1,0:T(8,128)(2,1)S(1)} %constant_dynamic-slice_fusion.refs_2_, bf16[128,2048]{1,0:T(8,128)(2,1)S(1)} %get-tuple-element.56.refs_3_, ...), custom_call_target="tpu_custom_call" | custom-call | tf_op jit(solution)/shard_map/project/pallas_call | solution.py:299
  89.5 1.5 %collective-permute-start.24 = (bf16[128,2048]{1,0:T(8,128)(2,1)S(1)}, bf16[128,2048]{1,0:T(8,128)(2,1)S(1)}, u32[]{:S(2)}, u32[]{:S(2)}) collective-permute-start(bf16[128,2048]{1,0:T(8,128)(2,1)S(1)} %get-tuple-element.60.refs_10_), channel_id=1, source_target_pairs={{0,6},{1,7},{2,4},{3,5},{4,2},{5,3},{6,0},{7,1},{8,14},{9,15},{10,... | collective-permute-start | bytes 1572872 | tf_op jit(solution)/shard_map/ppermute | solution.py:23
  91.0 8.3 %stage.1 = (bf16[2048,1024]{1,0:T(8,128)(2,1)S(1)}, bf16[2048,1024]{1,0:T(8,128)(2,1)S(1)}, bf16[2048,1024]{1,0:T(8,128)(2,1)S(1)}, bf16[2048,1024]{1,0:T(8,128)...) custom-call(bf16[4,2048,1024]{2,1,0:T(8,128)(2,1)} %gate_up, ...), custom_call_target="tpu_custom_call" | custom-call | bytes 25165824 | tf_op jit(solution)/shard_map/stage/pallas_call | solution.py:343
  99.3 5.8 %experts.3 = (bf16[1,128,2048]{2,1,0:T(8,128)(2,1)S(1)}, bf16[1,128,2048]{2,1,0:T(8,128)(2,1)S(1)}) custom-call(bf16[1,320,256]{2,1,0:T(8,128)(2,1)S(1)} %get-tuple-element.90.refs_0_, f32[1,320,1]{2,1,0:T(8,128)S(1)} %get-tuple-element.88.refs_1_, bf16[2048,1024]{1,0:T(8,128)(2,1)S(1)} %get-tuple-element.63.refs_2_, ...), custom_call_target="tpu_custom_call" | custom-call | flops 4026531840 | bytes 16777216 | tf_op jit(solution)/shard_map/experts/pallas_call | solution.py:453
  105.3 0.7 collective-permute-start.20
  106.0 1.4 collective-permute-start.22
  107.4 5.7 %experts.5 = (bf16[1,128,2048]{2,1,0:T(8,128)(2,1)S(1)}, bf16[1,128,2048]{2,1,0:T(8,128)(2,1)S(1)}) custom-call(bf16[1,320,256]{2,1,0:T(8,128)(2,1)S(1)} %get-tuple-element.91.refs_0_, f32[1,320,1]{2,1,0:T(8,128)S(1)} %get-tuple-element.89.refs_1_, bf16[2048,1024]{1,0:T(8,128)(2,1)S(1)} %get-tuple-element.63.refs_2_, ...), custom_call_target="tpu_custom_call" | custom-call | flops 4026531840 | bytes 16777216 | tf_op jit(solution)/shard_map/experts/pallas_call | solution.py:453
  113.2 6.4 %collective-permute-done.20.refs_10_ = bf16[128,2048]{1,0:T(8,128)(2,1)S(1)} collective-permute-done((bf16[128,2048]{1,0:T(8,128)(2,1)S(1)}, bf16[128,2048]{1,0:T(8,128)(2,1)S(1)}, u32[]{:S(2)}, u32[]{:S(2)}) %collective-permute-start.20) | collective-permute-done | bytes 524320 | tf_op jit(solution)/shard_map/ppermute | solution.py:23
  120.3 1.3 collective-permute-start.27
  121.6 1.5 %collective-permute-start.28 = (bf16[64,2048]{1,0:T(8,128)(2,1)S(1)}, bf16[64,2048]{1,0:T(8,128)(2,1)S(1)}, u32[]{:S(2)}, u32[]{:S(2)}) collective-permute-start(bf16[64,2048]{1,0:T(8,128)(2,1)S(1)} %get-tuple-element.92), channel_id=1, source_target_pairs={{0,4},{1,5},{2,6},{3,7},{4,0},{5,1},{6,2},{7,3},{8,12},{9,13},{10,... | collective-permute-start | bytes 786440 | tf_op jit(solution)/shard_map/ppermute | solution.py:23
  123.1 6.4 %experts.4 = (bf16[2,128,2048]{2,1,0:T(8,128)(2,1)S(1)}, bf16[2,128,2048]{2,1,0:T(8,128)(2,1)S(1)}) custom-call(bf16[2,320,256]{2,1,0:T(8,128)(2,1)S(1)} %slice.66.refs_0_, f32[2,320,1]{2,1,0:T(8,128)S(1)} %slice.67.refs_1_, bf16[2048,1024]{1,0:T(8,128)(2,1)S(1)} %get-tuple-element.63.refs_2_, bf16[2048,1024]{1,0:T(8,128)(2,1)S(1)} %get-tuple-element.64.refs_3_, ...), custom_call_target="tpu_custom_call" | custom-call | flops 8053063680 | bytes 16777216 | tf_op jit(solution)/shard_map/experts/pallas_call | solution.py:453
  129.6 0.5 collective-permute-done.28
  130.1 0.5 collective-permute-start.19
  130.6 2.1 %collective-permute-done.29 = bf16[2,128,2048]{2,1,0:T(8,128)(2,1)S(1)} collective-permute-done((bf16[2,128,2048]{2,1,0:T(8,128)(2,1)S(1)}, bf16[2,128,2048]{2,1,0:T(8,128)(2,1)S(1)}, u32[]{:S(2)}, u32[]{:S(2)}) %collective-permute-start.29) | collective-permute-done | bytes 1048608 | tf_op jit(solution)/shard_map/ppermute | solution.py:23
  133.4 0.7 collective-permute-start.30
  134.2 1.4 collective-permute-start.31
  135.6 11.8 %collective-permute-done.30 = bf16[128,2048]{1,0:T(8,128)(2,1)S(1)} collective-permute-done((bf16[128,2048]{1,0:T(8,128)(2,1)S(1)}, bf16[128,2048]{1,0:T(8,128)(2,1)S(1)}, u32[]{:S(2)}, u32[]{:S(2)}) %collective-permute-start.30) | collective-permute-done | bytes 524320 | tf_op jit(solution)/shard_map/ppermute | solution.py:23
  147.4 0.5 collective-permute-done.31
  147.9 1.2 fusion.2
  (78 shorter events, 4.6 us)
Async XLA Ops:
  0.6 9.5 %copy-start.4 = (s32[2]{0:T(128)S(1)}, s32[2]{0:T(128)}, u32[]{:S(2)}) copy-start(s32[2]{0:T(128)} %my_prompts.1) | copy-start | bytes 28
  0.6 9.6 %copy-start.10 = (s32[2,64]{1,0:T(2,128)S(1)}, s32[2,64]{1,0:T(2,128)}, u32[]{:S(2)}) copy-start(s32[2,64]{1,0:T(2,128)} %param.20) | copy-start | bytes 1540
  0.7 17.9 %copy-start.11 = (s32[2,16]{1,0:T(2,128)S(1)}, s32[2,16]{1,0:T(2,128)}, u32[]{:S(2)}) copy-start(s32[2,16]{1,0:T(2,128)} %param.21) | copy-start | bytes 388
  0.7 56.1 %copy-start.5 = (s32[4]{0:T(128)S(1)}, s32[4]{0:T(128)}, u32[]{:S(2)}) copy-start(s32[4]{0:T(128)} %lengths.1) | copy-start | bytes 52
  2.8 12.8 %collective-permute-start = (bf16[208,1024]{1,0:T(8,128)(2,1)S(1)}, bf16[208,1024]{1,0:T(8,128)(2,1)S(1)}, u32[]{:S(2)}, u32[]{:S(2)}) collective-permute-start(bf16[208,1024]{1,0:T(8,128)(2,1)S(1)} %get-tuple-element.41.prompts_here), channel_id=1, source_target_pairs={{0,2},{1,3},{2,0},{3,1},{4,6},{5,7},{6,4},{7,5},{8,10},{9,11},{10,... | collective-permute-start | bytes 1277960 | tf_op jit(solution)/shard_map/ppermute | solution.py:23
  5.8 12.4 %collective-permute-start.3 = (bf16[208,1024]{1,0:T(8,128)(2,1)S(1)}, bf16[208,1024]{1,0:T(8,128)(2,1)}, u32[]{:S(2)}, u32[]{:S(2)}) collective-permute-start(bf16[208,1024]{1,0:T(8,128)(2,1)S(1)} %get-tuple-element.44), channel_id=1, source_target_pairs={{0,1},{1,0},{2,3},{3,2},{4,5},{5,4},{6,7},{7,6},{8,9},{9,8},{10,11... | collective-permute-start | bytes 1277960 | tf_op jit(solution)/shard_map/ppermute | solution.py:23
  5.8 29.9 %collective-permute-start.2 = (bf16[384,1024]{1,0:T(8,128)(2,1)S(1)}, bf16[384,1024]{1,0:T(8,128)(2,1)S(1)}, u32[]{:S(2)}, u32[]{:S(2)}) collective-permute-start(bf16[384,1024]{1,0:T(8,128)(2,1)S(1)} %get-tuple-element.43), channel_id=1, source_target_pairs={{0,1},{1,0},{2,3},{3,2},{4,5},{5,4},{6,7},{7,6},{8,9},{9,8},{10,11... | collective-permute-start | bytes 2359304 | tf_op jit(solution)/shard_map/ppermute | solution.py:23
  6.3 22.1 %collective-permute-start.9 = (bf16[128,2048]{1,0:T(8,128)(2,1)S(1)}, bf16[128,2048]{1,0:T(8,128)(2,1)S(1)}, u32[]{:S(2)}, u32[]{:S(2)}) collective-permute-start(bf16[128,2048]{1,0:T(8,128)(2,1)S(1)} %get-tuple-element.47), channel_id=1, source_target_pairs={{0,8},{8,16},{16,24},{24,0},{1,9},{9,17},{17,25},{25,1},{2,10},{10... | collective-permute-start | bytes 1572872 | tf_op jit(solution)/shard_map/ppermute | solution.py:261
  7.9 24.8 %collective-permute-start.11 = (bf16[128,2048]{1,0:T(8,128)(2,1)S(1)}, bf16[128,2048]{1,0:T(8,128)(2,1)S(1)}, u32[]{:S(2)}, u32[]{:S(2)}) collective-permute-start(bf16[128,2048]{1,0:T(8,128)(2,1)S(1)} %get-tuple-element.47), channel_id=1, source_target_pairs={{0,24},{8,0},{16,8},{24,16},{1,25},{9,1},{17,9},{25,17},{2,26},{10... | collective-permute-start | bytes 1572872 | tf_op jit(solution)/shard_map/ppermute | solution.py:261
  15.6 33.0 %copy-start.6 = (bf16[208,1024]{1,0:T(8,128)(2,1)}, bf16[208,1024]{1,0:T(8,128)(2,1)S(1)}, u32[]{:S(2)}) copy-start(bf16[208,1024]{1,0:T(8,128)(2,1)S(1)} %collective-permute-done.refs_4_) | copy-start | bytes 1277956
  15.6 12.8 %collective-permute-start.5 = (bf16[208,1024]{1,0:T(8,128)(2,1)S(1)}, bf16[208,1024]{1,0:T(8,128)(2,1)S(1)}, u32[]{:S(2)}, u32[]{:S(2)}) collective-permute-start(bf16[208,1024]{1,0:T(8,128)(2,1)S(1)} %get-tuple-element.41.prompts_here), channel_id=1, source_target_pairs={{0,4},{1,5},{2,6},{3,7},{4,0},{5,1},{6,2},{7,3},{8,12},{9,13},{10,... | collective-permute-start | bytes 1277960 | tf_op jit(solution)/shard_map/ppermute | solution.py:23
  17.4 0.8 copy-start.1
  18.2 18.0 %collective-permute-start.6 = (bf16[208,1024]{1,0:T(8,128)(2,1)}, bf16[208,1024]{1,0:T(8,128)(2,1)}, u32[]{:S(2)}, u32[]{:S(2)}) collective-permute-start(bf16[208,1024]{1,0:T(8,128)(2,1)} %collective-permute-done.3.refs_3_), channel_id=1, source_target_pairs={{0,4},{1,5},{2,6},{3,7},{4,0},{5,1},{6,2},{7,3},{8,12},{9,13},{10,... | collective-permute-start | bytes 1277960 | tf_op jit(solution)/shard_map/ppermute | solution.py:23
  28.4 5.6 %copy-start.7 = (bf16[208,1024]{1,0:T(8,128)(2,1)}, bf16[208,1024]{1,0:T(8,128)(2,1)S(1)}, u32[]{:S(2)}) copy-start(bf16[208,1024]{1,0:T(8,128)(2,1)S(1)} %collective-permute-done.5.refs_6_) | copy-start | bytes 1277956
  28.4 5.7 %collective-permute-start.1 = (s32[4,64]{1,0:T(4,128)S(1)}, s32[4,64]{1,0:T(4,128)S(1)}, u32[]{:S(2)}, u32[]{:S(2)}) collective-permute-start(s32[4,64]{1,0:T(4,128)S(1)} %pad_add_fusion.2), channel_id=1, source_target_pairs={{0,1},{1,0},{2,3},{3,2},{4,5},{5,4},{6,7},{7,6},{8,9},{9,8},{10,11... | collective-permute-start | bytes 3080 | tf_op jit(solution)/shard_map/ppermute | solution.py:23
  28.4 38.3 %collective-permute-start.10 = (bf16[128,2048]{1,0:T(8,128)(2,1)S(1)}, bf16[128,2048]{1,0:T(8,128)(2,1)}, u32[]{:S(2)}, u32[]{:S(2)}) collective-permute-start(bf16[128,2048]{1,0:T(8,128)(2,1)S(1)} %collective-permute-done.9.upper), channel_id=1, source_target_pairs={{8,16},{16,24},{9,17},{17,25},{10,18},{18,26},{11,19},{19,27},{12,... | collective-permute-start | bytes 1572872 | tf_op jit(solution)/shard_map/ppermute | solution.py:264
  32.7 34.0 %collective-permute-start.12 = (bf16[128,2048]{1,0:T(8,128)(2,1)S(1)}, bf16[128,2048]{1,0:T(8,128)(2,1)}, u32[]{:S(2)}, u32[]{:S(2)}) collective-permute-start(bf16[128,2048]{1,0:T(8,128)(2,1)S(1)} %collective-permute-done.11.lower), channel_id=1, source_target_pairs={{16,8},{8,0},{17,9},{9,1},{18,10},{10,2},{19,11},{11,3},{20,12},{1... | collective-permute-start | bytes 1572872 | tf_op jit(solution)/shard_map/ppermute | solution.py:265
  34.1 11.4 %collective-permute-start.7 = (bf16[208,1024]{1,0:T(8,128)(2,1)S(1)}, bf16[208,1024]{1,0:T(8,128)(2,1)}, u32[]{:S(2)}, u32[]{:S(2)}) collective-permute-start(bf16[208,1024]{1,0:T(8,128)(2,1)S(1)} %collective-permute-done.refs_4_), channel_id=1, source_target_pairs={{0,4},{1,5},{2,6},{3,7},{4,0},{5,1},{6,2},{7,3},{8,12},{9,13},{10,... | collective-permute-start | bytes 1277960 | tf_op jit(solution)/shard_map/ppermute | solution.py:23
  35.7 13.0 %collective-permute-start.4 = (bf16[208,1024]{1,0:T(8,128)(2,1)}, bf16[208,1024]{1,0:T(8,128)(2,1)S(1)}, u32[]{:S(2)}, u32[]{:S(2)}) collective-permute-start(bf16[208,1024]{1,0:T(8,128)(2,1)} %collective-permute-done.3.refs_3_), channel_id=1, source_target_pairs={{0,2},{1,3},{2,0},{3,1},{4,6},{5,7},{6,4},{7,5},{8,10},{9,11},{10,... | collective-permute-start | bytes 1277960 | tf_op jit(solution)/shard_map/ppermute | solution.py:23
  36.2 19.8 %collective-permute-start.8 = (bf16[208,1024]{1,0:T(8,128)(2,1)}, bf16[208,1024]{1,0:T(8,128)(2,1)S(1)}, u32[]{:S(2)}, u32[]{:S(2)}) collective-permute-start(bf16[208,1024]{1,0:T(8,128)(2,1)} %collective-permute-done.6.refs_7_), channel_id=1, source_target_pairs={{0,2},{1,3},{2,0},{3,1},{4,6},{5,7},{6,4},{7,5},{8,10},{9,11},{10,... | collective-permute-start | bytes 1277960 | tf_op jit(solution)/shard_map/ppermute | solution.py:23
  48.6 7.3 %copy-start.8 = (bf16[208,1024]{1,0:T(8,128)(2,1)}, bf16[208,1024]{1,0:T(8,128)(2,1)S(1)}, u32[]{:S(2)}) copy-start(bf16[208,1024]{1,0:T(8,128)(2,1)S(1)} %collective-permute-done.4.refs_5_) | copy-start | bytes 1277956
  56.0 0.8 copy-start.9
  56.7 1.0 copy-start.2
  66.7 18.2 %collective-permute-start.13 = (bf16[128,2048]{1,0:T(8,128)(2,1)S(1)}, bf16[128,2048]{1,0:T(8,128)(2,1)S(1)}, u32[]{:S(2)}, u32[]{:S(2)}) collective-permute-start(bf16[128,2048]{1,0:T(8,128)(2,1)S(1)} %get-tuple-element.56.refs_3_), channel_id=1, source_target_pairs={{0,2},{1,3},{2,0},{3,1},{4,6},{5,7},{6,4},{7,5},{8,10},{9,11},{10,... | collective-permute-start | bytes 1572872 | tf_op jit(solution)/shard_map/ppermute | solution.py:23
  67.3 17.6 %collective-permute-start.14 = (bf16[128,2048]{1,0:T(8,128)(2,1)S(1)}, bf16[128,2048]{1,0:T(8,128)(2,1)S(1)}, u32[]{:S(2)}, u32[]{:S(2)}) collective-permute-start(bf16[128,2048]{1,0:T(8,128)(2,1)S(1)} %get-tuple-element.57.refs_4_), channel_id=1, source_target_pairs={{0,4},{1,5},{2,6},{3,7},{4,0},{5,1},{6,2},{7,3},{8,12},{9,13},{10,... | collective-permute-start | bytes 1572872 | tf_op jit(solution)/shard_map/ppermute | solution.py:23
  69.1 15.5 %collective-permute-start.15 = (bf16[64,2048]{1,0:T(8,128)(2,1)S(1)}, bf16[64,2048]{1,0:T(8,128)(2,1)S(1)}, u32[]{:S(2)}, u32[]{:S(2)}) collective-permute-start(bf16[64,2048]{1,0:T(8,128)(2,1)S(1)} %get-tuple-element.87.refs_7_), channel_id=1, source_target_pairs={{0,2},{1,3},{2,0},{3,1},{4,6},{5,7},{6,4},{7,5},{8,10},{9,11},{10,... | collective-permute-start | bytes 786440 | tf_op jit(solution)/shard_map/ppermute | solution.py:23
  70.6 14.3 %collective-permute-start.16 = (bf16[64,2048]{1,0:T(8,128)(2,1)S(1)}, bf16[64,2048]{1,0:T(8,128)(2,1)}, u32[]{:S(2)}, u32[]{:S(2)}) collective-permute-start(bf16[64,2048]{1,0:T(8,128)(2,1)S(1)} %get-tuple-element.86.refs_8_), channel_id=1, source_target_pairs={{0,4},{1,5},{2,6},{3,7},{4,0},{5,1},{6,2},{7,3},{8,12},{9,13},{10,... | collective-permute-start | bytes 786440 | tf_op jit(solution)/shard_map/ppermute | solution.py:23
  86.6 2.0 %copy-start = (bf16[128,2048]{1,0:T(8,128)(2,1)S(1)}, bf16[128,2048]{1,0:T(8,128)(2,1)}, u32[]{:S(2)}) copy-start(bf16[128,2048]{1,0:T(8,128)(2,1)} %hidden.1) | copy-start | bytes 1572868
  86.6 2.0 %copy-start.3 = (f32[2048]{0:T(1024)S(1)}, f32[2048]{0:T(1024)}, u32[]{:S(2)}) copy-start(f32[2048]{0:T(1024)} %param.27) | copy-start | bytes 24580
  86.6 2.0 %collective-permute-start.17 = (bf16[128,2048]{1,0:T(8,128)(2,1)S(1)}, bf16[128,2048]{1,0:T(8,128)(2,1)S(1)}, u32[]{:S(2)}, u32[]{:S(2)}) collective-permute-start(bf16[128,2048]{1,0:T(8,128)(2,1)S(1)} %project.3), channel_id=1, source_target_pairs={{0,1},{1,0},{2,3},{3,2},{4,5},{5,4},{6,7},{7,6},{8,9},{9,8},{10,11... | collective-permute-start | bytes 1572872 | tf_op jit(solution)/shard_map/ppermute | solution.py:23
  89.1 10.3 %collective-permute-start.18 = (bf16[128,2048]{1,0:T(8,128)(2,1)S(1)}, bf16[128,2048]{1,0:T(8,128)(2,1)S(1)}, u32[]{:S(2)}, u32[]{:S(2)}) collective-permute-start(bf16[128,2048]{1,0:T(8,128)(2,1)S(1)} %get-tuple-element.60.refs_10_), channel_id=1, source_target_pairs={{0,1},{1,0},{2,3},{3,2},{4,5},{5,4},{6,7},{7,6},{8,9},{9,8},{10,11... | collective-permute-start | bytes 1572872 | tf_op jit(solution)/shard_map/ppermute | solution.py:23
  89.5 15.7 %collective-permute-start.24 = (bf16[128,2048]{1,0:T(8,128)(2,1)S(1)}, bf16[128,2048]{1,0:T(8,128)(2,1)S(1)}, u32[]{:S(2)}, u32[]{:S(2)}) collective-permute-start(bf16[128,2048]{1,0:T(8,128)(2,1)S(1)} %get-tuple-element.60.refs_10_), channel_id=1, source_target_pairs={{0,6},{1,7},{2,4},{3,5},{4,2},{5,3},{6,0},{7,1},{8,14},{9,15},{10,... | collective-permute-start | bytes 1572872 | tf_op jit(solution)/shard_map/ppermute | solution.py:23
  105.2 2.2 %collective-permute-start.25 = (bf16[128,2048]{1,0:T(8,128)(2,1)S(1)}, bf16[128,2048]{1,0:T(8,128)(2,1)S(1)}, u32[]{:S(2)}, u32[]{:S(2)}) collective-permute-start(bf16[128,2048]{1,0:T(8,128)(2,1)S(1)} %collective-permute-done.24.refs_10_), channel_id=1, source_target_pairs={{0,1},{1,0},{2,3},{3,2},{4,5},{5,4},{6,7},{7,6},{8,9},{9,8},{10,11... | collective-permute-start | bytes 1572872 | tf_op jit(solution)/shard_map/ppermute | solution.py:23
  105.3 14.3 %collective-permute-start.20 = (bf16[128,2048]{1,0:T(8,128)(2,1)S(1)}, bf16[128,2048]{1,0:T(8,128)(2,1)S(1)}, u32[]{:S(2)}, u32[]{:S(2)}) collective-permute-start(bf16[128,2048]{1,0:T(8,128)(2,1)S(1)} %get-tuple-element.60.refs_10_), channel_id=1, source_target_pairs={{0,2},{1,3},{2,0},{3,1},{4,6},{5,7},{6,4},{7,5},{8,10},{9,11},{10,... | collective-permute-start | bytes 1572872 | tf_op jit(solution)/shard_map/ppermute | solution.py:23
  106.0 14.1 %collective-permute-start.22 = (bf16[128,2048]{1,0:T(8,128)(2,1)S(1)}, bf16[128,2048]{1,0:T(8,128)(2,1)S(1)}, u32[]{:S(2)}, u32[]{:S(2)}) collective-permute-start(bf16[128,2048]{1,0:T(8,128)(2,1)S(1)} %get-tuple-element.60.refs_10_), channel_id=1, source_target_pairs={{0,4},{1,5},{2,6},{3,7},{4,0},{5,1},{6,2},{7,3},{8,12},{9,13},{10,... | collective-permute-start | bytes 1572872 | tf_op jit(solution)/shard_map/ppermute | solution.py:23
  113.1 7.0 %collective-permute-start.26 = (bf16[1,128,2048]{2,1,0:T(8,128)(2,1)S(1)}, bf16[1,128,2048]{2,1,0:T(8,128)(2,1)S(1)}, u32[]{:S(2)}, u32[]{:S(2)}) collective-permute-start(bf16[1,128,2048]{2,1,0:T(8,128)(2,1)S(1)} %get-tuple-element.77), channel_id=1, source_target_pairs={{0,1},{1,0},{2,3},{3,2},{4,5},{5,4},{6,7},{7,6},{8,9},{9,8},{10,11... | collective-permute-start | bytes 1572872 | tf_op jit(solution)/shard_map/ppermute | solution.py:23
  119.6 3.5 %collective-permute-start.21 = (bf16[128,2048]{1,0:T(8,128)(2,1)S(1)}, bf16[128,2048]{1,0:T(8,128)(2,1)S(1)}, u32[]{:S(2)}, u32[]{:S(2)}) collective-permute-start(bf16[128,2048]{1,0:T(8,128)(2,1)S(1)} %collective-permute-done.20.refs_10_), channel_id=1, source_target_pairs={{0,1},{1,0},{2,3},{3,2},{4,5},{5,4},{6,7},{7,6},{8,9},{9,8},{10,11... | collective-permute-start | bytes 1572872 | tf_op jit(solution)/shard_map/ppermute | solution.py:23
  120.0 3.1 %collective-permute-start.23 = (bf16[128,2048]{1,0:T(8,128)(2,1)S(1)}, bf16[128,2048]{1,0:T(8,128)(2,1)S(1)}, u32[]{:S(2)}, u32[]{:S(2)}) collective-permute-start(bf16[128,2048]{1,0:T(8,128)(2,1)S(1)} %collective-permute-done.22.refs_12_), channel_id=1, source_target_pairs={{0,1},{1,0},{2,3},{3,2},{4,5},{5,4},{6,7},{7,6},{8,9},{9,8},{10,11... | collective-permute-start | bytes 1572872 | tf_op jit(solution)/shard_map/ppermute | solution.py:23
  120.3 9.3 %collective-permute-start.27 = (bf16[64,2048]{1,0:T(8,128)(2,1)S(1)}, bf16[64,2048]{1,0:T(8,128)(2,1)S(1)}, u32[]{:S(2)}, u32[]{:S(2)}) collective-permute-start(bf16[64,2048]{1,0:T(8,128)(2,1)S(1)} %get-tuple-element.93), channel_id=1, source_target_pairs={{0,2},{1,3},{2,0},{3,1},{4,6},{5,7},{6,4},{7,5},{8,10},{9,11},{10,... | collective-permute-start | bytes 786440 | tf_op jit(solution)/shard_map/ppermute | solution.py:23
  121.6 8.4 %collective-permute-start.28 = (bf16[64,2048]{1,0:T(8,128)(2,1)S(1)}, bf16[64,2048]{1,0:T(8,128)(2,1)S(1)}, u32[]{:S(2)}, u32[]{:S(2)}) collective-permute-start(bf16[64,2048]{1,0:T(8,128)(2,1)S(1)} %get-tuple-element.92), channel_id=1, source_target_pairs={{0,4},{1,5},{2,6},{3,7},{4,0},{5,1},{6,2},{7,3},{8,12},{9,13},{10,... | collective-permute-start | bytes 786440 | tf_op jit(solution)/shard_map/ppermute | solution.py:23
  130.1 2.7 %collective-permute-start.29 = (bf16[2,128,2048]{2,1,0:T(8,128)(2,1)S(1)}, bf16[2,128,2048]{2,1,0:T(8,128)(2,1)S(1)}, u32[]{:S(2)}, u32[]{:S(2)}) collective-permute-start(bf16[2,128,2048]{2,1,0:T(8,128)(2,1)S(1)} %get-tuple-element.78), channel_id=1, source_target_pairs={{0,1},{1,0},{2,3},{3,2},{4,5},{5,4},{6,7},{7,6},{8,9},{9,8},{10,11... | collective-permute-start | bytes 3145736 | tf_op jit(solution)/shard_map/ppermute | solution.py:23
  130.1 5.5 %collective-permute-start.19 = (bf16[1,128,2048]{2,1,0:T(8,128)(2,1)S(1)}, bf16[1,128,2048]{2,1,0:T(8,128)(2,1)S(1)}, u32[]{:S(2)}, u32[]{:S(2)}) collective-permute-start(bf16[1,128,2048]{2,1,0:T(8,128)(2,1)S(1)} %get-tuple-element.72), channel_id=1, source_target_pairs={{0,1},{1,0},{2,3},{3,2},{4,5},{5,4},{6,7},{7,6},{8,9},{9,8},{10,11... | collective-permute-start | bytes 1572872 | tf_op jit(solution)/shard_map/ppermute | solution.py:23
  133.4 14.0 %collective-permute-start.30 = (bf16[128,2048]{1,0:T(8,128)(2,1)S(1)}, bf16[128,2048]{1,0:T(8,128)(2,1)S(1)}, u32[]{:S(2)}, u32[]{:S(2)}) collective-permute-start(bf16[128,2048]{1,0:T(8,128)(2,1)S(1)} %pad_maximum_fusion), channel_id=1, source_target_pairs={{0,2},{1,3},{2,0},{3,1},{4,6},{5,7},{6,4},{7,5},{8,10},{9,11},{10,... | collective-permute-start | bytes 1572872 | tf_op jit(solution)/shard_map/ppermute | solution.py:23
  134.2 13.8 %collective-permute-start.31 = (bf16[128,2048]{1,0:T(8,128)(2,1)S(1)}, bf16[128,2048]{1,0:T(8,128)(2,1)S(1)}, u32[]{:S(2)}, u32[]{:S(2)}) collective-permute-start(bf16[128,2048]{1,0:T(8,128)(2,1)S(1)} %pad_maximum_fusion.1), channel_id=1, source_target_pairs={{0,4},{1,5},{2,6},{3,7},{4,0},{5,1},{6,2},{7,3},{8,12},{9,13},{10,... | collective-permute-start | bytes 1572872 | tf_op jit(solution)/shard_map/ppermute | solution.py:23
